TPU v7x, 128 devices: a whole 4x4x4 slice. The times are simulated.
128 devices in a mesh: rep: 2 (over x_lo), shard: 64 (over x_hi, z, y, core).
Axes of the slice: x: 4 (x_hi: 2, x_lo: 2; x = x_hi * 2 + x_lo), y: 4, z: 4, core: 2. Of those that a mesh axis runs over, the one named last changes fastest.
Arguments:
- tokens: bfloat16 [32768, 1024], P(('rep', 'shard')), may hold values from -6 to 6
- w_qkv: bfloat16 [2, 1024, 3072], P(None, 'shard'), may hold values from -0.1875 to 0.1875
- b_qkv: bfloat16 [2, 3072], P(None, 'shard'), may hold values from -1.796875 to 1.796875
- w_out: bfloat16 [2, 1024, 1024], P(None, 'shard'), may hold values from -0.5 to 0.5
- w_up: bfloat16 [2, 1024, 4096], P(None, 'shard'), may hold values from -0.1875 to 0.1875
- b_up: bfloat16 [2, 4096], P(None, 'shard'), may hold values from -1.796875 to 1.796875
- w_down: bfloat16 [2, 4096, 1024], P(None, 'shard'), may hold values from -0.125 to 0.125
- ln_gain: bfloat16 [2, 1024], P(None, 'shard'), may hold values from 0.5 to 1.5
- ln_bias: bfloat16 [2, 1024], P(None, 'shard'), may hold values from -1.796875 to 1.796875
- out_bias: bfloat16 [2, 1024], P(None, 'shard'), may hold values from -1.796875 to 1.796875
- out_grad: bfloat16 [32768, 1024], P(('rep', 'shard')), may hold values from -6 to 6
Outputs:
- result: bfloat16 [32768, 1024], P(('rep', 'shard'))
- in_grad: float32 [32768, 1024], P(('rep', 'shard'))
- w_qkv_grad: float32 [2, 1024, 3072], P(None, 'shard')
- b_qkv_grad: float32 [2, 3072], P(None, 'shard')
- w_out_grad: float32 [2, 1024, 1024], P(None, 'shard')
- w_up_grad: float32 [2, 1024, 4096], P(None, 'shard')
- b_up_grad: float32 [2, 4096], P(None, 'shard')
- w_down_grad: float32 [2, 4096, 1024], P(None, 'shard')
- ln_gain_grad: float32 [2, 1024], P(None, 'shard')
- ln_bias_grad: float32 [2, 1024], P(None, 'shard')
- out_bias_grad: float32 [2, 1024], P(None, 'shard')
All inputs are finite; a program needn't handle non-finite values.
Results may differ from a plain program's by a relative error of at most 0.013.
Values may be sent and summed in bfloat16 or wider, within the bound.
A program may use at most 320 MiB of HBM per device.

v0:
```python
import jax
import jax.numpy as jnp
from jax import lax
from jax.sharding import PartitionSpec as P

HEADS = 16
HEAD_DIM = 64
ROT = 16
LAYERS = 2


EPS = 1e-05
FILL = -1e30


def tables(count):
    places = jnp.arange(count, dtype=jnp.float32)
    rates = 10000.0 ** (-jnp.arange(0, ROT, 2, dtype=jnp.float32) / ROT)
    angles = places[:, None] * rates[None, :]
    cosine = jnp.concatenate([jnp.cos(angles), jnp.cos(angles)], -1)
    sine = jnp.concatenate([jnp.sin(angles), jnp.sin(angles)], -1)
    return (cosine, sine)


def rotate(values, cosine, sine):
    half = ROT // 2
    turned = values[..., :ROT]
    swapped = jnp.concatenate([-turned[..., half:], turned[..., :half]], -1)
    moved = turned * cosine[:, None, :] + swapped * sine[:, None, :]
    return jnp.concatenate([moved, values[..., ROT:]], -1)


def gelu_exact(values):
    return jax.nn.gelu(values, approximate=False)


def contract_rows(left, right):
    return lax.dot_general(
        left, right, (((0,), (0,)), ((), ())), preferred_element_type=jnp.float32
    )


def contract_cols(left, right):
    return lax.dot_general(
        left, right, (((1,), (1,)), ((), ())), preferred_element_type=jnp.float32
    )


def fetch_forward(stacks, layer_at):
    return (
        lax.all_gather(stacks[0][layer_at], "shard", axis=0, tiled=True),
        lax.all_gather(stacks[1][layer_at], "shard", axis=0, tiled=True),
        lax.all_gather(stacks[2][layer_at], "shard", axis=0, tiled=True),
        lax.all_gather(stacks[3][layer_at], "shard", axis=0, tiled=True),
        lax.all_gather(stacks[4][layer_at], "shard", axis=0, tiled=True),
        lax.all_gather(stacks[5][layer_at], "shard", axis=0, tiled=True),
        lax.all_gather(stacks[6][layer_at], "shard", axis=0, tiled=True),
        lax.all_gather(stacks[7][layer_at], "shard", axis=0, tiled=True),
        lax.all_gather(stacks[8][layer_at], "shard", axis=0, tiled=True),
    )


def fetch_backward(stacks, layer_at):
    return (
        lax.all_gather(stacks[0][layer_at], "shard", axis=0, tiled=True),
        lax.all_gather(stacks[1][layer_at], "shard", axis=0, tiled=True),
        lax.all_gather(stacks[2][layer_at], "shard", axis=0, tiled=True),
        lax.all_gather(stacks[3][layer_at], "shard", axis=0, tiled=True),
        lax.all_gather(stacks[4][layer_at], "shard", axis=0, tiled=True),
        lax.all_gather(stacks[5][layer_at], "shard", axis=0, tiled=True),
        lax.all_gather(stacks[6][layer_at], "shard", axis=0, tiled=True),
        lax.all_gather(stacks[7][layer_at], "shard", axis=0, tiled=True),
        lax.all_gather(stacks[8][layer_at], "shard", axis=0, tiled=True),
    )


def reduce_layer(full):
    pieces = (
        lax.psum_scatter(full[0], "shard", scatter_dimension=0, tiled=True),
        lax.psum_scatter(full[1], "shard", scatter_dimension=0, tiled=True),
        lax.psum_scatter(full[2], "shard", scatter_dimension=0, tiled=True),
        lax.psum_scatter(full[3], "shard", scatter_dimension=0, tiled=True),
        lax.psum_scatter(full[4], "shard", scatter_dimension=0, tiled=True),
        lax.psum_scatter(full[5], "shard", scatter_dimension=0, tiled=True),
        lax.psum_scatter(full[6], "shard", scatter_dimension=0, tiled=True),
        lax.psum_scatter(full[7], "shard", scatter_dimension=0, tiled=True),
        lax.psum_scatter(full[8], "shard", scatter_dimension=0, tiled=True),
    )
    return (
        lax.psum(pieces[0].astype(jnp.bfloat16), "rep").astype(jnp.float32),
        lax.psum(pieces[1].astype(jnp.bfloat16), "rep").astype(jnp.float32),
        lax.psum(pieces[2].astype(jnp.bfloat16), "rep").astype(jnp.float32),
        lax.psum(pieces[3].astype(jnp.bfloat16), "rep").astype(jnp.float32),
        lax.psum(pieces[4].astype(jnp.bfloat16), "rep").astype(jnp.float32),
        lax.psum(pieces[5].astype(jnp.bfloat16), "rep").astype(jnp.float32),
        lax.psum(pieces[6].astype(jnp.bfloat16), "rep").astype(jnp.float32),
        lax.psum(pieces[7].astype(jnp.bfloat16), "rep").astype(jnp.float32),
        lax.psum(pieces[8].astype(jnp.bfloat16), "rep").astype(jnp.float32),
    )


def forward_layer(inputs, gathered, cosine, sine, causal):
    w_qkv, b_qkv, w_out, w_up, b_up, w_down, gain, shift, out_bias = gathered
    width = w_out.shape[0]
    count = inputs.shape[0]
    centred = inputs - jnp.mean(inputs, -1, keepdims=True)
    inv_std = lax.rsqrt(jnp.mean(centred * centred, -1, keepdims=True) + EPS)
    normed = centred * inv_std
    hidden = (normed * gain.astype(jnp.float32) + shift.astype(jnp.float32)).astype(jnp.bfloat16)
    joined = jnp.dot(hidden, w_qkv, preferred_element_type=jnp.float32) + b_qkv.astype(jnp.float32)
    split_shape = (count, HEADS, HEAD_DIM)
    query = rotate(joined[:, :width].reshape(split_shape), cosine, sine).astype(jnp.bfloat16)
    key_rot = rotate(joined[:, width : 2 * width].reshape(split_shape), cosine, sine).astype(
        jnp.bfloat16
    )
    values = joined[:, 2 * width :].reshape(split_shape).astype(jnp.bfloat16)
    scores = jnp.einsum(
        "shd,thd->hst", query, key_rot, preferred_element_type=jnp.float32
    ) * HEAD_DIM ** (-0.5)
    scores = jnp.where(causal, scores, FILL)
    highest = jnp.max(scores, -1, keepdims=True)
    expo = jnp.exp(scores - highest)
    total = jnp.sum(expo, -1, keepdims=True)
    probs = (expo / total).astype(jnp.bfloat16)
    log_total = highest + jnp.log(total)
    mixed = jnp.einsum("hst,thd->shd", probs, values, preferred_element_type=jnp.float32)
    mixed = mixed.reshape(count, width).astype(jnp.bfloat16)
    attended = jnp.dot(mixed, w_out, preferred_element_type=jnp.float32)
    upward = jnp.dot(hidden, w_up, preferred_element_type=jnp.float32) + b_up.astype(jnp.float32)
    active = gelu_exact(upward).astype(jnp.bfloat16)
    lowered = jnp.dot(active, w_down, preferred_element_type=jnp.float32)
    outputs = inputs + (attended + lowered) + out_bias.astype(jnp.float32)
    kept = (normed, inv_std, hidden, query, key_rot, values, log_total, mixed, upward, active)
    return (outputs, kept)


def backward_layer(upstream, kept, gathered, cosine, sine, causal):
    w_qkv, b_qkv, w_out, w_up, b_up, w_down, gain, shift, out_bias = gathered
    normed, inv_std, hidden, query, key_rot, values, log_total, mixed, upward, active = kept
    width = w_out.shape[0]
    count = upstream.shape[0]
    split_shape = (count, HEADS, HEAD_DIM)
    out_bias_grad = jnp.sum(upstream, 0)
    up_low = upstream.astype(jnp.bfloat16)
    w_down_grad = contract_rows(active, up_low)
    d_active = contract_cols(up_low, w_down)
    unused, gelu_pull = jax.vjp(gelu_exact, upward)
    d_upward = gelu_pull(d_active)[0].astype(jnp.bfloat16)
    w_up_grad = contract_rows(hidden, d_upward)
    b_up_grad = jnp.sum(d_upward.astype(jnp.float32), 0)
    w_out_grad = contract_rows(mixed, up_low)
    d_mixed = contract_cols(up_low, w_out).astype(jnp.bfloat16).reshape(split_shape)
    scores = jnp.einsum(
        "shd,thd->hst", query, key_rot, preferred_element_type=jnp.float32
    ) * HEAD_DIM ** (-0.5)
    scores = jnp.where(causal, scores, FILL)
    probs_full = jnp.exp(scores - log_total)
    d_probs = jnp.einsum("shd,thd->hst", d_mixed, values, preferred_element_type=jnp.float32)
    row_terms = jnp.sum(d_probs * probs_full, -1, keepdims=True)
    d_scores = (probs_full * (d_probs - row_terms)).astype(jnp.bfloat16)
    d_query = jnp.einsum(
        "hst,thd->shd", d_scores, key_rot, preferred_element_type=jnp.float32
    ) * HEAD_DIM ** (-0.5)
    d_key = jnp.einsum(
        "hst,shd->thd", d_scores, query, preferred_element_type=jnp.float32
    ) * HEAD_DIM ** (-0.5)
    d_values = jnp.einsum(
        "hst,shd->thd", probs_full.astype(jnp.bfloat16), d_mixed, preferred_element_type=jnp.float32
    )
    d_query = rotate(d_query, cosine, -sine).reshape(count, width)
    d_key = rotate(d_key, cosine, -sine).reshape(count, width)
    d_joined = jnp.concatenate([d_query, d_key, d_values.reshape(count, width)], 1).astype(
        jnp.bfloat16
    )
    w_qkv_grad = contract_rows(hidden, d_joined)
    b_qkv_grad = jnp.sum(d_joined.astype(jnp.float32), 0)
    d_hidden = contract_cols(d_joined, w_qkv) + contract_cols(d_upward, w_up)
    gain_grad = jnp.sum(d_hidden * normed, 0)
    shift_grad = jnp.sum(d_hidden, 0)
    scaled = d_hidden * gain.astype(jnp.float32)
    d_inputs = upstream + inv_std * (
        scaled
        - jnp.mean(scaled, -1, keepdims=True)
        - normed * jnp.mean(scaled * normed, -1, keepdims=True)
    )
    full = (
        w_qkv_grad,
        b_qkv_grad,
        w_out_grad,
        w_up_grad,
        b_up_grad,
        w_down_grad,
        gain_grad,
        shift_grad,
        out_bias_grad,
    )
    return (d_inputs, full)


def on_device(
    tokens, w_qkv, b_qkv, w_out, w_up, b_up, w_down, ln_gain, ln_bias, out_bias, out_grad
):
    stacks = (w_qkv, b_qkv, w_out, w_up, b_up, w_down, ln_gain, ln_bias, out_bias)
    count = tokens.shape[0]
    cosine, sine = tables(count)
    causal = jnp.tril(jnp.ones((count, count), jnp.bool_))
    current = tokens.astype(jnp.float32)
    gathered_all = []
    kept_all = []
    for layer_at in range(LAYERS):
        gathered = fetch_forward(stacks, layer_at)
        current, kept = forward_layer(current, gathered, cosine, sine, causal)
        gathered_all.append(gathered)
        kept_all.append(kept)
    outcome = current.astype(jnp.bfloat16)
    upstream = out_grad.astype(jnp.float32)
    shares = [None] * LAYERS
    for layer_at in reversed(range(LAYERS)):
        gathered = fetch_backward(stacks, layer_at)
        upstream, full = backward_layer(
            upstream, kept_all[layer_at], gathered, cosine, sine, causal
        )
        shares[layer_at] = reduce_layer(full)
    stacked = tuple(
        (jnp.stack([shares[depth_at][member] for depth_at in range(LAYERS)]) for member in range(9))
    )
    return (
        outcome,
        upstream,
        stacked[0],
        stacked[1],
        stacked[2],
        stacked[3],
        stacked[4],
        stacked[5],
        stacked[6],
        stacked[7],
        stacked[8],
    )


def solution(mesh):
    placed = (
        P(("rep", "shard"), None),
        P(None, "shard", None),
        P(None, "shard"),
        P(None, "shard", None),
        P(None, "shard", None),
        P(None, "shard"),
        P(None, "shard", None),
        P(None, "shard"),
        P(None, "shard"),
        P(None, "shard"),
        P(("rep", "shard"), None),
    )
    return jax.shard_map(
        on_device,
        mesh=mesh,
        in_specs=placed,
        out_specs=(
            P(("rep", "shard"), None),
            P(("rep", "shard"), None),
            P(None, "shard", None),
            P(None, "shard"),
            P(None, "shard", None),
            P(None, "shard", None),
            P(None, "shard"),
            P(None, "shard", None),
            P(None, "shard"),
            P(None, "shard"),
            P(None, "shard"),
        ),
        check_vma=False,
    )
```

profile of v0, /device:TPU:1, one launch (start us, length us, event | category | flops | bytes accessed | tf_op | source)
XLA Modules:
  0.0 3202.1 jit_solution(5766189878112603238)
XLA Ops:
  25.8 326.4 %all-reduce.21 = (bf16[4096]{0:T(1024)(128)(2,1)S(1)}, bf16[1024]{0:T(1024)(128)(2,1)S(1)}, bf16[1024]{0:T(1024)(128)(2,1)S(1)}, bf16[3072]{0:T(1024)(128)(2,1)S...) all-reduce(bf16[4096]{0:T(1024)(128)(2,1)S(1)} %dynamic-update-slic, ...), channel_id=8, replica_groups=mesh['rep'=2,'shard'=64] {'shard'}, use_global_device_ids=true, to_apply=%add.3 | all-reduce | flops 20480 | bytes 81920
  359.8 2.5 fusion.108
  362.6 4.9 fusion.46
  369.8 2.1 copy.64
  382.6 16.3 multiply_convert_fusion.3
  398.9 7.3 fusion.10
  406.2 2.7 fusion.183
  409.5 65.9 %all-gather.35.cloned.1.call-done = bf16[1,1024,3072]{2,1,0:T(8,128)(2,1)} async-done(((bf16[1,16,3072]{2,1,0:T(8,128)(2,1)}), bf16[1,1024,3072]{2,1,0:T(8,128)(2,1)}) %all-gather.35.cloned.1.call-update) | async-done | bytes 6291472 | tf_op jit(solution)/shard_map/all_gather | solution.py:51
  475.5 4.6 fusion.49
  482.4 2.5 copy.69
  486.2 2.1 slice.373
  488.3 2.5 copy.70
  495.4 1.9 fusion.184
  502.7 2.7 fusion.186
  505.4 10.9 reduce-scatter.13.cloned.1.call-start
  516.4 2.2 fusion.92
  523.3 36.5 %all-gather.39.cloned.1.call-done = bf16[1,1024,4096]{2,1,0:T(8,128)(2,1)} async-done(((bf16[1,16,4096]{2,1,0:T(8,128)(2,1)}), bf16[1,1024,4096]{2,1,0:T(8,128)(2,1)}) %all-gather.39.cloned.1.call-update) | async-done | bytes 8388624 | tf_op jit(solution)/shard_map/all_gather | solution.py:54
  559.8 16.0 multiply_convert_fusion.2
  575.7 67.8 %all-gather.41.cloned.1.call-done = bf16[1,4096,1024]{2,1,0:T(8,128)(2,1)} async-done(((bf16[1,64,1024]{2,1,0:T(8,128)(2,1)}), bf16[1,4096,1024]{2,1,0:T(8,128)(2,1)}) %all-gather.41.cloned.1.call-update) | async-done | bytes 8388624 | tf_op jit(solution)/shard_map/all_gather | solution.py:56
  643.5 12.2 convert_reduce_fusion
  655.7 2.4 fusion.4
  658.2 5.6 multiply_reduce_fusion.2
  665.8 2.7 fusion.185
  670.1 3.3 fusion.105
  673.4 2.0 copy.76
  675.5 3.7 multiply_reduce_fusion
  683.9 6.6 fusion.165
  690.7 7.9 fusion.166
  698.6 9.8 fusion.187
  709.4 9.7 fusion.188
  719.2 11.5 convert_reduce_fusion.1
  732.1 8.3 fusion.167
  741.4 9.7 fusion.189
  755.0 1.8 convert_reduce_fusion.3
  756.9 6.5 fusion.12
  763.5 5.8 fusion.128
  769.4 320.1 %all-reduce.20 = (bf16[3072]{0:T(1024)(128)(2,1)S(1)}, bf16[3072]{0:T(1024)(128)(2,1)S(1)}, bf16[4096]{0:T(1024)(128)(2,1)S(1)}, bf16[4096]{0:T(1024)(128)(2,1)S...) all-reduce(f32[3072]{0:T(1024)S(1)} %convert_reduce_fusion.2, ...), channel_id=23, replica_groups=mesh['rep'=2,'shard'=64] {'shard'}, use_global_device_ids=true, to_apply=%region_22.23.clone | all-reduce | flops 20480 | bytes 122880
  1095.4 6.5 fusion.2
  1104.9 206.4 %reduce-scatter.13.cloned.1.call-done = f32[16,1024]{1,0:T(8,128)} async-done(((f32[1024,1024]{1,0:T(8,128)}), f32[16,1024]{1,0:T(8,128)}) %reduce-scatter.13.cloned.1.call-update) | async-done | bytes 65552 | tf_op jit(solution)/shard_map/reduce_scatter | solution.py:81
  1312.9 185.7 %reduce-scatter.9.cloned.1.call-done = f32[16,3072]{1,0:T(8,128)} async-done(((f32[1024,3072]{1,0:T(8,128)}), f32[16,3072]{1,0:T(8,128)}) %reduce-scatter.9.cloned.1.call-update) | async-done | bytes 196624 | tf_op jit(solution)/shard_map/reduce_scatter | solution.py:79
  1500.2 184.1 %reduce-scatter.11.cloned.1.call-done = f32[16,3072]{1,0:T(8,128)} async-done(((f32[1024,3072]{1,0:T(8,128)}), f32[16,3072]{1,0:T(8,128)}) %reduce-scatter.11.cloned.1.call-update) | async-done | bytes 196624 | tf_op jit(solution)/shard_map/reduce_scatter | solution.py:79
  1685.8 352.8 %reduce-scatter.19.cloned.1.call-done = f32[16,4096]{1,0:T(8,128)} async-done(((f32[1024,4096]{1,0:T(8,128)}), f32[16,4096]{1,0:T(8,128)}) %reduce-scatter.19.cloned.1.call-update) | async-done | bytes 262160 | tf_op jit(solution)/shard_map/reduce_scatter | solution.py:82
  2040.3 355.7 %reduce-scatter.21.cloned.1.call-done = f32[64,1024]{1,0:T(8,128)} async-done(((f32[4096,1024]{1,0:T(8,128)}), f32[64,1024]{1,0:T(8,128)}) %reduce-scatter.21.cloned.1.call-update) | async-done | bytes 262160 | tf_op jit(solution)/shard_map/reduce_scatter | solution.py:84
  2397.5 355.7 %reduce-scatter.17.cloned.1.call-done = f32[16,4096]{1,0:T(8,128)} async-done(((f32[1024,4096]{1,0:T(8,128)}), f32[16,4096]{1,0:T(8,128)}) %reduce-scatter.17.cloned.1.call-update) | async-done | bytes 262160 | tf_op jit(solution)/shard_map/reduce_scatter | solution.py:82
  2754.8 354.9 %reduce-scatter.23.cloned.1.call-done = f32[64,1024]{1,0:T(8,128)} async-done(((f32[4096,1024]{1,0:T(8,128)}), f32[64,1024]{1,0:T(8,128)}) %reduce-scatter.23.cloned.1.call-update) | async-done | bytes 262160 | tf_op jit(solution)/shard_map/reduce_scatter | solution.py:84
  3111.4 2.6 fusion.127
  3114.0 30.5 all-reduce.27.cloned.1.call-done
  3152.0 37.7 %all-reduce.29.cloned.1.call-done = (bf16[1,16,3072]{2,1,0:T(8,128)(2,1)}, bf16[1,16,3072]{2,1,0:T(8,128)(2,1)}, bf16[1,16,4096]{2,1,0:T(8,128)(2,1)}, bf16[1,16...) async-done(((bf16[1,16,3072]{2,1,0:T(8,128)(2,1)}, bf16[1,16,3072]{2,1,0:T(8,128)(2,1)}, bf16[1,16,4096]{2,1,0:T(8,128)(2,1)}, ...) | async-done | bytes 720912 | tf_op jit(solution)/shard_map/psum | solution.py:90
  (319 shorter events, 102.4 us)
Async XLA Ops:
  7.2 352.6 %all-gather.37.cloned.1.call-start = ((), (), s32[]{:S(2)}) async-start(), calls=%async_computation.21 | async-start | bytes 2129920 | tf_op jit(solution)/shard_map/all_gather | solution.py:53
  8.6 354.0 %copy-start.4 = (bf16[256,1024]{1,0:T(8,128)(2,1)S(1)}, bf16[256,1024]{1,0:T(8,128)(2,1)}, u32[]{:S(2)}) copy-start(bf16[256,1024]{1,0:T(8,128)(2,1)} %param.11) | copy-start | bytes 1572868
  8.6 353.9 %all-gather.27.cloned.1.call-start = ((), (), s32[]{:S(2)}) async-start(), calls=%async_computation.16 | async-start | bytes 6389760 | tf_op jit(solution)/shard_map/all_gather | solution.py:51
  10.4 372.2 %all-gather.31.cloned.1.call-start = ((), (), s32[]{:S(2)}) async-start(), calls=%async_computation.18 | async-start | bytes 8519680 | tf_op jit(solution)/shard_map/all_gather | solution.py:54
  12.2 386.8 %all-gather.33.cloned.1.call-start = ((), (), s32[]{:S(2)}) async-start(), calls=%async_computation.19 | async-start | bytes 8519680 | tf_op jit(solution)/shard_map/all_gather | solution.py:56
  13.9 392.3 %all-gather.29.cloned.1.call-start = ((), (), s32[]{:S(2)}) async-start(), calls=%async_computation.17 | async-start | bytes 2129920 | tf_op jit(solution)/shard_map/all_gather | solution.py:53
  14.5 460.9 %all-gather.35.cloned.1.call-start = ((), (), s32[]{:S(2)}) async-start(), calls=%async_computation.20 | async-start | bytes 6389760 | tf_op jit(solution)/shard_map/all_gather | solution.py:51
  15.1 544.7 %all-gather.39.cloned.1.call-start = ((), (), s32[]{:S(2)}) async-start(), calls=%async_computation.22 | async-start | bytes 8519680 | tf_op jit(solution)/shard_map/all_gather | solution.py:54
  15.8 627.6 %all-gather.41.cloned.1.call-start = ((), (), s32[]{:S(2)}) async-start(), calls=%async_computation.23 | async-start | bytes 8519680 | tf_op jit(solution)/shard_map/all_gather | solution.py:56
  16.6 1086.9 %reduce-scatter.15.cloned.1.call-start = ((), (), s32[]{:S(2)}) async-start(), calls=%async_computation.11 | async-start | bytes 4259840 | tf_op jit(solution)/shard_map/reduce_scatter | solution.py:81
  362.5 135.3 %copy-start.17 = (bf16[256,1024]{0,1:T(8,128)(2,1)}, bf16[256,1024]{0,1:T(8,128)(2,1)S(1)}, u32[]{:S(2)}) copy-start(bf16[256,1024]{0,1:T(8,128)(2,1)S(1)} %copy.72) | copy-start | bytes 1572868
  369.8 5.8 copy-start.29
  375.6 4.7 copy-start.36
  377.9 3.8 copy-start.31
  382.5 23.7 copy-start.26
  398.9 7.3 copy-start.59
  409.0 71.1 %copy-start.65 = (f32[256]{0:T(256)}, f32[256]{0:T(256)S(1)}, u32[]{:S(2)}) copy-start(f32[256]{0:T(256)S(1)} %broadcast_multiply_fusion.4) | copy-start | bytes 3076
  409.3 70.8 %copy-start.67 = (f32[256]{0:T(256)}, f32[256]{0:T(256)S(1)}, u32[]{:S(2)}) copy-start(f32[256]{0:T(256)S(1)} %add_rsqrt_fusion) | copy-start | bytes 3076
  486.2 11.7 copy-start.32
  497.3 4.4 copy-start.2
  505.4 10.9 copy-start.39
  505.4 10.9 copy-start.47
  505.4 805.9 %reduce-scatter.13.cloned.1.call-start = ((), (), s32[]{:S(2)}) async-start(), calls=%async_computation.10 | async-start | bytes 4259840 | tf_op jit(solution)/shard_map/reduce_scatter | solution.py:81
  516.4 5.3 copy-start.41
  516.4 6.1 copy-start.3
  516.4 6.1 copy-start.18
  516.4 6.1 copy-start.51
  523.3 134.8 %copy-start.9 = (bf16[16,64,256]{2,1,0:T(8,128)(2,1)}, bf16[16,64,256]{2,1,0:T(8,128)(2,1)S(1)}, u32[]{:S(2)}) copy-start(bf16[16,64,256]{2,1,0:T(8,128)(2,1)S(1)} %fusion.99) | copy-start | bytes 1572868
  643.5 12.2 copy-start.72
  658.2 5.7 copy-start.7
  668.5 830.1 %reduce-scatter.9.cloned.1.call-start = ((), (), s32[]{:S(2)}) async-start(), calls=%async_computation.8 | async-start | bytes 12779520 | tf_op jit(solution)/shard_map/reduce_scatter | solution.py:79
  690.6 993.6 %reduce-scatter.11.cloned.1.call-start = ((), (), s32[]{:S(2)}) async-start(), calls=%async_computation.9 | async-start | bytes 12779520 | tf_op jit(solution)/shard_map/reduce_scatter | solution.py:79
  698.5 1340.1 %reduce-scatter.19.cloned.1.call-start = ((), (), s32[]{:S(2)}) async-start(), calls=%async_computation.13 | async-start | bytes 17039360 | tf_op jit(solution)/shard_map/reduce_scatter | solution.py:82
  708.4 1687.5 %reduce-scatter.21.cloned.1.call-start = ((), (), s32[]{:S(2)}) async-start(), calls=%async_computation.14 | async-start | bytes 17039360 | tf_op jit(solution)/shard_map/reduce_scatter | solution.py:84
  719.2 2034.0 %reduce-scatter.17.cloned.1.call-start = ((), (), s32[]{:S(2)}) async-start(), calls=%async_computation.12 | async-start | bytes 17039360 | tf_op jit(solution)/shard_map/reduce_scatter | solution.py:82
  740.4 2369.4 %reduce-scatter.23.cloned.1.call-start = ((), (), s32[]{:S(2)}) async-start(), calls=%async_computation.15 | async-start | bytes 17039360 | tf_op jit(solution)/shard_map/reduce_scatter | solution.py:84
  751.2 2393.3 %all-reduce.27.cloned.1.call-start = ((), (), s32[]{:S(2)}) async-start(), calls=%async_computation.24 | async-start | bytes 141312 | tf_op jit(solution)/shard_map/psum | solution.py:91
  756.9 6.6 copy-start.14
  756.9 6.6 copy-start.20
  756.9 6.6 copy-start.22
  763.5 5.9 copy-start.60
  763.5 5.9 copy-start.61
  763.5 5.9 copy-start.63
  763.5 5.8 copy-start.69
  763.5 5.8 copy-start.70
  1095.4 6.5 copy-start.25
  1095.4 6.5 copy-start.30
  1312.9 1876.9 %all-reduce.29.cloned.1.call-start = ((), (), s32[]{:S(2)}) async-start(), calls=%async_computation.25 | async-start | bytes 1441792 | tf_op jit(solution)/shard_map/psum | solution.py:90
  (43 other events, 85.5 us)
Sparse Core Ops, SparseCore 0:
  11.9 71.9 all-gather.36
  87.7 73.1 all-gather.26
  164.8 80.4 all-gather.30
  248.5 80.3 all-gather.32
  332.1 67.0 all-gather.28
  402.2 73.2 all-gather.34
  479.3 80.3 all-gather.38
  563.1 80.3 all-gather.40
  645.9 329.9 reduce-scatter.14
  978.2 333.1 reduce-scatter.12
  1317.2 181.3 reduce-scatter.8
  1505.2 178.9 reduce-scatter.10
  1686.6 351.9 reduce-scatter.18
  2040.9 354.9 reduce-scatter.20
  2398.2 354.9 reduce-scatter.16
  2755.5 354.2 reduce-scatter.22
  3114.1 30.3 all-reduce.26
  3147.8 41.9 all-reduce.28
where the time goes:
time: 3210 us; the launch traced here: 3200 us
  waiting for transfers between devices  2240 us (70%)
  blocking collectives  647 us (20%)
  matrix products  183 us (6%)
  other arithmetic  54.8 us (2%)
  local copies, waits for them, and re-layouts  49.6 us (2%)
    reduce_scatter x2, waiting for transfers between devices, reduce_layer(): lax.psum_scatter(full[5], 'shard', scatter_dimension=0, tiled=True)  711 us
    reduce_scatter x2, waiting for transfers between devices, reduce_layer(): lax.psum_scatter(full[3], 'shard', scatter_dimension=0, tiled=True)  708 us
    unnamed x2, blocking collectives  647 us
    reduce_scatter x2, waiting for transfers between devices, reduce_layer(): lax.psum_scatter(full[0], 'shard', scatter_dimension=0, tiled=True)  370 us
    reduce_scatter x2, waiting for transfers between devices, reduce_layer(): lax.psum_scatter(full[2], 'shard', scatter_dimension=0, tiled=True)  206 us
    all_gather x2, waiting for transfers between devices, fetch_forward(): lax.all_gather(stacks[5][layer_at], 'shard', axis=0, tiled=True)  67.8 us
    all_gather x2, waiting for transfers between devices, fetch_forward(): lax.all_gather(stacks[0][layer_at], 'shard', axis=0, tiled=True)  65.9 us
  transfers between devices with their start and end apart: 18, of which 12 were waited for; matrix products, arithmetic and copies ran while one was open for 9% of the time, Pallas kernels for 0%

commit v1 on v0

v1 whole, which is shorter than its diff:
```python
import functools
import jax
import jax.numpy as jnp
from jax import lax
from jax.experimental import pallas as pl
from jax.experimental.pallas import tpu as pltpu
from jax.sharding import PartitionSpec as P

MESH = pl.DeviceIdType.MESH
LANE = 128
LAYERS = 2


def place():
    xl = lax.axis_index("rep")
    s = lax.axis_index("shard")
    return xl, s // 32, (s // 8) % 4, (s // 2) % 4, s % 2


def at(xl, xh, z, y, c):
    return (xl, xh * 32 + z * 8 + y * 2 + c)


def around(value, step):
    return lax.rem(value + (step + 4), 4)


def meet(others):
    barrier = pltpu.get_barrier_semaphore()
    for other in others:
        pl.semaphore_signal(barrier, inc=1, device_id=other, device_id_type=MESH)
    pl.semaphore_wait(barrier, len(others))


GATHERED = (
    ("small", True, 32, 128, 0, 1),
    ("qkv", True, 32, 1536, 4, 8),
    ("up", True, 32, 2048, 5, 11),
    ("out", False, 32, 1024, 3, 5),
    ("down", False, 128, 1024, 3, 5),
)
SLOTS = 18


class Stream:
    def __init__(self, number, spec, source, target, send, recv, xl, xh, z, y, core):
        self.name, self.by_columns, self.rows, self.columns, self.swapped, self.width = spec
        self.number = number
        self.source = source
        self.target = target
        self.send, self.recv = send, recv
        self.xl, self.xh, self.z, self.y, self.core = xl, xh, z, y, core
        self.half = self.rows // 2
        self.wide = pl.ds(pl.multiple_of(xl * (self.swapped * LANE), LANE), self.width * LANE)
        self.mine = pl.ds(
            pl.multiple_of(xl * ((self.width - self.swapped) * LANE) + xl * (self.swapped * LANE), LANE),
            max(self.swapped, 1) * LANE,
        )
        self.theirs = pl.ds(
            pl.multiple_of((1 - xl) * (self.width * LANE), LANE), max(self.swapped, 1) * LANE
        )
        self.across = lambda core_of: at(1 - xl, 1 - xh, z, y, core_of)
        self.partner = at(1 - xl, xh, z, y, core) if core == 0 else self.across(core)
        if core == 0:
            self.first, self.second = y, z
        else:
            self.first, self.second = z, y
        self.sent = []

    def neighbour(self, ring, step):
        z, y = self.z, self.y
        if (ring == 0) == (self.core == 0):
            y = around(y, step)
        else:
            z = around(z, step)
        return at(self.xl, self.xh, z, y, self.core)

    def block(self, first, rows, columns):
        if self.core == 0:
            return self.target.at[:, self.second, first, rows, columns]
        return self.target.at[:, first, self.second, rows, columns]

    def line(self, second, rows, columns):
        if self.core == 0:
            return self.target.at[:, second, :, rows, columns]
        return self.target.at[:, :, second, rows, columns]

    def push(self, source, target, slot, device):
        copy = pltpu.make_async_remote_copy(
            source,
            target,
            self.send.at[self.number, slot],
            self.recv.at[self.number, slot],
            device_id=device,
            device_id_type=MESH,
        )
        copy.start()
        self.sent.append((source, slot))

    def arrived(self, region, slot):
        pltpu.make_async_copy(region, region, self.recv.at[self.number, slot]).wait()

    def part(self, core_of):
        return pl.ds(core_of * self.half, self.half)

    def stage0(self):
        xh, z, y, core = self.xh, self.z, self.y, self.core
        whole = slice(None)
        if self.by_columns:
            here = self.target.at[xh, z, y, self.part(core), :]
            pltpu.make_async_copy(
                self.source(core), here, self.recv.at[self.number, xh * 2 + core]
            ).start()
            for slot, half, device in (
                (0, 1 - core, at(self.xl, xh, z, y, 1 - core)),
                (1, core, self.across(core)),
                (2, 1 - core, self.across(1 - core)),
            ):
                copy = pltpu.make_async_remote_copy(
                    self.source(half),
                    here,
                    self.send.at[self.number, slot],
                    self.recv.at[self.number, xh * 2 + core],
                    device_id=device,
                    device_id_type=MESH,
                )
                copy.start()
                self.sent.append((self.source(half), slot))
        else:
            here = self.target.at[0, z, y, self.part(core), :]
            mine = self.source(0)

            @pl.when(xh == core)
            def _():
                pltpu.make_async_copy(mine, here, self.recv.at[self.number, core]).start()

            @pl.when(xh != core)
            def _():
                pltpu.make_async_remote_copy(
                    mine,
                    here,
                    self.send.at[self.number, 0],
                    self.recv.at[self.number, core],
                    device_id=at(self.xl, xh, z, y, 1 - core),
                    device_id_type=MESH,
                ).start()

            pltpu.make_async_remote_copy(
                mine,
                here,
                self.send.at[self.number, 1],
                self.recv.at[self.number, core],
                device_id=self.across(xh),
                device_id_type=MESH,
            ).start()
            self.sent.append((mine, 1))

    def stage1(self):
        whole = slice(None)
        for bank in range(2 if self.by_columns else 1):
            for core_of in range(2):
                self.arrived(
                    self.target.at[bank, self.z, self.y, self.part(core_of), :], bank * 2 + core_of
                )
        own = self.block(self.first, whole, self.wide)
        self.push(own, own, 4, self.neighbour(0, 1))
        self.push(own, own, 5, self.neighbour(0, -1))

    def share(self, region, slot):
        if self.swapped:
            self.push(region(self.mine), region(self.mine), slot, self.partner)

    def stage2(self):
        whole = slice(None)
        for step, slot in ((-1, 4), (1, 5)):
            origin = around(self.first, step)
            self.arrived(self.block(origin, whole, self.wide), slot)
            half = self.block(origin, self.part(slot - 4), self.wide)
            self.push(half, half, slot + 2, self.neighbour(0, -step))
            self.share(lambda columns: self.block(origin, whole, columns), slot + 8)

    def stage3(self):
        whole = slice(None)
        far = around(self.first, 2)
        for half in range(2):
            self.arrived(self.block(far, self.part(half), self.wide), 6 + half)
        own = self.line(self.second, whole, self.wide)
        self.push(own, own, 8, self.neighbour(1, 1))
        self.push(own, own, 9, self.neighbour(1, -1))
        self.share(lambda columns: self.block(far, whole, columns), 14)

    def stage4(self):
        whole = slice(None)
        for step, slot in ((-1, 8), (1, 9)):
            origin = around(self.second, step)
            self.arrived(self.line(origin, whole, self.wide), slot)
            half = self.line(origin, self.part(slot - 8), self.wide)
            self.push(half, half, slot + 2, self.neighbour(1, -step))
            self.share(lambda columns: self.line(origin, whole, columns), slot + 7)

    def stage5(self):
        whole = slice(None)
        far = around(self.second, 2)
        for half in range(2):
            self.arrived(self.line(far, self.part(half), self.wide), 10 + half)
        self.share(lambda columns: self.line(far, whole, columns), 17)

    def stage6(self):
        whole = slice(None)
        if self.swapped:
            for step, slot in ((-1, 12), (1, 13), (2, 14)):
                self.arrived(self.block(around(self.first, step), whole, self.theirs), slot)
            for step, slot in ((-1, 15), (1, 16), (2, 17)):
                self.arrived(self.line(around(self.second, step), whole, self.theirs), slot)

    def finish(self):
        for source, slot in self.sent:
            pltpu.make_async_copy(source, source, self.send.at[self.number, slot]).wait()
        if not self.by_columns:

            @pl.when(self.xh != self.core)
            def _():
                mine = self.source(0)
                pltpu.make_async_copy(mine, mine, self.send.at[self.number, 0]).wait()


def streams_of(sources, targets, send, recv, core, xl, xh, z, y, layers):
    found = []
    small, qkv, up, out, down = sources
    for layer_at in layers:
        from_args = (
            lambda half: small,
            lambda half, layer_at=layer_at: qkv.at[half, layer_at],
            lambda half, layer_at=layer_at: up.at[layer_at, :, pl.ds(half * 2048, 2048)],
            lambda half, layer_at=layer_at: out.at[layer_at],
            lambda half, layer_at=layer_at: down.at[layer_at],
        )
        for spec, source in zip(GATHERED, from_args):
            if spec[0] == "small" and layer_at != layers[0]:
                continue
            number = len(found)
            found.append(
                Stream(number, spec, source, targets[number], send, recv, xl, xh, z, y, core)
            )
    return found


def gather_kernel(small, qkv, up, out, down, *rest):
    targets, (send, recv) = rest[:-2], rest[-2:]
    xl, xh, z, y, c = place()
    meet(
        [
            at(xl, xh, z, y, 1 - c),
            at(1 - xl, 1 - xh, z, y, c),
            at(1 - xl, 1 - xh, z, y, 1 - c),
            at(1 - xl, xh, z, y, c),
            at(xl, xh, around(z, 1), y, c),
            at(xl, xh, around(z, -1), y, c),
            at(xl, xh, z, around(y, 1), c),
            at(xl, xh, z, around(y, -1), c),
        ]
    )

    def run(core):
        streams = streams_of(
            (small, qkv, up, out, down), targets, send, recv, core, xl, xh, z, y, range(LAYERS)
        )
        for tick in range(len(streams) + 6):
            for stage in range(7):
                if 0 <= tick - stage < len(streams):
                    getattr(streams[tick - stage], f"stage{stage}")()
        for stream in streams:
            stream.finish()

    for core in range(2):
        pl.when(c == core)(functools.partial(run, core))


def gather(small, qkv, up, out, down):
    shapes = []
    for layer_at in range(LAYERS):
        for name, by_columns, rows, columns, swapped, width in GATHERED:
            if name == "small" and layer_at:
                continue
            shapes.append(
                jax.ShapeDtypeStruct((2 if by_columns else 1, 4, 4, rows, columns), jnp.bfloat16)
            )
    return pl.pallas_call(
        gather_kernel,
        out_shape=shapes,
        in_specs=[pl.BlockSpec(memory_space=pltpu.HBM)] * 5,
        out_specs=[pl.BlockSpec(memory_space=pltpu.HBM)] * len(shapes),
        scratch_shapes=[
            pltpu.SemaphoreType.DMA((len(shapes), SLOTS)),
            pltpu.SemaphoreType.DMA((len(shapes), SLOTS)),
        ],
        name="gather",
        compiler_params=pltpu.CompilerParams(collective_id=0, has_side_effects=True),
    )(small, qkv, up, out, down)


def halves(w_qkv):
    rows = w_qkv.shape[1]
    return w_qkv.reshape(LAYERS, rows, 3, 2, 512).transpose(3, 0, 1, 2, 4).reshape(
        2, LAYERS, rows, 1536
    )


SUMMED = (
    ("qkv", True, 32, 1536, 3, 9),
    ("up", True, 32, 2048, 4, 12),
    ("out", False, 32, 1024, 2, 6),
    ("down", False, 128, 1024, 2, 6),
)
SMALL = ("small", True, 16, 128, 0, 1)
SUM_SLOTS = 18


def scratch_of(spec):
    name, by_columns, rows, columns, swapped, width = spec
    banks = 2 if by_columns else 1
    kind = jnp.float32 if name == "small" else jnp.bfloat16
    wide = width * LANE
    return [
        pltpu.VMEM((banks, 4, 4, rows, columns), kind),
        pltpu.VMEM((banks, 4, 4, rows, max(swapped, 1) * LANE) if swapped else (8, LANE), kind),
        pltpu.VMEM((2, banks, 4, rows // 2, wide), kind),
        pltpu.VMEM((2, banks, 4, rows, wide), kind),
        pltpu.VMEM((2, banks, rows // 2, wide), kind),
        pltpu.VMEM((2, banks, rows, wide), kind),
        pltpu.VMEM((3, rows, wide), kind),
        pltpu.VMEM((rows, columns), jnp.float32),
        pltpu.VMEM((2, 8, LANE), jnp.float32),
    ]


class Sum:
    def __init__(self, number, spec, source, outputs, buffers, send, recv, xl, xh, z, y, core):
        self.name, self.by_columns, self.rows, self.columns, self.swapped, self.width = spec
        self.number, self.source, self.outputs = number, source, outputs
        (
            self.total,
            self.swap,
            self.far_line,
            self.near_line,
            self.far_block,
            self.near_block,
            self.last,
            self.ready,
            self.tail,
        ) = buffers
        self.send, self.recv = send, recv
        self.xl, self.xh, self.z, self.y, self.core = xl, xh, z, y, core
        self.banks = 2 if self.by_columns else 1
        self.half = self.rows // 2
        s, w = self.swapped, self.width
        self.wide = pl.ds(pl.multiple_of(xl * (s * LANE), LANE), w * LANE)
        self.mine = pl.ds(pl.multiple_of(xl * (w * LANE), LANE), max(s, 1) * LANE)
        self.theirs = pl.ds(pl.multiple_of((1 - xl) * (w * LANE), LANE), max(s, 1) * LANE)
        self.beside = at(1 - xl, xh, z, y, core)
        self.across = at(1 - xl, 1 - xh, z, y, core)
        self.beyond = at(xl, 1 - xh, z, y, core)
        self.sibling = at(xl, xh, z, y, 1 - core)
        self.partner = self.beside if core == 0 else self.across
        self.first, self.second = (y, z) if core == 0 else (z, y)
        self.sent = []

    def neighbour(self, ring, step):
        z, y = self.z, self.y
        if (ring == 0) == (self.core == 0):
            y = around(y, step)
        else:
            z = around(z, step)
        return at(self.xl, self.xh, z, y, self.core)

    def block(self, first, rows, columns):
        if self.core == 0:
            return self.total.at[:, self.second, first, rows, columns]
        return self.total.at[:, first, self.second, rows, columns]

    def line(self, second, rows, columns):
        if self.core == 0:
            return self.total.at[:, second, :, rows, columns]
        return self.total.at[:, :, second, rows, columns]

    def push(self, source, target, slot, device):
        copy = pltpu.make_async_remote_copy(
            source,
            target,
            self.send.at[self.number, slot],
            self.recv.at[self.number, slot],
            device_id=device,
            device_id_type=MESH,
        )
        copy.start()
        return (source, slot)

    def arrived(self, region, slot):
        pltpu.make_async_copy(region, region, self.recv.at[self.number, slot]).wait()

    def part(self, core_of):
        return pl.ds(core_of * self.half, self.half)

    def stage0(self):
        pltpu.make_async_copy(self.source, self.total, self.recv.at[self.number, 17]).start()

    def stage1(self):
        self.arrived(self.total, 17)
        if self.swapped:
            whole = self.total.at[:, :, :, :, self.theirs]
            self.sent.append(self.push(whole, self.swap, 0, self.partner))

    def stage2(self):
        whole = slice(None)
        if self.swapped:
            self.arrived(self.swap, 0)

            def add(step, carry):
                bank, z, y = step // 16, (step // 4) % 4, step % 4
                self.total[bank, z, y, :, self.mine] = (
                    self.total[bank, z, y, :, self.mine].astype(jnp.float32)
                    + self.swap[bank, z, y].astype(jnp.float32)
                ).astype(self.total.dtype)
                return carry

            lax.fori_loop(0, self.banks * 16, add, 0)
        far = around(self.second, 2)
        for half in range(2):
            self.sent.append(
                self.push(
                    self.line(far, self.part(half), self.wide),
                    self.far_line.at[half],
                    1 + half,
                    self.neighbour(1, 1 - 2 * half),
                )
            )

    def stage3(self):
        for half in range(2):
            self.arrived(self.far_line.at[half], 1 + half)
            to = around(self.second, 1 - 2 * half)
            rows = self.part(half)

            def add(step, carry):
                bank, at_ = step // 4, step % 4
                region = self.line(to, rows, self.wide).at[bank, at_]
                region[...] = (
                    region[...].astype(jnp.float32)
                    + self.far_line[half, bank, at_].astype(jnp.float32)
                ).astype(self.total.dtype)
                return carry

            lax.fori_loop(0, self.banks * 4, add, 0)
            self.sent.append(
                self.push(
                    self.line(to, slice(None), self.wide),
                    self.near_line.at[half],
                    3 + half,
                    self.neighbour(1, 1 - 2 * half),
                )
            )

    def stage4(self):
        for half in range(2):
            self.arrived(self.near_line.at[half], 3 + half)

        def add(step, carry):
            bank, at_ = step // 4, step % 4
            region = self.line(self.second, slice(None), self.wide).at[bank, at_]
            region[...] = (
                region[...].astype(jnp.float32)
                + self.near_line[0, bank, at_].astype(jnp.float32)
                + self.near_line[1, bank, at_].astype(jnp.float32)
            ).astype(self.total.dtype)
            return carry

        lax.fori_loop(0, self.banks * 4, add, 0)
        far = around(self.first, 2)
        for half in range(2):
            self.sent.append(
                self.push(
                    self.block(far, self.part(half), self.wide),
                    self.far_block.at[half],
                    5 + half,
                    self.neighbour(0, 1 - 2 * half),
                )
            )

    def stage5(self):
        for half in range(2):
            self.arrived(self.far_block.at[half], 5 + half)
            to = around(self.first, 1 - 2 * half)
            for bank in range(self.banks):
                region = self.block(to, self.part(half), self.wide).at[bank]
                region[...] = (
                    region[...].astype(jnp.float32)
                    + self.far_block[half, bank].astype(jnp.float32)
                ).astype(self.total.dtype)
            self.sent.append(
                self.push(
                    self.block(to, slice(None), self.wide),
                    self.near_block.at[half],
                    7 + half,
                    self.neighbour(0, 1 - 2 * half),
                )
            )

    def stage6(self):
        for half in range(2):
            self.arrived(self.near_block.at[half], 7 + half)
        own = self.block(self.first, slice(None), self.wide)
        for bank in range(self.banks):
            region = own.at[bank]
            region[...] = (
                region[...].astype(jnp.float32)
                + self.near_block[0, bank].astype(jnp.float32)
                + self.near_block[1, bank].astype(jnp.float32)
            ).astype(self.total.dtype)
        if self.by_columns:
            self.sent.append(self.push(own.at[self.xh], self.last.at[0], 9, self.beside))
            self.sent.append(self.push(own.at[1 - self.xh], self.last.at[1], 10, self.across))
            self.sent.append(self.push(own.at[1 - self.xh], self.last.at[2], 11, self.beyond))
        else:

            @pl.when(self.xh == self.core)
            def _():
                self.push(own.at[0], self.last.at[0], 9, self.beside)

            @pl.when(self.xh != self.core)
            def _():
                self.push(own.at[0], self.last.at[1], 10, self.across)
                self.push(own.at[0], self.last.at[2], 11, self.beyond)

    def add_last(self):
        for slot in range(3):
            self.arrived(self.last.at[slot], 9 + slot)
        s, w = self.swapped, self.width
        c = w - s
        own = self.block(self.first, slice(None), self.wide).at[self.xh if self.by_columns else 0]
        self.ready[:, self.wide] = own[...].astype(jnp.float32) + self.last[2].astype(jnp.float32)
        if s:
            there = pl.ds(pl.multiple_of((1 - self.xl) * (c * LANE), LANE), s * LANE)
            self.ready[:, self.theirs] = self.last[0, :, there].astype(jnp.float32) + self.last[
                1, :, there
            ].astype(jnp.float32)
        middle = pl.ds(s * LANE, c * LANE)
        there = pl.ds(pl.multiple_of(self.xl * (s * LANE), LANE), c * LANE)
        self.ready[:, middle] = (
            self.ready[:, middle]
            + self.last[0, :, there].astype(jnp.float32)
            + self.last[1, :, there].astype(jnp.float32)
        )

    def pieces(self, core_of, target):
        rows = self.part(core_of)
        if self.name == "qkv":
            return [
                (
                    self.ready.at[rows, pl.ds(third * 512, 512)],
                    target.at[:, pl.ds(third * 1024 + self.core * 512, 512)],
                )
                for third in range(3)
            ]
        if self.name == "up":
            return [(self.ready.at[rows, :], target.at[:, pl.ds(self.core * 2048, 2048)])]
        return [(self.ready.at[rows, :], target)]

    def deliver(self):
        core = self.core
        for index, (source, target) in enumerate(self.pieces(core, self.outputs)):
            pltpu.make_async_copy(source, target, self.recv.at[self.number, 15 + index]).start()
        for index, (source, target) in enumerate(self.pieces(1 - core, self.outputs)):
            self.push(source, target, 12 + index, self.sibling)

    def delivered(self):
        for index, (source, target) in enumerate(self.pieces(self.core, self.outputs)):
            pltpu.make_async_copy(source, target, self.recv.at[self.number, 15 + index]).wait()
        for index, (source, target) in enumerate(self.pieces(1 - self.core, self.outputs)):
            pltpu.make_async_copy(source, source, self.send.at[self.number, 12 + index]).wait()

    def stage7(self):
        if self.name == "small":
            self.add_last()
            self.sent.append(
                self.push(
                    self.ready.at[self.part(1 - self.core), :], self.tail.at[0], 12, self.sibling
                )
            )
        elif self.by_columns:
            self.add_last()
            self.deliver()
        else:

            @pl.when(self.xh == self.core)
            def _():
                self.add_last()
                self.deliver()

    def stage8(self):
        core = self.core
        if self.name == "small":
            self.arrived(self.tail.at[0], 12)
            self.tail[1] = self.ready[self.part(core), :] + self.tail[0]
            copy = pltpu.make_async_copy(
                self.tail.at[1], self.outputs, self.recv.at[self.number, 15]
            )
            copy.start()
            copy.wait()
        elif self.by_columns:
            self.delivered()
            for index, (source, target) in enumerate(self.pieces(1 - core, self.outputs)):
                there = target
                self.arrived(source, 12 + index)
        else:

            @pl.when(self.xh == core)
            def _():
                self.delivered()

            @pl.when(self.xh != core)
            def _():
                self.arrived(self.outputs, 12)

        for source, slot in self.sent:
            pltpu.make_async_copy(source, source, self.send.at[self.number, slot]).wait()
        if not self.by_columns:
            own = self.block(self.first, slice(None), self.wide).at[0]

            @pl.when(self.xh == core)
            def _():
                pltpu.make_async_copy(own, own, self.send.at[self.number, 9]).wait()

            @pl.when(self.xh != core)
            def _():
                pltpu.make_async_copy(own, own, self.send.at[self.number, 10]).wait()
                pltpu.make_async_copy(own, own, self.send.at[self.number, 11]).wait()


def plan(layers):
    found = []
    for layer_at in reversed(range(layers)):
        for which, spec in enumerate(SUMMED):
            found.append((spec, layer_at, which))
    found.insert(len(found) - 3, (SMALL, None, 4))
    return found


def scatter_kernel(streams, *rest):
    count = len(streams)
    sources, rest = rest[:count], rest[count:]
    outputs, rest = rest[:5], rest[5:]
    buffers, (send, recv) = rest[:-2], rest[-2:]
    xl, xh, z, y, c = place()
    meet(
        [
            at(xl, xh, z, y, 1 - c),
            at(1 - xl, 1 - xh, z, y, c),
            at(xl, 1 - xh, z, y, c),
            at(1 - xl, xh, z, y, c),
            at(xl, xh, around(z, 1), y, c),
            at(xl, xh, around(z, -1), y, c),
            at(xl, xh, z, around(y, 1), c),
            at(xl, xh, z, around(y, -1), c),
        ]
    )

    def run(core):
        sums = []
        for number, (spec, layer_at, which) in enumerate(streams):
            target = outputs[which] if layer_at is None else outputs[which].at[layer_at]
            sums.append(
                Sum(
                    number,
                    spec,
                    sources[number],
                    target,
                    buffers[9 * number : 9 * number + 9],
                    send,
                    recv,
                    xl,
                    xh,
                    z,
                    y,
                    core,
                )
            )
        for item in sums:
            item.stage0()
        for tick in range(len(sums) + 7):
            for stage in range(1, 9):
                if 0 <= tick - (stage - 1) < len(sums):
                    getattr(sums[tick - (stage - 1)], f"stage{stage}")()

    for core in range(2):
        pl.when(c == core)(functools.partial(run, core))


def scatter(grads, small):
    streams = plan(LAYERS)
    sources = [
        small if layer_at is None else grads[layer_at][which] for spec, layer_at, which in streams
    ]
    scratch = []
    for spec, layer_at, which in streams:
        scratch.extend(scratch_of(spec))
    f32 = jnp.float32
    return pl.pallas_call(
        functools.partial(scatter_kernel, streams),
        out_shape=[
            jax.ShapeDtypeStruct((LAYERS, 16, 3072), f32),
            jax.ShapeDtypeStruct((LAYERS, 16, 4096), f32),
            jax.ShapeDtypeStruct((LAYERS, 16, 1024), f32),
            jax.ShapeDtypeStruct((LAYERS, 64, 1024), f32),
            jax.ShapeDtypeStruct((8, LANE), f32),
        ],
        in_specs=[pl.BlockSpec(memory_space=pltpu.HBM)] * len(sources),
        out_specs=[pl.BlockSpec(memory_space=pltpu.HBM)] * 5,
        scratch_shapes=scratch
        + [
            pltpu.SemaphoreType.DMA((len(streams), SUM_SLOTS)),
            pltpu.SemaphoreType.DMA((len(streams), SUM_SLOTS)),
        ],
        name="scatter",
        compiler_params=pltpu.CompilerParams(
            collective_id=1, has_side_effects=True, vmem_limit_bytes=60 * 2**20
        ),
    )(*sources)


HEADS = 16
HEAD_DIM = 64
ROT = 16
EPS = 1e-05
FILL = -1e30


def tables(count):
    places = jnp.arange(count, dtype=jnp.float32)
    rates = 10000.0 ** (-jnp.arange(0, ROT, 2, dtype=jnp.float32) / ROT)
    angles = places[:, None] * rates[None, :]
    cosine = jnp.concatenate([jnp.cos(angles), jnp.cos(angles)], -1)
    sine = jnp.concatenate([jnp.sin(angles), jnp.sin(angles)], -1)
    return (cosine, sine)


def rotate(values, cosine, sine):
    half = ROT // 2
    turned = values[..., :ROT]
    swapped = jnp.concatenate([-turned[..., half:], turned[..., :half]], -1)
    moved = turned * cosine[:, None, :] + swapped * sine[:, None, :]
    return jnp.concatenate([moved, values[..., ROT:]], -1)


def gelu_exact(values):
    return jax.nn.gelu(values, approximate=False)


def contract_rows(left, right):
    return lax.dot_general(
        left, right, (((0,), (0,)), ((), ())), preferred_element_type=jnp.float32
    )


def contract_cols(left, right):
    return lax.dot_general(
        left, right, (((1,), (1,)), ((), ())), preferred_element_type=jnp.float32
    )


def exchange(values):
    return lax.ppermute(values, "shard", [(s, s ^ 1) for s in range(64)])


def forward_layer(inputs, gathered, cosine, sine, causal):
    w_qkv, b_qkv, w_out, w_up, b_up, w_down, gain, shift, out_bias = gathered
    count = inputs.shape[0]
    centred = inputs - jnp.mean(inputs, -1, keepdims=True)
    inv_std = lax.rsqrt(jnp.mean(centred * centred, -1, keepdims=True) + EPS)
    normed = centred * inv_std
    hidden = (normed * gain + shift).astype(jnp.bfloat16)
    hidden = jnp.concatenate([hidden, exchange(hidden)], 0)
    joined = jnp.dot(hidden, w_qkv, preferred_element_type=jnp.float32) + b_qkv
    split_shape = (2, count, 8, HEAD_DIM)
    query = rotate(joined[:, :512].reshape(split_shape), cosine, sine).astype(jnp.bfloat16)
    key_rot = rotate(joined[:, 512:1024].reshape(split_shape), cosine, sine).astype(jnp.bfloat16)
    values = joined[:, 1024:].reshape(split_shape).astype(jnp.bfloat16)
    scores = jnp.einsum(
        "gshd,gthd->ghst", query, key_rot, preferred_element_type=jnp.float32
    ) * HEAD_DIM ** (-0.5)
    scores = jnp.where(causal, scores, FILL)
    highest = jnp.max(scores, -1, keepdims=True)
    expo = jnp.exp(scores - highest)
    total = jnp.sum(expo, -1, keepdims=True)
    probs = (expo / total).astype(jnp.bfloat16)
    log_total = highest + jnp.log(total)
    mixed = jnp.einsum("ghst,gthd->gshd", probs, values, preferred_element_type=jnp.float32)
    mixed = mixed.reshape(2 * count, 512).astype(jnp.bfloat16)
    attended = jnp.dot(mixed, w_out, preferred_element_type=jnp.float32)
    upward = jnp.dot(hidden, w_up, preferred_element_type=jnp.float32) + b_up
    active = gelu_exact(upward).astype(jnp.bfloat16)
    lowered = jnp.dot(active, w_down, preferred_element_type=jnp.float32)
    partial = attended + lowered
    outputs = inputs + (partial[:count] + exchange(partial[count:])) + out_bias
    kept = (normed, inv_std, hidden, query, key_rot, values, log_total, mixed, upward, active)
    return (outputs, kept)


def backward_layer(upstream, kept, gathered, cosine, sine, causal):
    w_qkv, b_qkv, w_out, w_up, b_up, w_down, gain, shift, out_bias = gathered
    normed, inv_std, hidden, query, key_rot, values, log_total, mixed, upward, active = kept
    count = upstream.shape[0]
    split_shape = (2, count, 8, HEAD_DIM)
    out_bias_grad = jnp.sum(upstream, 0)
    up_low = upstream.astype(jnp.bfloat16)
    up_low = jnp.concatenate([up_low, exchange(up_low)], 0)
    w_down_grad = contract_rows(active, up_low).astype(jnp.bfloat16)
    d_active = contract_cols(up_low, w_down)
    unused, gelu_pull = jax.vjp(gelu_exact, upward)
    d_upward = gelu_pull(d_active)[0].astype(jnp.bfloat16)
    w_up_grad = contract_rows(hidden, d_upward).astype(jnp.bfloat16)
    b_up_grad = jnp.sum(d_upward.astype(jnp.float32), 0)
    w_out_grad = contract_rows(mixed, up_low).astype(jnp.bfloat16)
    d_mixed = contract_cols(up_low, w_out).astype(jnp.bfloat16).reshape(split_shape)
    scores = jnp.einsum(
        "gshd,gthd->ghst", query, key_rot, preferred_element_type=jnp.float32
    ) * HEAD_DIM ** (-0.5)
    scores = jnp.where(causal, scores, FILL)
    probs_full = jnp.exp(scores - log_total)
    d_probs = jnp.einsum("gshd,gthd->ghst", d_mixed, values, preferred_element_type=jnp.float32)
    row_terms = jnp.sum(d_probs * probs_full, -1, keepdims=True)
    d_scores = (probs_full * (d_probs - row_terms)).astype(jnp.bfloat16)
    d_query = jnp.einsum(
        "ghst,gthd->gshd", d_scores, key_rot, preferred_element_type=jnp.float32
    ) * HEAD_DIM ** (-0.5)
    d_key = jnp.einsum(
        "ghst,gshd->gthd", d_scores, query, preferred_element_type=jnp.float32
    ) * HEAD_DIM ** (-0.5)
    d_values = jnp.einsum(
        "ghst,gshd->gthd", probs_full.astype(jnp.bfloat16), d_mixed,
        preferred_element_type=jnp.float32,
    )
    wide = (2 * count, 512)
    d_query = rotate(d_query, cosine, -sine).reshape(wide)
    d_key = rotate(d_key, cosine, -sine).reshape(wide)
    d_joined = jnp.concatenate([d_query, d_key, d_values.reshape(wide)], 1).astype(jnp.bfloat16)
    w_qkv_grad = contract_rows(hidden, d_joined).astype(jnp.bfloat16)
    b_qkv_grad = jnp.sum(d_joined.astype(jnp.float32), 0)
    d_hidden = contract_cols(d_joined, w_qkv) + contract_cols(d_upward, w_up)
    d_hidden = d_hidden[:count] + exchange(d_hidden[count:])
    gain_grad = jnp.sum(d_hidden * normed, 0)
    shift_grad = jnp.sum(d_hidden, 0)
    scaled = d_hidden * gain
    d_inputs = upstream + inv_std * (
        scaled
        - jnp.mean(scaled, -1, keepdims=True)
        - normed * jnp.mean(scaled * normed, -1, keepdims=True)
    )
    large = (w_qkv_grad, w_up_grad, w_out_grad, w_down_grad)
    small = (b_qkv_grad, b_up_grad, gain_grad, shift_grad, out_bias_grad)
    return (d_inputs, large, small)


def pack_small(b_qkv, b_up, ln_gain, ln_bias, out_bias):
    own = jnp.concatenate([b_qkv, b_up, ln_gain, ln_bias, out_bias], 1).reshape(320)
    return jnp.pad(own, (0, 2048 - 320)).reshape(16, 128)


def unpack_small(full, core):
    rows = full.reshape(64, 2048)[:, :320].reshape(64, 2, 160).astype(jnp.float32)
    layers = []
    for layer_at in range(LAYERS):
        b_qkv = rows[:, layer_at, :48].reshape(3, 2, 512)
        b_qkv = lax.dynamic_index_in_dim(b_qkv, core, 1, False).reshape(1536)
        b_up = rows[:, layer_at, 48:112].reshape(2, 2048)
        b_up = lax.dynamic_index_in_dim(b_up, core, 0, False)
        rest = [rows[:, layer_at, 112 + 16 * i : 128 + 16 * i].reshape(1024) for i in range(3)]
        layers.append((b_qkv, b_up, *rest))
    return layers


def pack_small_grads(layers, core):
    flag = jnp.stack([core == 0, core == 1]).astype(jnp.float32)
    found = []
    for b_qkv, b_up, gain, shift, out_bias in layers:
        found.append((b_qkv.reshape(3, 1, 512) * flag[None, :, None]).reshape(64, 48))
        found.append((b_up.reshape(1, 2048) * flag[:, None]).reshape(64, 64))
        found.extend([gain.reshape(64, 16), shift.reshape(64, 16), out_bias.reshape(64, 16)])
    return jnp.pad(jnp.concatenate(found, 1), ((0, 0), (0, 704))).reshape(2, 4, 4, 16, 128)


def on_device(
    tokens, w_qkv, b_qkv, w_out, w_up, b_up, w_down, ln_gain, ln_bias, out_bias, out_grad
):
    core = lax.axis_index("shard") % 2
    count = tokens.shape[0]
    cosine, sine = tables(count)
    causal = jnp.tril(jnp.ones((count, count), jnp.bool_))
    found = gather(
        pack_small(b_qkv, b_up, ln_gain, ln_bias, out_bias), halves(w_qkv), w_up, w_out, w_down
    )
    small = unpack_small(found[0], core)
    current = tokens.astype(jnp.float32)
    gathered_all = []
    kept_all = []
    for layer_at in range(LAYERS):
        wq, wu, wo, wd = found[1 + 4 * layer_at : 5 + 4 * layer_at]
        bq, bu, gain, shift, ob = small[layer_at]
        gathered = (
            wq.reshape(1024, 1536),
            bq,
            wo.reshape(512, 1024),
            wu.reshape(1024, 2048),
            bu,
            wd.reshape(2048, 1024),
            gain,
            shift,
            ob,
        )
        current, kept = forward_layer(current, gathered, cosine, sine, causal)
        gathered_all.append(gathered)
        kept_all.append(kept)
    outcome = current.astype(jnp.bfloat16)
    upstream = out_grad.astype(jnp.float32)
    large = [None] * LAYERS
    small_grads = [None] * LAYERS
    for layer_at in reversed(range(LAYERS)):
        upstream, large[layer_at], small_grads[layer_at] = backward_layer(
            upstream, kept_all[layer_at], gathered_all[layer_at], cosine, sine, causal
        )
    blocks = []
    for layer_at in range(LAYERS):
        q, u, o, d = large[layer_at]
        blocks.append(
            [
                q.reshape(2, 4, 4, 32, 1536),
                u.reshape(2, 4, 4, 32, 2048),
                o.reshape(1, 4, 4, 32, 1024),
                d.reshape(1, 4, 4, 128, 1024),
            ]
        )
    g_qkv, g_up, g_out, g_down, g_small = scatter(blocks, pack_small_grads(small_grads, core))
    g_small = g_small.reshape(1024)[:320].reshape(2, 160)
    return (
        outcome,
        upstream,
        g_qkv,
        g_small[:, :48],
        g_out,
        g_up,
        g_small[:, 48:112],
        g_down,
        g_small[:, 112:128],
        g_small[:, 128:144],
        g_small[:, 144:160],
    )


def solution(mesh):
    placed = (
        P(("rep", "shard"), None),
        P(None, "shard", None),
        P(None, "shard"),
        P(None, "shard", None),
        P(None, "shard", None),
        P(None, "shard"),
        P(None, "shard", None),
        P(None, "shard"),
        P(None, "shard"),
        P(None, "shard"),
        P(("rep", "shard"), None),
    )
    return jax.shard_map(
        on_device,
        mesh=mesh,
        in_specs=placed,
        out_specs=(
            P(("rep", "shard"), None),
            P(("rep", "shard"), None),
            P(None, "shard", None),
            P(None, "shard"),
            P(None, "shard", None),
            P(None, "shard", None),
            P(None, "shard"),
            P(None, "shard", None),
            P(None, "shard"),
            P(None, "shard"),
            P(None, "shard"),
        ),
        check_vma=False,
    )
```

time: 3210 us -> 539 us (0.17)
  waiting for transfers between devices: 2240 us -> 0.13 us
  blocking collectives: 647 us -> 0 us
  Pallas kernels: 0 us -> 268 us
  matrix products: 183 us -> 112 us
  local copies, waits for them, and re-layouts: 49.6 us -> 120 us
    reduce_scatter x8 -> x0, waiting for transfers between devices: 2000 us -> none  [the longest x2 711 us: reduce_layer(): lax.psum_scatter(full[5], 'shard', scatter_dimension=0, tiled=True)]
    unnamed x2 -> x0, blocking collectives: 647 us -> none
    pallas_call x0 -> x2, Pallas kernels: none -> 268 us  [the longest x1 142 us: scatter(): pl.pallas_call(functools.partial(scatter_kernel, streams), out_shape=[jax...]
    all_gather x8 -> x0, waiting for transfers between devices: 170 us -> none  [the longest x2 67.8 us: fetch_forward(): lax.all_gather(stacks[5][layer_at], 'shard', axis=0, tiled=True)]
    psum x2 -> x0, waiting for transfers between devices: 68.2 us -> none  [the longest x1 37.7 us: reduce_layer(): lax.psum(pieces[0].astype(jnp.bfloat16), 'rep').astype(jnp.float32)]
    unnamed x172 -> x261, local copies, waits for them, and re-layouts: 13.9 us -> 46.9 us
  transfers between devices with their start and end apart: 18 -> 8, of which waited for: 12 -> 1; matrix products, arithmetic and copies ran while one was open for 9% -> 10% of each run, Pallas kernels for 0% -> 0%
where the time goes in v1:
time: 539 us; the launch traced here: 531 us
  Pallas kernels  268 us (50%)
  local copies, waits for them, and re-layouts  120 us (22%)
  matrix products  112 us (21%)
  other arithmetic  24.2 us (4%)
    pallas_call x1, Pallas kernels, scatter(): pl.pallas_call(functools.partial(scatter_kernel, streams), out_shape=[jax...  142 us
    pallas_call x1, Pallas kernels, gather(): pl.pallas_call(gather_kernel, out_shape=shapes, in_specs=[pl.BlockSpec(me...  127 us
    unnamed x261, local copies, waits for them, and re-layouts  46.9 us
    dot_general x8, matrix products, contract_rows(): lax.dot_general(left, right, (((0,), (0,)), ((), ())), preferred_element_...  34.8 us
    dot_general x8, matrix products, contract_cols(): lax.dot_general(left, right, (((1,), (1,)), ((), ())), preferred_element_...  33.1 us
    dot_general x2, matrix products, forward_layer(): upward = jnp.dot(hidden, w_up, preferred_element_type=jnp.float32) + b_up  17.1 us
  transfers between devices with their start and end apart: 8, of which 1 were waited for; matrix products, arithmetic and copies ran while one was open for 10% of the time, Pallas kernels for 0%

profile of v1, /device:TPU:1, one launch (start us, length us, event | category | flops | bytes accessed | tf_op | source)
XLA Modules:
  0.0 531.4 jit_solution(6166211682383136236)
XLA Ops:
  6.9 126.7 %gather.1 = (bf16[2,4,4,32,128]{4,3,2,1,0:T(8,128)(2,1)}, bf16[2,4,4,32,1536]{4,3,2,1,0:T(8,128)(2,1)}, bf16[2,4,4,32,2048]{4,3,2,1,0:T(8,128)(2,1)}, bf16[1,4,4...) custom-call(bf16[16,128]{1,0:T(8,128)(2,1)} %pad_bitcast_fusion.smal, ...), custom_call_target="tpu_custom_call" | custom-call | tf_op jit(solution)/shard_map/gather/pallas_call | solution.py:288
  140.3 3.9 convolution_add_fusion.1
  146.3 1.8 reshape.375
  149.4 2.6 fusion.100
  152.0 1.7 reshape.374
  153.7 3.1 slice.287
  156.8 2.7 fusion.99
  162.5 3.0 copy.169
  165.4 1.7 copy.172
  169.9 2.2 copy.174
  174.1 2.2 copy.170
  176.3 2.2 copy.171
  179.3 1.8 fusion.102
  185.3 13.6 %multiply_convert_fusion.3 = (bf16[512,2048]{1,0:T(8,128)(2,1)S(1)}, f32[512,2048]{1,0:T(8,128)}, f32[512,2048]{1,0:T(8,128)}) fusion(f32[2048]{0:T(1024)S(1)} %bitcast.177, bf16[1024,2048]{1,0:T(8,128)(2,1)S(1)} %bitcast.180, bf16[256,1024]{1,0:T(8,128)(2,1)S(1)} %copy-done.105, bf16[256,1024]{1,0:T(8,128)(2,1)S(1)} %copy-done.40), kind=kOutput, calls=%fused_computation.30 | convolution fusion | flops 2218786816 | bytes 15736832 | tf_op jit(solution)/shard_map/dot_general | solution.py:799
  198.9 2.3 fusion.104
  214.7 3.9 convolution_add_fusion
  223.8 2.6 fusion.98
  226.4 2.8 reshape.377
  229.2 3.0 slice.305
  232.2 2.6 fusion.97
  234.9 2.5 reshape.376
  237.4 2.5 copy.122
  239.9 2.9 copy.177
  245.9 2.6 copy.184
  248.5 2.8 copy.182
  254.2 2.2 copy.178
  256.5 2.2 copy.179
  269.4 3.6 fusion.88
  273.0 12.5 %convert_reduce_fusion = (f32[2048]{0:T(1024)S(1)}, bf16[512,2048]{1,0:T(8,128)(2,1)S(1)}, f32[512,2048]{1,0:T(8,128)S(1)}) fusion(f32[512,2048]{1,0:T(8,128)S(1)} %fusion.88, f32[2048]{0:T(1024)S(1)} %bitcast.175, bf16[512,1024]{1,0:T(8,128)(2,1)S(1)} %copy-done.57, bf16[2048,1024]{1,0:T(8,128)(2,1)S(1)} %bitcast.184), kind=kOutput, calls=%fused_computation.4 | convolution fusion | flops 2226124800 | bytes 15745024 | tf_op jit(solution)/shard_map/dot_general | solution.py:765
  285.5 2.4 fusion.106
  289.0 2.4 fusion.105
  293.3 1.9 convolution_add_fusion.5
  296.2 4.5 convolution_convert_fusion.5
  300.7 5.5 %convolution_convert_fusion.4 = bf16[1024,2048]{1,0:T(8,128)(2,1)} fusion(bf16[512,2048]{1,0:T(8,128)(2,1)S(1)} %get-tuple-element.58, bf16[256,1024]{1,0:T(8,128)(2,1)} %collective-permute-done.2, bf16[256,1024]{1,0:T(8,128)(2,1)S(1)} %copy-done.44), kind=kOutput, calls=%fused_computation.52 | convolution fusion | flops 2151677952 | bytes 7340032 | tf_op jit(solution)/shard_map/dot_general | solution.py:759
  306.3 1.7 convolution_convert_fusion.7
  312.1 6.3 %convolution_convert_fusion.3 = bf16[2048,1024]{1,0:T(8,128)(2,1)} fusion(bf16[512,2048]{1,0:T(8,128)(2,1)} %copy-done.18, bf16[512,1024]{1,0:T(8,128)(2,1)} %copy-done.56), kind=kOutput, calls=%fused_computation.51 | convolution fusion | flops 2149580800 | bytes 7340032 | tf_op jit(solution)/shard_map/dot_general | solution.py:759
  321.1 2.6 convolution_convert_fusion.8
  326.0 3.9 fusion.44
  336.6 6.0 %convert_reduce_fusion.1 = (f32[2048]{0:T(1024)}, bf16[512,2048]{1,0:T(8,128)(2,1)S(1)}) fusion(f32[512,2048]{1,0:T(8,128)S(1)} %copy-done.112, bf16[2048,1024]{1,0:T(8,128)(2,1)S(1)} %bitcast.183, bf16[256,1024]{1,0:T(8,128)(2,1)} %collective-permute-done.6, bf16[256,1024]{1,0:T(8,128)(2,1)S(1)} %copy-done.37, f32[512,2048]{1,0:T(8,128)S(1)} %copy-done.113, ...), kind=kOutput, calls=%fused_computation.5 | convolution fusion | flops 2167404544 | bytes 15745024 | tf_op jit(solution)/shard_map/dot_general | solution.py:765
  342.7 3.8 fusion.107
  355.5 3.2 convolution_add_fusion.4
  360.9 2.7 convolution_convert_fusion.6
  363.7 3.5 convolution_convert_fusion.2
  367.5 6.2 %convolution_convert_fusion = bf16[2048,1024]{1,0:T(8,128)(2,1)} fusion(bf16[512,2048]{1,0:T(8,128)(2,1)} %copy-done.111, bf16[256,1024]{1,0:T(8,128)(2,1)} %collective-permute-done.6, bf16[256,1024]{1,0:T(8,128)(2,1)S(1)} %copy-done.38), kind=kOutput, calls=%fused_computation.48 | convolution fusion | flops 2151677952 | bytes 7340032 | tf_op jit(solution)/shard_map/dot_general | solution.py:759
  373.8 4.4 convolution_convert_fusion.1
  378.3 1.8 fusion.56
  381.2 141.7 %scatter.1 = (f32[2,16,3072]{2,1,0:T(8,128)}, f32[2,16,4096]{2,1,0:T(8,128)}, f32[2,16,1024]{2,1,0:T(8,128)}, f32[2,64,1024]{2,1,0:T(8,128)}, f32[8,128]{1,0:T(8,128)}) custom-call(bf16[2,4,4,32,1536]{4,3,2,1,0:T(8,128)(2,1)} %bitcast.148, bf16[2,4,4,32,2048]{4,3,2,1,0:T(8,128)(2,1)} %bitcast.144, bf16[1,4,4,32,1024]{4,3,2,1,0:T(8,128)(2,1)} %bitcast.168, ...), custom_call_target="tpu_custom_call" | custom-call | tf_op jit(solution)/shard_map/scatter/pallas_call | solution.py:707
  526.9 1.8 copy.204
  (411 shorter events, 102.3 us)
Async XLA Ops:
  0.6 135.5 %copy-start.4 = (bf16[256,1024]{1,0:T(8,128)(2,1)S(1)}, bf16[256,1024]{1,0:T(8,128)(2,1)}, u32[]{:S(2)}) copy-start(bf16[256,1024]{1,0:T(8,128)(2,1)} %param.11) | copy-start | bytes 1572868
  2.8 141.4 %copy-start.82 = (f32[256]{0:T(256)}, f32[256]{0:T(256)S(1)}, u32[]{:S(2)}) copy-start(f32[256]{0:T(256)S(1)} %broadcast_multiply_fusion.7) | copy-start | bytes 3076
  4.2 140.1 %copy-start.86 = (f32[256]{0:T(256)}, f32[256]{0:T(256)S(1)}, u32[]{:S(2)}) copy-start(f32[256]{0:T(256)S(1)} %add_rsqrt_fusion.1) | copy-start | bytes 3076
  136.1 8.2 %copy-start.71 = (f32[1024]{0:T(1024)}, f32[1024]{0:T(1024)S(1)}, u32[]{:S(2)}) copy-start(f32[1024]{0:T(1024)S(1)} %mul.422) | copy-start | bytes 12292
  136.5 7.8 %copy-start.39 = (bf16[256,1024]{1,0:T(8,128)(2,1)}, bf16[256,1024]{1,0:T(8,128)(2,1)S(1)}, u32[]{:S(2)}) copy-start(bf16[256,1024]{1,0:T(8,128)(2,1)S(1)} %fusion.51) | copy-start | bytes 1572868
  136.5 3.9 collective-permute-start
  162.5 6.1 %copy-start.11 = (bf16[2,256,8,48]{3,2,1,0:T(8,128)(2,1)S(1)}, bf16[2,256,8,48]{3,2,1,0:T(8,128)(2,1)}, u32[]{:S(2)}) copy-start(bf16[2,256,8,48]{3,2,1,0:T(8,128)(2,1)} %slice.292) | copy-start | bytes 1179652
  167.1 12.2 %copy-start.23 = (bf16[2,256,8,48]{1,3,2,0:T(8,128)(2,1)}, bf16[2,256,8,48]{1,3,2,0:T(8,128)(2,1)S(1)}, u32[]{:S(2)}) copy-start(bf16[2,256,8,48]{1,3,2,0:T(8,128)(2,1)S(1)} %copy.172) | copy-start | bytes 1179652
  169.9 8.6 %copy-start.29 = (f32[2,256,8,16]{1,3,2,0:T(8,128)S(1)}, f32[2,256,8,16]{1,3,2,0:T(8,128)}, u32[]{:S(2)}) copy-start(f32[2,256,8,16]{1,3,2,0:T(8,128)} %copy.169) | copy-start | bytes 786436
  169.9 8.6 %copy-start.31 = (f32[2,256,8,16]{1,3,2,0:T(8,128)S(1)}, f32[2,256,8,16]{1,3,2,0:T(8,128)}, u32[]{:S(2)}) copy-start(f32[2,256,8,16]{1,3,2,0:T(8,128)} %copy.173) | copy-start | bytes 786436
  172.8 6.6 %copy-start.25 = (bf16[2,256,8,48]{1,3,2,0:T(8,128)(2,1)S(1)}, bf16[2,256,8,48]{1,3,2,0:T(8,128)(2,1)}, u32[]{:S(2)}) copy-start(bf16[2,256,8,48]{1,3,2,0:T(8,128)(2,1)} %copy.176) | copy-start | bytes 1179652
  183.8 17.4 %copy-start.21 = (bf16[64,8,2,256]{3,1,2,0:T(8,128)(2,1)}, bf16[64,8,2,256]{3,1,2,0:T(8,128)(2,1)S(1)}, u32[]{:S(2)}) copy-start(bf16[64,8,2,256]{3,1,2,0:T(8,128)(2,1)S(1)} %copy.185) | copy-start | bytes 1572868
  185.3 13.6 %copy-start.98 = (bf16[1,4,4,128,1024]{4,3,2,1,0:T(8,128)(2,1)S(1)}, bf16[1,4,4,128,1024]{4,3,2,1,0:T(8,128)(2,1)}, u32[]{:S(2)}) copy-start(bf16[1,4,4,128,1024]{4,3,2,1,0:T(8,128)(2,1)} %get-tuple-element.29) | copy-start | bytes 12582916
  201.3 5.5 %copy-start.5 = (bf16[256,1024]{1,0:T(8,128)(2,1)S(1)}, bf16[256,1024]{1,0:T(8,128)(2,1)}, u32[]{:S(2)}) copy-start(bf16[256,1024]{1,0:T(8,128)(2,1)} %param.11) | copy-start | bytes 1572868
  203.5 3.3 collective-permute-start.1
  204.0 5.3 collective-permute-start.4
  206.0 5.4 %copy-start.34 = (bf16[1,4,4,32,1024]{4,3,2,1,0:T(8,128)(2,1)S(1)}, bf16[1,4,4,32,1024]{4,3,2,1,0:T(8,128)(2,1)}, u32[]{:S(2)}) copy-start(bf16[1,4,4,32,1024]{4,3,2,1,0:T(8,128)(2,1)} %get-tuple-element.31) | copy-start | bytes 3145732
  208.5 5.5 %copy-start.89 = (f32[256]{0:T(256)}, f32[256]{0:T(256)S(1)}, u32[]{:S(2)}) copy-start(f32[256]{0:T(256)S(1)} %add_rsqrt_fusion) | copy-start | bytes 3076
  208.8 9.7 %copy-start.43 = (bf16[256,1024]{1,0:T(8,128)(2,1)}, bf16[256,1024]{1,0:T(8,128)(2,1)S(1)}, u32[]{:S(2)}) copy-start(bf16[256,1024]{1,0:T(8,128)(2,1)S(1)} %add_convert_fusion.2) | copy-start | bytes 1572868
  208.8 5.2 copy-start.74
  208.8 5.8 %collective-permute-start.2 = (bf16[256,1024]{1,0:T(8,128)(2,1)S(1)}, bf16[256,1024]{1,0:T(8,128)(2,1)}, u32[]{:S(2)}, u32[]{:S(2)}) collective-permute-start(bf16[256,1024]{1,0:T(8,128)(2,1)S(1)} %add_convert_fusion.2), channel_id=1, source_target_pairs={{0,1},{1,0},{2,3},{3,2},{4,5},{5,4},{6,7},{7,6},{8,9},{9,8},{10,11... | collective-permute-start | bytes 1572872 | tf_op jit(solution)/shard_map/ppermute | solution.py:771
  245.9 7.0 %copy-start.9 = (f32[2,256,8,8]{3,2,1,0:T(8,128)S(1)}, f32[2,256,8,8]{3,2,1,0:T(8,128)}, u32[]{:S(2)}) copy-start(f32[2,256,8,8]{3,2,1,0:T(8,128)} %get-tuple-element.75) | copy-start | bytes 393220
  295.2 12.8 %collective-permute-start.5 = (f32[256,1024]{1,0:T(8,128)S(1)}, f32[256,1024]{1,0:T(8,128)S(1)}, u32[]{:S(2)}, u32[]{:S(2)}) collective-permute-start(f32[256,1024]{1,0:T(8,128)S(1)} %slice.324), channel_id=1, source_target_pairs={{0,1},{1,0},{2,3},{3,2},{4,5},{5,4},{6,7},{7,6},{8,9},{9,8},{10,11... | collective-permute-start | bytes 3145736 | tf_op jit(solution)/shard_map/ppermute | solution.py:771
  295.4 13.2 %collective-permute-start.3 = (f32[256,1024]{1,0:T(8,128)S(1)}, f32[256,1024]{1,0:T(8,128)S(1)}, u32[]{:S(2)}, u32[]{:S(2)}) collective-permute-start(f32[256,1024]{1,0:T(8,128)S(1)} %slice.313), channel_id=1, source_target_pairs={{0,1},{1,0},{2,3},{3,2},{4,5},{5,4},{6,7},{7,6},{8,9},{9,8},{10,11... | collective-permute-start | bytes 3145736 | tf_op jit(solution)/shard_map/ppermute | solution.py:771
  300.7 7.3 %copy-start.79 = (f32[1024]{0:T(1024)S(1)}, f32[1024]{0:T(1024)}, u32[]{:S(2)}) copy-start(f32[1024]{0:T(1024)} %copy-done.78) | copy-start | bytes 12292
  300.7 7.3 %copy-start.85 = (f32[256]{0:T(256)S(1)}, f32[256]{0:T(256)}, u32[]{:S(2)}) copy-start(f32[256]{0:T(256)} %copy-done.84) | copy-start | bytes 3076
  300.7 7.3 %copy-start.90 = (f32[256]{0:T(256)S(1)}, f32[256]{0:T(256)}, u32[]{:S(2)}) copy-start(f32[256]{0:T(256)} %copy-done.89) | copy-start | bytes 3076
  310.2 10.9 %copy-start.36 = (bf16[256,1024]{1,0:T(8,128)(2,1)}, bf16[256,1024]{1,0:T(8,128)(2,1)S(1)}, u32[]{:S(2)}) copy-start(bf16[256,1024]{1,0:T(8,128)(2,1)S(1)} %convert_element_type.171) | copy-start | bytes 1572868
  310.2 10.9 %collective-permute-start.6 = (bf16[256,1024]{1,0:T(8,128)(2,1)S(1)}, bf16[256,1024]{1,0:T(8,128)(2,1)}, u32[]{:S(2)}, u32[]{:S(2)}) collective-permute-start(bf16[256,1024]{1,0:T(8,128)(2,1)S(1)} %convert_element_type.171), channel_id=1, source_target_pairs={{0,1},{1,0},{2,3},{3,2},{4,5},{5,4},{6,7},{7,6},{8,9},{9,8},{10,11... | collective-permute-start | bytes 1572872 | tf_op jit(solution)/shard_map/ppermute | solution.py:771
  312.1 9.0 %copy-start.33 = (bf16[1,4,4,32,1024]{4,3,2,1,0:T(8,128)(2,1)S(1)}, bf16[1,4,4,32,1024]{4,3,2,1,0:T(8,128)(2,1)}, u32[]{:S(2)}) copy-start(bf16[1,4,4,32,1024]{4,3,2,1,0:T(8,128)(2,1)} %get-tuple-element.27) | copy-start | bytes 3145732
  318.4 7.6 %copy-start.55 = (f32[2,8,256]{2,1,0:T(8,128)S(1)}, f32[2,8,256]{2,1,0:T(8,128)}, u32[]{:S(2)}) copy-start(f32[2,8,256]{2,1,0:T(8,128)} %log_add_fusion) | copy-start | bytes 49156
  323.7 6.2 %copy-start.15 = (bf16[2,256,8,64]{1,3,2,0:T(8,128)(2,1)S(1)}, bf16[2,256,8,64]{1,3,2,0:T(8,128)(2,1)}, u32[]{:S(2)}) copy-start(bf16[2,256,8,64]{1,3,2,0:T(8,128)(2,1)} %copy.108) | copy-start | bytes 1572868
  336.6 6.1 %copy-start.97 = (bf16[2,4,4,32,2048]{4,3,2,1,0:T(8,128)(2,1)S(1)}, bf16[2,4,4,32,2048]{4,3,2,1,0:T(8,128)(2,1)}, u32[]{:S(2)}) copy-start(bf16[2,4,4,32,2048]{4,3,2,1,0:T(8,128)(2,1)} %get-tuple-element.28) | copy-start | bytes 12582916
  355.5 5.4 %copy-start.22 = (bf16[64,8,2,256]{3,1,2,0:T(8,128)(2,1)S(1)}, bf16[64,8,2,256]{3,1,2,0:T(8,128)(2,1)}, u32[]{:S(2)}) copy-start(bf16[64,8,2,256]{3,1,2,0:T(8,128)(2,1)} %copy-done.21) | copy-start | bytes 1572868
  355.5 5.4 %copy-start.38 = (bf16[256,1024]{1,0:T(8,128)(2,1)S(1)}, bf16[256,1024]{1,0:T(8,128)(2,1)}, u32[]{:S(2)}) copy-start(bf16[256,1024]{1,0:T(8,128)(2,1)} %copy-done.36) | copy-start | bytes 1572868
  358.7 4.9 copy-start.41
  358.7 4.9 copy-start.106
  360.2 18.1 %collective-permute-start.7 = (f32[256,1024]{1,0:T(8,128)S(1)}, f32[256,1024]{1,0:T(8,128)}, u32[]{:S(2)}, u32[]{:S(2)}) collective-permute-start(f32[256,1024]{1,0:T(8,128)S(1)} %slice.334), channel_id=1, source_target_pairs={{0,1},{1,0},{2,3},{3,2},{4,5},{5,4},{6,7},{7,6},{8,9},{9,8},{10,11... | collective-permute-start | bytes 3145736 | tf_op jit(solution)/shard_map/ppermute | solution.py:771
  367.5 6.2 %copy-start.42 = (bf16[256,1024]{1,0:T(8,128)(2,1)S(1)}, bf16[256,1024]{1,0:T(8,128)(2,1)}, u32[]{:S(2)}) copy-start(bf16[256,1024]{1,0:T(8,128)(2,1)} %copy-done.39) | copy-start | bytes 1572868
  367.5 6.2 %copy-start.107 = (bf16[256,1024]{1,0:T(8,128)(2,1)S(1)}, bf16[256,1024]{1,0:T(8,128)(2,1)}, u32[]{:S(2)}) copy-start(bf16[256,1024]{1,0:T(8,128)(2,1)} %copy-done.104) | copy-start | bytes 1572868
  367.5 6.2 %copy-start.110 = (bf16[512,2048]{1,0:T(8,128)(2,1)S(1)}, bf16[512,2048]{1,0:T(8,128)(2,1)}, u32[]{:S(2)}) copy-start(bf16[512,2048]{1,0:T(8,128)(2,1)} %copy-done.109) | copy-start | bytes 6291460
  373.8 6.4 %copy-start.67 = (f32[64,16]{1,0:T(8,128)S(1)}, f32[64,16]{1,0:T(8,128)}, u32[]{:S(2)}) copy-start(f32[64,16]{1,0:T(8,128)} %reshape.363) | copy-start | bytes 12292
  373.8 6.4 %copy-start.68 = (f32[64,16]{1,0:T(8,128)S(1)}, f32[64,16]{1,0:T(8,128)}, u32[]{:S(2)}) copy-start(f32[64,16]{1,0:T(8,128)} %reshape.364) | copy-start | bytes 12292
  373.8 6.4 %copy-start.69 = (f32[64,16]{1,0:T(8,128)S(1)}, f32[64,16]{1,0:T(8,128)}, u32[]{:S(2)}) copy-start(f32[64,16]{1,0:T(8,128)} %reshape.362) | copy-start | bytes 12292
  373.8 6.4 %copy-start.70 = (f32[64,16]{1,0:T(8,128)S(1)}, f32[64,16]{1,0:T(8,128)}, u32[]{:S(2)}) copy-start(f32[64,16]{1,0:T(8,128)} %reshape.365) | copy-start | bytes 12292
  522.9 5.8 %copy-start.64 = (f32[2,16,1024]{2,1,0:T(8,128)S(1)}, f32[2,16,1024]{2,1,0:T(8,128)}, u32[]{:S(2)}) copy-start(f32[2,16,1024]{2,1,0:T(8,128)} %get-tuple-element.136) | copy-start | bytes 393220
  522.9 7.3 %copy-start.45 = (f32[2,64,1024]{2,1,0:T(8,128)S(1)}, f32[2,64,1024]{2,1,0:T(8,128)}, u32[]{:S(2)}) copy-start(f32[2,64,1024]{2,1,0:T(8,128)} %get-tuple-element.139) | copy-start | bytes 1572868
  523.7 5.6 %copy-start.46 = (f32[2,16,4096]{2,1,0:T(8,128)S(1)}, f32[2,16,4096]{2,1,0:T(8,128)}, u32[]{:S(2)}) copy-start(f32[2,16,4096]{2,1,0:T(8,128)} %get-tuple-element.137) | copy-start | bytes 1572868
  (74 other events, 237.0 us)

commit v2 on v1

--- a/solution.py
+++ b/solution.py
@@ -1,10 +1,14 @@
 import functools
+import math
+
 import jax
 import jax.numpy as jnp
+import numpy as np
 from jax import lax
 from jax.experimental import pallas as pl
 from jax.experimental.pallas import tpu as pltpu
 from jax.sharding import PartitionSpec as P
+
 
 MESH = pl.DeviceIdType.MESH
 LANE = 128
@@ -33,7 +37,7 @@
 
 
 GATHERED = (
-    ("small", True, 32, 128, 0, 1),
+    ("small", True, 16, 128, 0, 1),
     ("qkv", True, 32, 1536, 4, 8),
     ("up", True, 32, 2048, 5, 11),
     ("out", False, 32, 1024, 3, 5),
@@ -283,7 +287,10 @@
             if name == "small" and layer_at:
                 continue
             shapes.append(
-                jax.ShapeDtypeStruct((2 if by_columns else 1, 4, 4, rows, columns), jnp.bfloat16)
+                jax.ShapeDtypeStruct(
+                    (2 if by_columns else 1, 4, 4, rows, columns),
+                    jnp.float32 if name == "small" else jnp.bfloat16,
+                )
             )
     return pl.pallas_call(
         gather_kernel,
@@ -727,231 +734,584 @@
     )(*sources)
 
 
-HEADS = 16
+COUNT = 256
+BOTH = 512
+D = 1024
 HEAD_DIM = 64
 ROT = 16
 EPS = 1e-05
 FILL = -1e30
-
-
-def tables(count):
-    places = jnp.arange(count, dtype=jnp.float32)
-    rates = 10000.0 ** (-jnp.arange(0, ROT, 2, dtype=jnp.float32) / ROT)
+F32 = jnp.float32
+BF16 = jnp.bfloat16
+TILE = 256
+
+
+def turn_tables():
+    places = np.arange(COUNT, dtype=np.float32)
+    rates = np.float32(10000.0) ** (-np.arange(0, ROT, 2, dtype=np.float32) / np.float32(ROT))
     angles = places[:, None] * rates[None, :]
-    cosine = jnp.concatenate([jnp.cos(angles), jnp.cos(angles)], -1)
-    sine = jnp.concatenate([jnp.sin(angles), jnp.sin(angles)], -1)
-    return (cosine, sine)
-
-
-def rotate(values, cosine, sine):
+    cosine, sine = np.cos(angles), np.sin(angles)
     half = ROT // 2
-    turned = values[..., :ROT]
-    swapped = jnp.concatenate([-turned[..., half:], turned[..., :half]], -1)
-    moved = turned * cosine[:, None, :] + swapped * sine[:, None, :]
-    return jnp.concatenate([moved, values[..., ROT:]], -1)
-
-
-def gelu_exact(values):
-    return jax.nn.gelu(values, approximate=False)
-
-
-def contract_rows(left, right):
-    return lax.dot_general(
-        left, right, (((0,), (0,)), ((), ())), preferred_element_type=jnp.float32
+    keep = np.ones((COUNT, HEAD_DIM), np.float32)
+    ahead = np.zeros((COUNT, HEAD_DIM), np.float32)
+    behind = np.zeros((COUNT, HEAD_DIM), np.float32)
+    keep[:, :half] = cosine
+    keep[:, half:ROT] = cosine
+    ahead[:, :half] = -sine
+    behind[:, half:ROT] = sine
+    return np.stack([np.concatenate([t, t], 1) for t in (keep, ahead, behind)])
+
+
+def turn(values, tables, sign):
+    return values * tables[0] + sign * (
+        pltpu.roll(values, LANE - ROT // 2, 1) * tables[1]
+        + pltpu.roll(values, ROT // 2, 1) * tables[2]
     )
 
 
-def contract_cols(left, right):
-    return lax.dot_general(
-        left, right, (((1,), (1,)), ((), ())), preferred_element_type=jnp.float32
+def dot(left, right):
+    return jnp.dot(left, right, preferred_element_type=F32)
+
+
+def dot_nt(left, right):
+    return lax.dot_general(left, right, (((1,), (1,)), ((), ())), preferred_element_type=F32)
+
+
+def dot_tn(left, right):
+    return lax.dot_general(left, right, (((0,), (0,)), ((), ())), preferred_element_type=F32)
+
+
+def columns_of(index, width=TILE):
+    return pl.ds(pl.multiple_of(index * width, width), width)
+
+
+def loop(count, body):
+    def step(index, carry):
+        body(index)
+        return carry
+
+    lax.fori_loop(0, count, step, 0)
+
+
+KINDS = {
+    "b_qkv": (0, 0, 48, 43691, 21),
+    "b_up": (1, 0, 64, 1, 6),
+    "gain": (2, 0, 16, 1, 4),
+    "shift": (2, 16, 16, 1, 4),
+    "out_bias": (2, 32, 16, 1, 4),
+}
+CHUNK = 512
+
+
+def chunks_of(kind, core):
+    if kind == "b_qkv":
+        return [(t * CHUNK, t * 1024 + core * CHUNK) for t in range(3)]
+    if kind == "b_up":
+        return [(t * CHUNK, core * 2048 + t * CHUNK) for t in range(4)]
+    return [(t * CHUNK, t * CHUNK) for t in range(2)]
+
+
+def owner_masks(kind, start):
+    row, lane, size, factor, shift = KINDS[kind]
+    place_of = lax.broadcasted_iota(jnp.int32, (LANE, CHUNK), 1) + start
+    owner = lax.shift_right_logical(place_of * factor, shift)
+    within = place_of - owner * size + lane
+    spread = lax.broadcasted_iota(jnp.int32, (LANE, CHUNK), 0) == within
+    owned = lax.broadcasted_iota(jnp.int32, (64, CHUNK), 0) == owner[:64]
+    return spread, owned
+
+
+def unpack_vector(rows_ref, layer_at, kind, core, target):
+    row = KINDS[kind][0] + 3 * layer_at
+    held = rows_ref[pl.ds(row, 64, stride=8), :].astype(BF16)
+    for place_at, start in chunks_of(kind, core):
+        spread, owned = owner_masks(kind, start)
+        every = dot(held, jnp.where(spread, 1.0, 0.0).astype(BF16))
+        target[:, pl.ds(place_at, CHUNK)] = jnp.sum(
+            jnp.where(owned, every, 0.0), 0, keepdims=True
+        )
+
+
+def pack_vectors(rows_ref, layer_at, core, vectors):
+    found = {}
+    for kind, vector in vectors.items():
+        total = jnp.zeros((64, LANE), F32)
+        for place_at, start in chunks_of(kind, core):
+            spread, owned = owner_masks(kind, start)
+            mine = jnp.where(owned, vector[:, pl.ds(place_at, CHUNK)], 0.0)
+            total = total + lax.dot_general(
+                mine,
+                jnp.where(spread, 1.0, 0.0),
+                (((1,), (1,)), ((), ())),
+                precision=lax.Precision.HIGHEST,
+                preferred_element_type=F32,
+            )
+        row = KINDS[kind][0]
+        found[row] = found[row] + total if row in found else total
+    for row, total in found.items():
+        rows_ref[pl.ds(row + 3 * layer_at, 64, stride=8), :] = total
+
+
+def centre(values):
+    centred = values - jnp.mean(values, -1, keepdims=True)
+    inv_std = lax.rsqrt(jnp.mean(centred * centred, -1, keepdims=True) + EPS)
+    return centred * inv_std, inv_std
+
+
+def norm_piece(x_ref, gain, shift, hidden):
+    def body(index):
+        rows = columns_of(index, 64)
+        normed, unused = centre(x_ref[rows, :])
+        hidden[rows, :] = (normed * gain[...] + shift[...]).astype(BF16)
+
+    loop(COUNT // 64, body)
+
+
+def joined_piece(third, hidden, w_qkv, b_qkv, tables, target):
+    def body(index):
+        columns = columns_of(index + third * 2)
+        found = dot(hidden[...], w_qkv(columns)) + b_qkv[:, columns]
+        for sequence in range(2):
+            for pair in range(2):
+                part = found[sequence * COUNT : (sequence + 1) * COUNT, pair * LANE : (pair + 1) * LANE]
+                if third < 2:
+                    part = turn(part, tables, 1.0)
+                if third == 0:
+                    part = part * HEAD_DIM**-0.5
+                target[pl.ds(sequence * COUNT, COUNT), columns_of(index * 2 + pair, LANE)] = (
+                    part.astype(BF16)
+                )
+
+    loop(2, body)
+
+
+def first_head():
+    return lax.broadcasted_iota(jnp.int32, (COUNT, LANE), 1) < HEAD_DIM
+
+
+def only_head(values, half):
+    keep = first_head() if half == 0 else jnp.logical_not(first_head())
+    return jnp.where(keep, values, jnp.zeros_like(values))
+
+
+def attention_piece(query, key, value, probs, mixed):
+    def body(index):
+        sequence, pair = index // 4, index % 4
+        rows, columns = columns_of(sequence, COUNT), columns_of(pair, LANE)
+        q2, k2, v2 = query[rows, columns], key[rows, columns], value[rows, columns]
+        causal = lax.broadcasted_iota(jnp.int32, (COUNT, COUNT), 0) >= lax.broadcasted_iota(
+            jnp.int32, (COUNT, COUNT), 1
+        )
+        out = []
+        for half in range(2):
+            scores = jnp.where(causal, dot_nt(only_head(q2, half), k2), FILL)
+            expo = jnp.exp(scores - jnp.max(scores, -1, keepdims=True))
+            prob = (expo * (1.0 / jnp.sum(expo, -1, keepdims=True))).astype(BF16)
+            probs[index * 2 + half] = prob
+            out.append(dot(prob, v2))
+        mixed[rows, columns] = jnp.where(first_head(), out[0], out[1]).astype(BF16)
+
+    loop(8, body)
+
+
+def up_piece(hidden, w_up, b_up, active, slope):
+    def body(index):
+        columns = columns_of(index)
+        upward = dot(hidden[...], w_up(columns)) + b_up[:, columns]
+        spread = 0.5 + 0.5 * lax.erf(upward * (0.5**0.5))
+        active[:, columns] = (upward * spread).astype(BF16)
+        dense = jnp.exp(upward * upward * -0.5) * (1.0 / math.sqrt(2.0 * math.pi))
+        slope[:, columns] = (spread + upward * dense).astype(BF16)
+
+    loop(8, body)
+
+
+def down_piece(active, w_down, mixed, w_out, partial):
+    def body(index):
+        columns = columns_of(index)
+        partial[:, columns] = dot(mixed[...], w_out(columns)) + dot(active[...], w_down(columns))
+
+    loop(4, body)
+
+
+def residual_piece(x_ref, partial, received, out_bias, target):
+    def body(index):
+        rows = columns_of(index, 64)
+        target[rows, :] = (
+            x_ref[rows, :] + (partial[rows, :] + received[rows, :]) + out_bias[...]
+        ).astype(target.dtype)
+
+    loop(COUNT // 64, body)
+
+
+def start_piece(dy, dy_low, out_bias_grad):
+    def body(index):
+        rows = columns_of(index, 64)
+        values = dy[rows, :].astype(F32)
+        dy_low[rows, :] = values.astype(BF16)
+        out_bias_grad[...] += jnp.sum(values, 0, keepdims=True)
+
+    out_bias_grad[...] = jnp.zeros_like(out_bias_grad)
+    loop(COUNT // 64, body)
+
+
+def flip_piece(source, target):
+    rows, columns = source.shape
+    for at_row in range(rows // TILE):
+
+        def body(index, at_row=at_row):
+            target[columns_of(index), pl.ds(at_row * TILE, TILE)] = source[
+                pl.ds(at_row * TILE, TILE), columns_of(index)
+            ].T
+
+        loop(columns // TILE, body)
+
+
+def rows_grad_piece(count, left, right, store):
+    def body(index):
+        store(index, dot_tn(left[:, columns_of(index)], right[...]).astype(BF16))
+
+    loop(count, body)
+
+
+def columns_grad_piece(count, left_flipped, right, store):
+    def body(index):
+        store(index, dot(left_flipped[...], right[:, columns_of(index)]).astype(BF16))
+
+    loop(count, body)
+
+
+def slope_piece(dy_low, w_down_rows, slope, d_up, b_up_grad):
+    def body(index):
+        columns = columns_of(index)
+        found = (dot_nt(dy_low[...], w_down_rows(index)) * slope[:, columns].astype(F32)).astype(BF16)
+        d_up[:, columns] = found
+        b_up_grad[:, columns] = jnp.sum(found.astype(F32), 0, keepdims=True)
+
+    loop(8, body)
+
+
+def d_mixed_piece(dy_low, w_out_rows, d_mixed):
+    def body(index):
+        d_mixed[:, columns_of(index)] = dot_nt(dy_low[...], w_out_rows(index)).astype(BF16)
+
+    loop(2, body)
+
+
+def attention_back_piece(query, key, value, probs, d_mixed, tables, d_joined, b_qkv_grad):
+    b_qkv_grad[...] = jnp.zeros_like(b_qkv_grad)
+
+    def body(index):
+        sequence, pair = index // 4, index % 4
+        rows, columns = columns_of(sequence, COUNT), columns_of(pair, LANE)
+        q2, k2, v2 = query[rows, columns], key[rows, columns], value[rows, columns]
+        dm2 = d_mixed[rows, columns]
+        found = []
+        for half in range(2):
+            prob = probs[index * 2 + half]
+            full = prob.astype(F32)
+            d_probs = dot_nt(only_head(dm2, half), v2)
+            d_scores = (
+                full * (d_probs - jnp.sum(d_probs * full, -1, keepdims=True))
+            ).astype(BF16)
+            found.append((dot(d_scores, k2), dot_tn(d_scores, q2), dot_tn(prob, dm2)))
+        for third in range(3):
+            part = jnp.where(first_head(), found[0][third], found[1][third])
+            if third == 0:
+                part = part * HEAD_DIM**-0.5
+            if third < 2:
+                part = turn(part, tables, -1.0)
+            part = part.astype(BF16)
+            there = columns_of(pair + third * 4, LANE)
+            d_joined[rows, there] = part
+            b_qkv_grad[:, there] += jnp.sum(part.astype(F32), 0, keepdims=True)
+
+    loop(8, body)
+
+
+def d_hidden_piece(d_joined, w_qkv_rows, d_up, w_up_rows, d_hidden):
+    def body(index):
+        d_hidden[:, columns_of(index)] = dot_nt(d_joined[...], w_qkv_rows(index)) + dot_nt(
+            d_up[...], w_up_rows(index)
+        )
+
+    loop(4, body)
+
+
+def norm_back_piece(x_ref, gain, dy, d_hidden, received, target, gain_grad, shift_grad):
+    gain_grad[...] = jnp.zeros_like(gain_grad)
+    shift_grad[...] = jnp.zeros_like(shift_grad)
+
+    def body(index):
+        rows = columns_of(index, 64)
+        normed, inv_std = centre(x_ref[rows, :].astype(F32))
+        total = d_hidden[rows, :] + received[rows, :]
+        gain_grad[...] += jnp.sum(total * normed, 0, keepdims=True)
+        shift_grad[...] += jnp.sum(total, 0, keepdims=True)
+        scaled = total * gain[...]
+        target[rows, :] = dy[rows, :].astype(F32) + inv_std * (
+            scaled
+            - jnp.mean(scaled, -1, keepdims=True)
+            - normed * jnp.mean(scaled * normed, -1, keepdims=True)
+        )
+
+    loop(COUNT // 64, body)
+
+
+class Pair:
+    def __init__(self, send, recv):
+        xl, xh, z, y, c = place()
+        self.device = at(xl, xh, z, y, 1 - c)
+        self.send, self.recv = send, recv
+
+    def push(self, source, target, slot):
+        pltpu.make_async_remote_copy(
+            source,
+            target,
+            self.send.at[slot],
+            self.recv.at[slot],
+            device_id=self.device,
+            device_id_type=MESH,
+        ).start()
+
+    def wait(self, source, target, slot):
+        pltpu.make_async_copy(source, source, self.send.at[slot]).wait()
+        pltpu.make_async_copy(target, target, self.recv.at[slot]).wait()
+
+
+def forward_kernel(layer_at, x_in, rows_ref, w_qkv, w_up, w_out, w_down, tables, *rest):
+    (
+        x_out, hidden, query, key, value, probs, mixed, active, slope, gain,
+        x_ref, b_qkv, b_up, shift, out_bias, partial, received, send, recv,
+    ) = rest
+    xl, xh, z, y, c = place()
+    meet([at(xl, xh, z, y, 1 - c)])
+    pair = Pair(send, recv)
+    for core in range(2):
+
+        @pl.when(c == core)
+        def _():
+            for kind, target in (
+                ("b_qkv", b_qkv), ("b_up", b_up), ("gain", gain), ("shift", shift), ("out_bias", out_bias),
+            ):
+                unpack_vector(rows_ref, layer_at, kind, core, target)
+
+    x_ref[...] = x_in[...].astype(F32)
+    own, other = pl.ds(0, COUNT), pl.ds(COUNT, COUNT)
+    norm_piece(x_ref, gain, shift, hidden)
+    pair.push(hidden.at[own], hidden.at[other], 0)
+    pair.wait(hidden.at[own], hidden.at[other], 0)
+    for third, target in enumerate((query, key, value)):
+        joined_piece(third, hidden, lambda n: w_qkv[:, n], b_qkv, tables, target)
+    attention_piece(query, key, value, probs, mixed)
+    up_piece(hidden, lambda n: w_up[:, n], b_up, active, slope)
+    down_piece(active, lambda n: w_down[:, n], mixed, lambda n: w_out[:, n], partial)
+    pair.push(partial.at[other], received, 1)
+    pair.wait(partial.at[other], received, 1)
+    residual_piece(x_ref, partial, received, out_bias, x_out)
+
+
+def forward_call(layer_at, x, rows, w_qkv, w_up, w_out, w_down, tables):
+    last = layer_at == LAYERS - 1
+    vmem = pl.BlockSpec(memory_space=pltpu.VMEM)
+    shape = jax.ShapeDtypeStruct
+    return pl.pallas_call(
+        functools.partial(forward_kernel, layer_at),
+        out_shape=[
+            shape((COUNT, D), BF16 if last else F32),
+            shape((BOTH, D), BF16),
+            shape((BOTH, 512), BF16),
+            shape((BOTH, 512), BF16),
+            shape((BOTH, 512), BF16),
+            shape((16, COUNT, COUNT), BF16),
+            shape((BOTH, 512), BF16),
+            shape((BOTH, 2048), BF16),
+            shape((BOTH, 2048), BF16),
+            shape((1, D), F32),
+        ],
+        in_specs=[vmem] * 7,
+        out_specs=[vmem] * 10,
+        scratch_shapes=[
+            pltpu.VMEM((COUNT, D), F32),
+            pltpu.VMEM((1, 1536), F32),
+            pltpu.VMEM((1, 2048), F32),
+            pltpu.VMEM((1, D), F32),
+            pltpu.VMEM((1, D), F32),
+            pltpu.VMEM((BOTH, D), F32),
+            pltpu.VMEM((COUNT, D), F32),
+            pltpu.SemaphoreType.DMA((2,)),
+            pltpu.SemaphoreType.DMA((2,)),
+        ],
+        name=f"forward{layer_at}",
+        compiler_params=pltpu.CompilerParams(
+            collective_id=2 + layer_at, has_side_effects=True, vmem_limit_bytes=60 * 2**20
+        ),
+    )(x, rows, w_qkv, w_up, w_out, w_down, tables)
+
+
+def backward_kernel(
+    layer_at, x_in, dy, hidden, query, key, value, probs, mixed, active, slope, gain,
+    w_qkv, w_up, w_out, w_down, tables, *rest
+):
+    (
+        dx, g_qkv, g_up, g_out, g_down, g_small,
+        hidden_flipped, dy_low, d_up, d_mixed, d_joined, d_hidden, received,
+        b_qkv_grad, b_up_grad, gain_grad, shift_grad, out_bias_grad, send, recv,
+    ) = rest
+    xl, xh, z, y, c = place()
+    meet([at(xl, xh, z, y, 1 - c)])
+    pair = Pair(send, recv)
+    own, other = pl.ds(0, COUNT), pl.ds(COUNT, COUNT)
+    start_piece(dy, dy_low, out_bias_grad)
+    pair.push(dy_low.at[own], dy_low.at[other], 0)
+    flip_piece(hidden, hidden_flipped)
+    pair.wait(dy_low.at[own], dy_low.at[other], 0)
+
+    def by_rows(target):
+        def store(index, found):
+            target[columns_of(index), :] = found
+
+        return store
+
+    def by_columns(target):
+        def store(index, found):
+            target[:, columns_of(index)] = found
+
+        return store
+
+    rows_grad_piece(8, active, dy_low, by_rows(g_down))
+    slope_piece(dy_low, lambda n: w_down[columns_of(n), :], slope, d_up, b_up_grad)
+    columns_grad_piece(8, hidden_flipped, d_up, by_columns(g_up))
+    d_mixed_piece(dy_low, lambda n: w_out[columns_of(n), :], d_mixed)
+    rows_grad_piece(2, mixed, dy_low, by_rows(g_out))
+    attention_back_piece(query, key, value, probs, d_mixed, tables, d_joined, b_qkv_grad)
+    d_hidden_piece(
+        d_joined, lambda n: w_qkv[columns_of(n), :], d_up, lambda n: w_up[columns_of(n), :], d_hidden
     )
-
-
-def exchange(values):
-    return lax.ppermute(values, "shard", [(s, s ^ 1) for s in range(64)])
-
-
-def forward_layer(inputs, gathered, cosine, sine, causal):
-    w_qkv, b_qkv, w_out, w_up, b_up, w_down, gain, shift, out_bias = gathered
-    count = inputs.shape[0]
-    centred = inputs - jnp.mean(inputs, -1, keepdims=True)
-    inv_std = lax.rsqrt(jnp.mean(centred * centred, -1, keepdims=True) + EPS)
-    normed = centred * inv_std
-    hidden = (normed * gain + shift).astype(jnp.bfloat16)
-    hidden = jnp.concatenate([hidden, exchange(hidden)], 0)
-    joined = jnp.dot(hidden, w_qkv, preferred_element_type=jnp.float32) + b_qkv
-    split_shape = (2, count, 8, HEAD_DIM)
-    query = rotate(joined[:, :512].reshape(split_shape), cosine, sine).astype(jnp.bfloat16)
-    key_rot = rotate(joined[:, 512:1024].reshape(split_shape), cosine, sine).astype(jnp.bfloat16)
-    values = joined[:, 1024:].reshape(split_shape).astype(jnp.bfloat16)
-    scores = jnp.einsum(
-        "gshd,gthd->ghst", query, key_rot, preferred_element_type=jnp.float32
-    ) * HEAD_DIM ** (-0.5)
-    scores = jnp.where(causal, scores, FILL)
-    highest = jnp.max(scores, -1, keepdims=True)
-    expo = jnp.exp(scores - highest)
-    total = jnp.sum(expo, -1, keepdims=True)
-    probs = (expo / total).astype(jnp.bfloat16)
-    log_total = highest + jnp.log(total)
-    mixed = jnp.einsum("ghst,gthd->gshd", probs, values, preferred_element_type=jnp.float32)
-    mixed = mixed.reshape(2 * count, 512).astype(jnp.bfloat16)
-    attended = jnp.dot(mixed, w_out, preferred_element_type=jnp.float32)
-    upward = jnp.dot(hidden, w_up, preferred_element_type=jnp.float32) + b_up
-    active = gelu_exact(upward).astype(jnp.bfloat16)
-    lowered = jnp.dot(active, w_down, preferred_element_type=jnp.float32)
-    partial = attended + lowered
-    outputs = inputs + (partial[:count] + exchange(partial[count:])) + out_bias
-    kept = (normed, inv_std, hidden, query, key_rot, values, log_total, mixed, upward, active)
-    return (outputs, kept)
-
-
-def backward_layer(upstream, kept, gathered, cosine, sine, causal):
-    w_qkv, b_qkv, w_out, w_up, b_up, w_down, gain, shift, out_bias = gathered
-    normed, inv_std, hidden, query, key_rot, values, log_total, mixed, upward, active = kept
-    count = upstream.shape[0]
-    split_shape = (2, count, 8, HEAD_DIM)
-    out_bias_grad = jnp.sum(upstream, 0)
-    up_low = upstream.astype(jnp.bfloat16)
-    up_low = jnp.concatenate([up_low, exchange(up_low)], 0)
-    w_down_grad = contract_rows(active, up_low).astype(jnp.bfloat16)
-    d_active = contract_cols(up_low, w_down)
-    unused, gelu_pull = jax.vjp(gelu_exact, upward)
-    d_upward = gelu_pull(d_active)[0].astype(jnp.bfloat16)
-    w_up_grad = contract_rows(hidden, d_upward).astype(jnp.bfloat16)
-    b_up_grad = jnp.sum(d_upward.astype(jnp.float32), 0)
-    w_out_grad = contract_rows(mixed, up_low).astype(jnp.bfloat16)
-    d_mixed = contract_cols(up_low, w_out).astype(jnp.bfloat16).reshape(split_shape)
-    scores = jnp.einsum(
-        "gshd,gthd->ghst", query, key_rot, preferred_element_type=jnp.float32
-    ) * HEAD_DIM ** (-0.5)
-    scores = jnp.where(causal, scores, FILL)
-    probs_full = jnp.exp(scores - log_total)
-    d_probs = jnp.einsum("gshd,gthd->ghst", d_mixed, values, preferred_element_type=jnp.float32)
-    row_terms = jnp.sum(d_probs * probs_full, -1, keepdims=True)
-    d_scores = (probs_full * (d_probs - row_terms)).astype(jnp.bfloat16)
-    d_query = jnp.einsum(
-        "ghst,gthd->gshd", d_scores, key_rot, preferred_element_type=jnp.float32
-    ) * HEAD_DIM ** (-0.5)
-    d_key = jnp.einsum(
-        "ghst,gshd->gthd", d_scores, query, preferred_element_type=jnp.float32
-    ) * HEAD_DIM ** (-0.5)
-    d_values = jnp.einsum(
-        "ghst,gshd->gthd", probs_full.astype(jnp.bfloat16), d_mixed,
-        preferred_element_type=jnp.float32,
-    )
-    wide = (2 * count, 512)
-    d_query = rotate(d_query, cosine, -sine).reshape(wide)
-    d_key = rotate(d_key, cosine, -sine).reshape(wide)
-    d_joined = jnp.concatenate([d_query, d_key, d_values.reshape(wide)], 1).astype(jnp.bfloat16)
-    w_qkv_grad = contract_rows(hidden, d_joined).astype(jnp.bfloat16)
-    b_qkv_grad = jnp.sum(d_joined.astype(jnp.float32), 0)
-    d_hidden = contract_cols(d_joined, w_qkv) + contract_cols(d_upward, w_up)
-    d_hidden = d_hidden[:count] + exchange(d_hidden[count:])
-    gain_grad = jnp.sum(d_hidden * normed, 0)
-    shift_grad = jnp.sum(d_hidden, 0)
-    scaled = d_hidden * gain
-    d_inputs = upstream + inv_std * (
-        scaled
-        - jnp.mean(scaled, -1, keepdims=True)
-        - normed * jnp.mean(scaled * normed, -1, keepdims=True)
-    )
-    large = (w_qkv_grad, w_up_grad, w_out_grad, w_down_grad)
-    small = (b_qkv_grad, b_up_grad, gain_grad, shift_grad, out_bias_grad)
-    return (d_inputs, large, small)
+    pair.push(d_hidden.at[other], received, 1)
+    columns_grad_piece(6, hidden_flipped, d_joined, by_columns(g_qkv))
+    pair.wait(d_hidden.at[other], received, 1)
+    norm_back_piece(x_in, gain, dy, d_hidden, received, dx, gain_grad, shift_grad)
+    for core in range(2):
+
+        @pl.when(c == core)
+        def _():
+            pack_vectors(
+                g_small,
+                0,
+                core,
+                {
+                    "b_qkv": b_qkv_grad,
+                    "b_up": b_up_grad,
+                    "gain": gain_grad,
+                    "shift": shift_grad,
+                    "out_bias": out_bias_grad,
+                },
+            )
+
+
+def backward_call(layer_at, x, dy, kept, weights, tables):
+    vmem = pl.BlockSpec(memory_space=pltpu.VMEM)
+    shape = jax.ShapeDtypeStruct
+    return pl.pallas_call(
+        functools.partial(backward_kernel, layer_at),
+        out_shape=[
+            shape((COUNT, D), F32),
+            shape((D, 1536), BF16),
+            shape((D, 2048), BF16),
+            shape((512, D), BF16),
+            shape((2048, D), BF16),
+            shape((512, LANE), F32),
+        ],
+        in_specs=[vmem] * (2 + len(kept) + 5),
+        out_specs=[vmem] * 6,
+        scratch_shapes=[
+            pltpu.VMEM((D, BOTH), BF16),
+            pltpu.VMEM((BOTH, D), BF16),
+            pltpu.VMEM((BOTH, 2048), BF16),
+            pltpu.VMEM((BOTH, 512), BF16),
+            pltpu.VMEM((BOTH, 1536), BF16),
+            pltpu.VMEM((BOTH, D), F32),
+            pltpu.VMEM((COUNT, D), F32),
+            pltpu.VMEM((1, 1536), F32),
+            pltpu.VMEM((1, 2048), F32),
+            pltpu.VMEM((1, D), F32),
+            pltpu.VMEM((1, D), F32),
+            pltpu.VMEM((1, D), F32),
+            pltpu.SemaphoreType.DMA((2,)),
+            pltpu.SemaphoreType.DMA((2,)),
+        ],
+        name=f"backward{layer_at}",
+        compiler_params=pltpu.CompilerParams(
+            collective_id=4 + layer_at, has_side_effects=True, vmem_limit_bytes=60 * 2**20
+        ),
+    )(x, dy, *kept, *weights, tables)
 
 
 def pack_small(b_qkv, b_up, ln_gain, ln_bias, out_bias):
-    own = jnp.concatenate([b_qkv, b_up, ln_gain, ln_bias, out_bias], 1).reshape(320)
-    return jnp.pad(own, (0, 2048 - 320)).reshape(16, 128)
-
-
-def unpack_small(full, core):
-    rows = full.reshape(64, 2048)[:, :320].reshape(64, 2, 160).astype(jnp.float32)
-    layers = []
+    rows = []
     for layer_at in range(LAYERS):
-        b_qkv = rows[:, layer_at, :48].reshape(3, 2, 512)
-        b_qkv = lax.dynamic_index_in_dim(b_qkv, core, 1, False).reshape(1536)
-        b_up = rows[:, layer_at, 48:112].reshape(2, 2048)
-        b_up = lax.dynamic_index_in_dim(b_up, core, 0, False)
-        rest = [rows[:, layer_at, 112 + 16 * i : 128 + 16 * i].reshape(1024) for i in range(3)]
-        layers.append((b_qkv, b_up, *rest))
-    return layers
-
-
-def pack_small_grads(layers, core):
-    flag = jnp.stack([core == 0, core == 1]).astype(jnp.float32)
-    found = []
-    for b_qkv, b_up, gain, shift, out_bias in layers:
-        found.append((b_qkv.reshape(3, 1, 512) * flag[None, :, None]).reshape(64, 48))
-        found.append((b_up.reshape(1, 2048) * flag[:, None]).reshape(64, 64))
-        found.extend([gain.reshape(64, 16), shift.reshape(64, 16), out_bias.reshape(64, 16)])
-    return jnp.pad(jnp.concatenate(found, 1), ((0, 0), (0, 704))).reshape(2, 4, 4, 16, 128)
+        rows.append(jnp.pad(b_qkv[layer_at], (0, LANE - 48)))
+        rows.append(jnp.pad(b_up[layer_at], (0, LANE - 64)))
+        rows.append(
+            jnp.pad(
+                jnp.concatenate([ln_gain[layer_at], ln_bias[layer_at], out_bias[layer_at]]),
+                (0, LANE - 48),
+            )
+        )
+    return jnp.pad(jnp.stack(rows).astype(F32), ((0, 2), (0, 0)))
 
 
 def on_device(
     tokens, w_qkv, b_qkv, w_out, w_up, b_up, w_down, ln_gain, ln_bias, out_bias, out_grad
 ):
-    core = lax.axis_index("shard") % 2
-    count = tokens.shape[0]
-    cosine, sine = tables(count)
-    causal = jnp.tril(jnp.ones((count, count), jnp.bool_))
+    tables = jnp.asarray(turn_tables())
     found = gather(
         pack_small(b_qkv, b_up, ln_gain, ln_bias, out_bias), halves(w_qkv), w_up, w_out, w_down
     )
-    small = unpack_small(found[0], core)
-    current = tokens.astype(jnp.float32)
-    gathered_all = []
+    rows = found[0].reshape(512, LANE)
+    current = tokens
+    inputs = []
+    weights_all = []
     kept_all = []
     for layer_at in range(LAYERS):
         wq, wu, wo, wd = found[1 + 4 * layer_at : 5 + 4 * layer_at]
-        bq, bu, gain, shift, ob = small[layer_at]
-        gathered = (
-            wq.reshape(1024, 1536),
-            bq,
-            wo.reshape(512, 1024),
-            wu.reshape(1024, 2048),
-            bu,
-            wd.reshape(2048, 1024),
-            gain,
-            shift,
-            ob,
+        weights = (
+            wq.reshape(D, 1536), wu.reshape(D, 2048), wo.reshape(512, D), wd.reshape(2048, D)
         )
-        current, kept = forward_layer(current, gathered, cosine, sine, causal)
-        gathered_all.append(gathered)
+        inputs.append(current)
+        current, *kept = forward_call(layer_at, current, rows, *weights, tables)
+        weights_all.append(weights)
         kept_all.append(kept)
-    outcome = current.astype(jnp.bfloat16)
-    upstream = out_grad.astype(jnp.float32)
-    large = [None] * LAYERS
-    small_grads = [None] * LAYERS
+    outcome = current
+    upstream = out_grad
+    blocks = [None] * LAYERS
+    small = [None] * LAYERS
     for layer_at in reversed(range(LAYERS)):
-        upstream, large[layer_at], small_grads[layer_at] = backward_layer(
-            upstream, kept_all[layer_at], gathered_all[layer_at], cosine, sine, causal
+        upstream, q, u, o, d, small[layer_at] = backward_call(
+            layer_at, inputs[layer_at], upstream, kept_all[layer_at], weights_all[layer_at], tables
         )
-    blocks = []
-    for layer_at in range(LAYERS):
-        q, u, o, d = large[layer_at]
-        blocks.append(
-            [
-                q.reshape(2, 4, 4, 32, 1536),
-                u.reshape(2, 4, 4, 32, 2048),
-                o.reshape(1, 4, 4, 32, 1024),
-                d.reshape(1, 4, 4, 128, 1024),
-            ]
-        )
-    g_qkv, g_up, g_out, g_down, g_small = scatter(blocks, pack_small_grads(small_grads, core))
-    g_small = g_small.reshape(1024)[:320].reshape(2, 160)
+        blocks[layer_at] = [
+            q.reshape(2, 4, 4, 32, 1536),
+            u.reshape(2, 4, 4, 32, 2048),
+            o.reshape(1, 4, 4, 32, 1024),
+            d.reshape(1, 4, 4, 128, 1024),
+        ]
+    small = jnp.concatenate([s.reshape(64, 8, LANE)[:, :3] for s in small] + [jnp.zeros((64, 2, LANE), F32)], 1)
+    g_qkv, g_up, g_out, g_down, g_small = scatter(blocks, small.reshape(2, 4, 4, 16, LANE))
+    g_small = g_small[:6].reshape(LAYERS, 3, LANE)
     return (
         outcome,
         upstream,
         g_qkv,
-        g_small[:, :48],
+        g_small[:, 0, :48],
         g_out,
         g_up,
-        g_small[:, 48:112],
+        g_small[:, 1, :64],
         g_down,
-        g_small[:, 112:128],
-        g_small[:, 128:144],
-        g_small[:, 144:160],
+        g_small[:, 2, :16],
+        g_small[:, 2, 16:32],
+        g_small[:, 2, 32:48],
     )
 
 

time: 539 us -> 459 us (0.85)
  Pallas kernels: 268 us -> 434 us
  matrix products: 112 us -> 0 us
  local copies, waits for them, and re-layouts: 120 us -> 14.3 us
  other arithmetic: 24.2 us -> 1.47 us
    pallas_call x0 -> x4, Pallas kernels: none -> 166 us  [the longest x2 97.3 us: backward_call(): pl.pallas_call(functools.partial(backward_kernel, layer_at), out_shape=[s...]
    dot_general x36 -> x0, matrix products: 112 us -> none  [the longest x8 34.8 us: contract_rows(): lax.dot_general(left, right, (((0,), (0,)), ((), ())), preferred_element_...]
    unnamed x261 -> x20, local copies, waits for them, and re-layouts: 46.9 us -> 4.78 us
    slice x27 -> x5, local copies, waits for them, and re-layouts: 31.5 us -> 2.76 us  [the longest x2 0.99 us: on_device(): s.reshape(64, 8, LANE)[:, :3]]
    reshape x19 -> x1, local copies, waits for them, and re-layouts: 17.5 us -> 0.8 us  [on_device(): g_small = g_small[:6].reshape(LAYERS, 3, LANE)]
    reduce_sum x11 -> x0, other arithmetic: 9.77 us -> none  [the longest x2 2.67 us: forward_layer(): centred = inputs - jnp.mean(inputs, -1, keepdims=True)]
    convert_element_type x7 -> x0, local copies, waits for them, and re-layouts: 9.3 us -> none  [the longest x4 8.07 us: forward_layer(): values = joined[:, 1024:].reshape(split_shape).astype(jnp.bfloat16)]
  transfers between devices with their start and end apart: 8 -> 0, of which waited for: 1 -> 0; matrix products, arithmetic and copies ran while one was open for 10% -> 0% of each run, Pallas kernels for 0% -> 0%
where the time goes in v2:
time: 459 us; the launch traced here: 451 us
  Pallas kernels  434 us (95%)
  local copies, waits for them, and re-layouts  14.3 us (3%)
    pallas_call x1, Pallas kernels, scatter(): pl.pallas_call(functools.partial(scatter_kernel, streams), out_shape=[jax...  142 us
    pallas_call x1, Pallas kernels, gather(): pl.pallas_call(gather_kernel, out_shape=shapes, in_specs=[pl.BlockSpec(me...  127 us
    pallas_call x2, Pallas kernels, backward_call(): pl.pallas_call(functools.partial(backward_kernel, layer_at), out_shape=[s...  97.3 us
    pallas_call x2, Pallas kernels, forward_call(): pl.pallas_call(functools.partial(forward_kernel, layer_at), out_shape=[sh...  68.3 us

profile of v2, /device:TPU:1, one launch (start us, length us, event | category | flops | bytes accessed | tf_op | source)
XLA Modules:
  0.0 451.0 jit_solution(6333060387642391163)
XLA Ops:
  0.6 0.7 slice_bitcast_fusion.4
  1.4 0.7 slice_bitcast_fusion.3
  2.1 0.7 slice_bitcast_fusion
  2.9 0.7 slice_bitcast_fusion.1
  3.6 0.7 slice_bitcast_fusion.2
  4.3 0.1 fusion
  4.5 0.6 pad_convert_fusion.small
  5.1 1.1 reshape.91
  6.1 0.1 copy.31
  6.2 0.9 reshape.92.qkv
  7.2 126.7 %gather.1 = (f32[2,4,4,16,128]{4,3,2,1,0:T(8,128)}, bf16[2,4,4,32,1536]{4,3,2,1,0:T(8,128)(2,1)}, bf16[2,4,4,32,2048]{4,3,2,1,0:T(8,128)(2,1)}, bf16[1,4,4,32,10...) custom-call(f32[8,128]{1,0:T(8,128)} %pad_convert_fusion.small, ...), custom_call_target="tpu_custom_call" | custom-call | tf_op jit(solution)/shard_map/gather/pallas_call | solution.py:295
  133.9 34.0 %forward0.1 = (f32[256,1024]{1,0:T(8,128)}, bf16[512,1024]{1,0:T(8,128)(2,1)}, bf16[512,512]{1,0:T(8,128)(2,1)}, bf16[512,512]{1,0:T(8,128)(2,1)}, bf16[512,512]...) custom-call(bf16[256,1024]{1,0:T(8,128)(2,1)} %x_in.3, ...), custom_call_target="tpu_custom_call" | custom-call | tf_op jit(solution)/shard_map/forward0/pallas_call | solution.py:1118
  167.9 34.3 %forward1.1 = (bf16[256,1024]{1,0:T(8,128)(2,1)}, bf16[512,1024]{1,0:T(8,128)(2,1)}, bf16[512,512]{1,0:T(8,128)(2,1)}, bf16[512,512]{1,0:T(8,128)(2,1)}, bf16[51...) custom-call(f32[256,1024]{1,0:T(8,128)} %get-tuple-element.62.x_in, ...), custom_call_target="tpu_custom_call" | custom-call | tf_op jit(solution)/shard_map/forward1/pallas_call | solution.py:1118
  202.2 48.5 %backward1.1 = (f32[256,1024]{1,0:T(8,128)}, bf16[1024,1536]{1,0:T(8,128)(2,1)}, bf16[1024,2048]{1,0:T(8,128)(2,1)}, bf16[512,1024]{1,0:T(8,128)(2,1)}, bf16[2048,1024]{1,0:T(8,128)(2,1)}, /*index=5*/f32[512,128]{1,0:T(8,128)}) custom-call(f32[256,1024]{1,0:T(8,128)} %get-tuple-element.62.x_in, bf16[256,1024]{1,0:T(8,128)(2,1)} %dy.1, ...), custom_call_target="tpu_custom_call" | custom-call | tf_op jit(solution)/shard_map/backward1/pallas_call | solution.py:1216
  250.8 0.0 copy-start.6
  250.8 48.8 %backward0.1 = (f32[256,1024]{1,0:T(8,128)}, bf16[1024,1536]{1,0:T(8,128)(2,1)}, bf16[1024,2048]{1,0:T(8,128)(2,1)}, bf16[512,1024]{1,0:T(8,128)(2,1)}, bf16[2048,1024]{1,0:T(8,128)(2,1)}, /*index=5*/f32[512,128]{1,0:T(8,128)}) custom-call(bf16[256,1024]{1,0:T(8,128)(2,1)} %x_in.3, f32[256,1024]{1,0:T(8,128)} %get-tuple-element.77.dy, ...), custom_call_target="tpu_custom_call" | custom-call | tf_op jit(solution)/shard_map/backward0/pallas_call | solution.py:1216
  299.6 0.0 copy-done.6
  299.6 1.0 slice.72
  300.6 0.1 pad.36.clone
  300.7 0.8 maximum_maximum_fusion
  301.4 0.0 copy-start.1
  301.4 0.0 copy-start
  301.5 141.7 %scatter.1 = (f32[2,16,3072]{2,1,0:T(8,128)}, f32[2,16,4096]{2,1,0:T(8,128)}, f32[2,16,1024]{2,1,0:T(8,128)}, f32[2,64,1024]{2,1,0:T(8,128)}, f32[8,128]{1,0:T(8,128)}) custom-call(bf16[2,4,4,32,1536]{4,3,2,1,0:T(8,128)(2,1)} %bitcast.81, bf16[2,4,4,32,2048]{4,3,2,1,0:T(8,128)(2,1)} %bitcast.73, bf16[1,4,4,32,1024]{4,3,2,1,0:T(8,128)(2,1)} %bitcast.84, ...), custom_call_target="tpu_custom_call" | custom-call | tf_op jit(solution)/shard_map/scatter/pallas_call | solution.py:714
  443.2 0.0 copy-start.4
  443.2 0.0 copy-start.5
  443.2 0.0 copy-start.3
  443.2 0.0 copy-start.2
  443.2 0.8 reshape.113
  444.0 0.6 slice.74
  444.6 0.6 slice.75
  445.1 0.6 fusion.2
  445.8 0.0 copy-done.1
  445.8 0.8 copy.38
  446.6 0.0 copy-done
  446.6 1.0 copy.39
  447.5 0.0 copy-done.4
  447.5 0.7 copy.40
  448.3 0.0 copy-done.5
  448.3 0.7 copy.41
  448.9 0.0 copy-done.3
  449.0 0.8 copy.42
  449.7 0.0 copy-done.2
  449.7 0.8 copy.43
  (5 shorter events, 0.1 us)
Async XLA Ops:
  250.8 48.8 %copy-start.6 = (f32[512,128]{1,0:T(8,128)S(1)}, f32[512,128]{1,0:T(8,128)}, u32[]{:S(2)}) copy-start(f32[512,128]{1,0:T(8,128)} %get-tuple-element.94) | copy-start | bytes 786436
  301.4 144.3 %copy-start.1 = (bf16[256,1024]{1,0:T(8,128)(2,1)S(1)}, bf16[256,1024]{1,0:T(8,128)(2,1)}, u32[]{:S(2)}) copy-start(bf16[256,1024]{1,0:T(8,128)(2,1)} %get-tuple-element.133) | copy-start | bytes 1572868
  301.4 145.1 %copy-start = (f32[256,1024]{1,0:T(8,128)S(1)}, f32[256,1024]{1,0:T(8,128)}, u32[]{:S(2)}) copy-start(f32[256,1024]{1,0:T(8,128)} %get-tuple-element.134) | copy-start | bytes 3145732
  443.2 4.4 copy-start.4
  443.2 5.1 %copy-start.5 = (f32[2,16,1024]{2,1,0:T(8,128)S(1)}, f32[2,16,1024]{2,1,0:T(8,128)}, u32[]{:S(2)}) copy-start(f32[2,16,1024]{2,1,0:T(8,128)} %get-tuple-element.137) | copy-start | bytes 393220
  443.2 5.8 %copy-start.3 = (f32[2,16,4096]{2,1,0:T(8,128)S(1)}, f32[2,16,4096]{2,1,0:T(8,128)}, u32[]{:S(2)}) copy-start(f32[2,16,4096]{2,1,0:T(8,128)} %get-tuple-element.138) | copy-start | bytes 1572868
  443.2 6.6 %copy-start.2 = (f32[2,64,1024]{2,1,0:T(8,128)S(1)}, f32[2,64,1024]{2,1,0:T(8,128)}, u32[]{:S(2)}) copy-start(f32[2,64,1024]{2,1,0:T(8,128)} %get-tuple-element.140) | copy-start | bytes 1572868

commit v3 on v0

v3 whole, which is shorter than its diff:
```python
import functools
import math

import jax
import jax.numpy as jnp
import numpy as np
from jax import lax
from jax.experimental import pallas as pl
from jax.experimental.pallas import tpu as pltpu
from jax.sharding import PartitionSpec as P


MESH = pl.DeviceIdType.MESH
LANE = 128
LAYERS = 2


def place():
    xl = lax.axis_index("rep")
    s = lax.axis_index("shard")
    return xl, s // 32, (s // 8) % 4, (s // 2) % 4, s % 2


def at(xl, xh, z, y, c):
    return (xl, xh * 32 + z * 8 + y * 2 + c)


def around(value, step):
    return lax.rem(value + (step + 4), 4)


def meet(others):
    barrier = pltpu.get_barrier_semaphore()
    for other in others:
        pl.semaphore_signal(barrier, inc=1, device_id=other, device_id_type=MESH)
    pl.semaphore_wait(barrier, len(others))


GATHERED = (
    ("small", True, 32, 128, 0, 1),
    ("qkv", True, 32, 1536, 4, 8),
    ("up", True, 32, 2048, 5, 11),
    ("out", False, 32, 1024, 3, 5),
    ("down", False, 128, 1024, 3, 5),
)
SLOTS = 18


class Stream:
    def __init__(self, number, spec, source, target, send, recv, xl, xh, z, y, core):
        self.name, self.by_columns, self.rows, self.columns, self.swapped, self.width = spec
        self.number = number
        self.source = source
        self.target = target
        self.send, self.recv = send, recv
        self.xl, self.xh, self.z, self.y, self.core = xl, xh, z, y, core
        self.half = self.rows // 2
        self.wide = pl.ds(pl.multiple_of(xl * (self.swapped * LANE), LANE), self.width * LANE)
        self.mine = pl.ds(
            pl.multiple_of(xl * ((self.width - self.swapped) * LANE) + xl * (self.swapped * LANE), LANE),
            max(self.swapped, 1) * LANE,
        )
        self.theirs = pl.ds(
            pl.multiple_of((1 - xl) * (self.width * LANE), LANE), max(self.swapped, 1) * LANE
        )
        self.across = lambda core_of: at(1 - xl, 1 - xh, z, y, core_of)
        self.partner = at(1 - xl, xh, z, y, core) if core == 0 else self.across(core)
        if core == 0:
            self.first, self.second = y, z
        else:
            self.first, self.second = z, y
        self.sent = []

    def neighbour(self, ring, step):
        z, y = self.z, self.y
        if (ring == 0) == (self.core == 0):
            y = around(y, step)
        else:
            z = around(z, step)
        return at(self.xl, self.xh, z, y, self.core)

    def block(self, first, rows, columns):
        if self.core == 0:
            return self.target.at[:, self.second, first, rows, columns]
        return self.target.at[:, first, self.second, rows, columns]

    def line(self, second, rows, columns):
        if self.core == 0:
            return self.target.at[:, second, :, rows, columns]
        return self.target.at[:, :, second, rows, columns]

    def push(self, region, slot, device):
        copy = pltpu.make_async_remote_copy(
            region(),
            region(),
            self.send.at[self.number, slot],
            self.recv.at[self.number, slot],
            device_id=device,
            device_id_type=MESH,
        )
        copy.start()
        self.sent.append((region, slot))

    def arrived(self, region, slot):
        pltpu.make_async_copy(region, region, self.recv.at[self.number, slot]).wait()

    def part(self, core_of):
        return pl.ds(core_of * self.half, self.half)

    def stage0(self):
        xh, z, y, core = self.xh, self.z, self.y, self.core
        whole = slice(None)
        if self.by_columns:
            region = lambda: self.target.at[xh, z, y, self.part(core), :]
            here = region()
            landed = self.recv.at[self.number, xh * 2 + core]
            for source, columns in self.source(core):
                pltpu.make_async_copy(source, here.at[:, columns], landed).start()
            for slot, half, device in (
                (0, 1 - core, at(self.xl, xh, z, y, 1 - core)),
                (1, core, self.across(core)),
                (2, 1 - core, self.across(1 - core)),
            ):
                for source, columns in self.source(half):
                    pltpu.make_async_remote_copy(
                        source,
                        here.at[:, columns],
                        self.send.at[self.number, slot],
                        landed,
                        device_id=device,
                        device_id_type=MESH,
                    ).start()
                self.sent.append((region, slot))
        else:
            here = self.target.at[0, z, y, self.part(core), :]
            mine = self.source(0)

            @pl.when(xh == core)
            def _():
                pltpu.make_async_copy(mine, here, self.recv.at[self.number, core]).start()

            @pl.when(xh != core)
            def _():
                pltpu.make_async_remote_copy(
                    mine,
                    here,
                    self.send.at[self.number, 0],
                    self.recv.at[self.number, core],
                    device_id=at(self.xl, xh, z, y, 1 - core),
                    device_id_type=MESH,
                ).start()

            pltpu.make_async_remote_copy(
                mine,
                here,
                self.send.at[self.number, 1],
                self.recv.at[self.number, core],
                device_id=self.across(xh),
                device_id_type=MESH,
            ).start()
            self.sent.append((lambda: self.source(0), 1))

    def stage1(self):
        whole = slice(None)
        for bank in range(2 if self.by_columns else 1):
            for core_of in range(2):
                self.arrived(
                    self.target.at[bank, self.z, self.y, self.part(core_of), :], bank * 2 + core_of
                )
        own = lambda: self.block(self.first, whole, self.wide)
        self.push(own, 4, self.neighbour(0, 1))
        self.push(own, 5, self.neighbour(0, -1))

    def share(self, region, slot):
        if self.swapped:
            self.push(lambda: region(self.mine), slot, self.partner)

    def stage2(self):
        whole = slice(None)
        for step, slot in ((-1, 4), (1, 5)):
            found = lambda rows, columns, step=step: self.block(
                around(self.first, step), rows, columns
            )
            self.arrived(found(whole, self.wide), slot)
            self.push(
                lambda found=found, slot=slot: found(self.part(slot - 4), self.wide),
                slot + 2,
                self.neighbour(0, -step),
            )
            self.share(lambda columns, found=found: found(whole, columns), slot + 8)

    def stage3(self):
        whole = slice(None)
        far = lambda rows, columns: self.block(around(self.first, 2), rows, columns)
        for half in range(2):
            self.arrived(far(self.part(half), self.wide), 6 + half)
        own = lambda: self.line(self.second, whole, self.wide)
        self.push(own, 8, self.neighbour(1, 1))
        self.push(own, 9, self.neighbour(1, -1))
        self.share(lambda columns: far(whole, columns), 14)

    def stage4(self):
        whole = slice(None)
        for step, slot in ((-1, 8), (1, 9)):
            found = lambda rows, columns, step=step: self.line(
                around(self.second, step), rows, columns
            )
            self.arrived(found(whole, self.wide), slot)
            self.push(
                lambda found=found, slot=slot: found(self.part(slot - 8), self.wide),
                slot + 2,
                self.neighbour(1, -step),
            )
            self.share(lambda columns, found=found: found(whole, columns), slot + 7)

    def stage5(self):
        whole = slice(None)
        far = lambda rows, columns: self.line(around(self.second, 2), rows, columns)
        for half in range(2):
            self.arrived(far(self.part(half), self.wide), 10 + half)
        self.share(lambda columns: far(whole, columns), 17)

    def stage6(self):
        whole = slice(None)
        if self.swapped:
            for step, slot in ((-1, 12), (1, 13), (2, 14)):
                self.arrived(self.block(around(self.first, step), whole, self.theirs), slot)
            for step, slot in ((-1, 15), (1, 16), (2, 17)):
                self.arrived(self.line(around(self.second, step), whole, self.theirs), slot)

    def finish(self):
        for region, slot in self.sent:
            pltpu.make_async_copy(region(), region(), self.send.at[self.number, slot]).wait()
        if not self.by_columns:

            @pl.when(self.xh != self.core)
            def _():
                mine = self.source(0)
                pltpu.make_async_copy(mine, mine, self.send.at[self.number, 0]).wait()


def owned_pieces(name, owned, layer_at):
    if name == "small":
        return lambda half: [(owned, slice(None))]
    if name == "qkv":
        return lambda half: [
            (
                owned.at[layer_at, :, pl.ds(third * 1024 + half * 512, 512)],
                pl.ds(third * 512, 512),
            )
            for third in range(3)
        ]
    if name == "up":
        return lambda half: [(owned.at[layer_at, :, pl.ds(half * 2048, 2048)], slice(None))]
    return lambda half: owned.at[layer_at]


def neighbours():
    xl, xh, z, y, c = place()
    return [
        at(xl, xh, z, y, 1 - c),
        at(1 - xl, 1 - xh, z, y, c),
        at(1 - xl, 1 - xh, z, y, 1 - c),
        at(xl, 1 - xh, z, y, c),
        at(1 - xl, xh, z, y, c),
        at(xl, xh, around(z, 1), y, c),
        at(xl, xh, around(z, -1), y, c),
        at(xl, xh, z, around(y, 1), c),
        at(xl, xh, z, around(y, -1), c),
    ]


COUNT = 256
BOTH = 512
D = 1024
HEAD_DIM = 64
ROT = 16
EPS = 1e-05
FILL = -1e30
F32 = jnp.float32
BF16 = jnp.bfloat16
TILE = 256


def turn_tables():
    places = np.arange(COUNT, dtype=np.float32)
    rates = np.float32(10000.0) ** (-np.arange(0, ROT, 2, dtype=np.float32) / np.float32(ROT))
    angles = places[:, None] * rates[None, :]
    cosine, sine = np.cos(angles), np.sin(angles)
    half = ROT // 2
    keep = np.ones((COUNT, HEAD_DIM), np.float32)
    ahead = np.zeros((COUNT, HEAD_DIM), np.float32)
    behind = np.zeros((COUNT, HEAD_DIM), np.float32)
    keep[:, :half] = cosine
    keep[:, half:ROT] = cosine
    ahead[:, :half] = -sine
    behind[:, half:ROT] = sine
    return np.stack([np.concatenate([t, t], 1) for t in (keep, ahead, behind)])


def turn(values, tables, sign):
    return values * tables[0] + sign * (
        pltpu.roll(values, LANE - ROT // 2, 1) * tables[1]
        + pltpu.roll(values, ROT // 2, 1) * tables[2]
    )


def dot(left, right):
    return jnp.dot(left, right, preferred_element_type=F32)


def dot_nt(left, right):
    return lax.dot_general(left, right, (((1,), (1,)), ((), ())), preferred_element_type=F32)


def dot_tn(left, right):
    return lax.dot_general(left, right, (((0,), (0,)), ((), ())), preferred_element_type=F32)


def columns_of(index, width=TILE):
    return pl.ds(pl.multiple_of(index * width, width), width)


def loop(count, body):
    def step(index, carry):
        body(index)
        return carry

    lax.fori_loop(0, count, step, 0)


KINDS = {
    "b_qkv": (0, 48, 43691, 21),
    "b_up": (1, 64, 1, 6),
    "gain": (2, 16, 1, 4),
    "shift": (3, 16, 1, 4),
    "out_bias": (4, 16, 1, 4),
}
OWNED_ROWS = 16
CHUNK = 512


def chunks_of(kind, core):
    if kind == "b_qkv":
        return [(t * CHUNK, t * 1024 + core * CHUNK) for t in range(3)]
    if kind == "b_up":
        return [(t * CHUNK, core * 2048 + t * CHUNK) for t in range(4)]
    return [(t * CHUNK, t * CHUNK) for t in range(2)]


def owner_masks(kind, start):
    row, size, factor, shift = KINDS[kind]
    place_of = lax.broadcasted_iota(jnp.int32, (LANE, CHUNK), 1) + start
    owner = lax.shift_right_logical(place_of * factor, shift)
    within = place_of - owner * size
    spread = lax.broadcasted_iota(jnp.int32, (LANE, CHUNK), 0) == within
    owned = lax.broadcasted_iota(jnp.int32, (64, CHUNK), 0) == owner[:64]
    return spread, owned


def unpack_vector(rows_ref, layer_at, kind, core, target):
    row = KINDS[kind][0] + 5 * layer_at
    held = rows_ref[pl.ds(row, 64, stride=OWNED_ROWS), :].astype(BF16)
    for place_at, start in chunks_of(kind, core):
        spread, owned = owner_masks(kind, start)
        every = dot(held, jnp.where(spread, 1.0, 0.0).astype(BF16))
        target[:, pl.ds(place_at, CHUNK)] = jnp.sum(
            jnp.where(owned, every, 0.0), 0, keepdims=True
        )


def pack_vector(rows_ref, layer_at, kind, core, vector):
    total = jnp.zeros((64, LANE), F32)
    for place_at, start in chunks_of(kind, core):
        spread, owned = owner_masks(kind, start)
        mine = jnp.where(owned, vector[:, pl.ds(place_at, CHUNK)], 0.0)
        spread = jnp.where(spread, 1.0, 0.0).astype(BF16)
        high = mine.astype(BF16)
        total = total + dot_nt(high, spread)
        total = total + dot_nt((mine - high.astype(F32)).astype(BF16), spread)
    rows_ref[pl.ds(KINDS[kind][0] + 5 * layer_at, 64, stride=OWNED_ROWS), :] = total


def centre(values):
    centred = values - jnp.mean(values, -1, keepdims=True)
    inv_std = lax.rsqrt(jnp.mean(centred * centred, -1, keepdims=True) + EPS)
    return centred * inv_std, inv_std


def norm_piece(x_ref, gain, shift, hidden):
    def body(index):
        rows = columns_of(index, 64)
        normed, unused = centre(x_ref[rows, :])
        hidden[rows, :] = (normed * gain[...] + shift[...]).astype(BF16)

    loop(COUNT // 64, body)


def joined_piece(third, hidden, w_qkv, b_qkv, tables, target):
    def body(index):
        columns = columns_of(index + third * 2)
        found = dot(hidden[...], w_qkv(columns)) + b_qkv[:, columns]
        for sequence in range(2):
            for pair in range(2):
                part = found[sequence * COUNT : (sequence + 1) * COUNT, pair * LANE : (pair + 1) * LANE]
                if third < 2:
                    part = turn(part, tables, 1.0)
                if third == 0:
                    part = part * HEAD_DIM**-0.5
                target[
                    pl.ds(sequence * COUNT, COUNT), columns_of(index * 2 + pair + third * 4, LANE)
                ] = part.astype(BF16)

    loop(2, body)


def first_head():
    return lax.broadcasted_iota(jnp.int32, (COUNT, LANE), 1) < HEAD_DIM


def only_head(values, half):
    keep = first_head() if half == 0 else jnp.logical_not(first_head())
    return jnp.where(keep, values, jnp.zeros_like(values))


def attention_piece(turned, probs, mixed, start=0, stop=8):
    def body(index):
        index = index + start
        sequence, pair = index // 4, index % 4
        rows, columns = columns_of(sequence, COUNT), columns_of(pair, LANE)
        q2, k2, v2 = (turned[rows, columns_of(pair + third * 4, LANE)] for third in range(3))
        causal = lax.broadcasted_iota(jnp.int32, (COUNT, COUNT), 0) >= lax.broadcasted_iota(
            jnp.int32, (COUNT, COUNT), 1
        )
        out = []
        for half in range(2):
            scores = jnp.where(causal, dot_nt(only_head(q2, half), k2), FILL)
            expo = jnp.exp(scores - jnp.max(scores, -1, keepdims=True))
            prob = (expo * (1.0 / jnp.sum(expo, -1, keepdims=True))).astype(BF16)
            probs[index * 2 + half] = prob
            out.append(dot(prob, v2))
        mixed[rows, columns] = jnp.where(first_head(), out[0], out[1]).astype(BF16)

    loop(stop - start, body)


def up_piece(hidden, w_up, b_up, active, slope):
    def body(index):
        columns = columns_of(index)
        upward = dot(hidden[...], w_up(columns)) + b_up[:, columns]
        spread = 0.5 + 0.5 * lax.erf(upward * (0.5**0.5))
        active[:, columns] = (upward * spread).astype(BF16)
        dense = jnp.exp(upward * upward * -0.5) * (1.0 / math.sqrt(2.0 * math.pi))
        slope[:, columns] = (spread + upward * dense).astype(BF16)

    loop(8, body)


def down_piece(active, w_down, mixed, w_out, partial):
    def body(index):
        columns = columns_of(index)
        partial[:, columns] = dot(mixed[...], w_out(columns)) + dot(active[...], w_down(columns))

    loop(4, body)


def residual_piece(x_ref, partial, received, out_bias, target):
    def body(index):
        rows = columns_of(index, 64)
        target[rows, :] = (
            x_ref[rows, :] + (partial[rows, :] + received[rows, :]) + out_bias[...]
        ).astype(target.dtype)

    loop(COUNT // 64, body)


def start_piece(dy, dy_low, out_bias_grad):
    def body(index):
        rows = columns_of(index, 64)
        values = dy[rows, :]
        dy_low[rows, :] = values.astype(BF16)
        out_bias_grad[...] += jnp.sum(values, 0, keepdims=True)

    out_bias_grad[...] = jnp.zeros_like(out_bias_grad)
    loop(COUNT // 64, body)


def flip_piece(source, target):
    rows, columns = source.shape
    for at_row in range(rows // TILE):

        def body(index, at_row=at_row):
            target[columns_of(index), pl.ds(at_row * TILE, TILE)] = source[
                pl.ds(at_row * TILE, TILE), columns_of(index)
            ].T

        loop(columns // TILE, body)


def rows_grad_piece(count, left, right, store):
    def body(index):
        store(index, dot_tn(left[:, columns_of(index)], right[...]).astype(BF16))

    loop(count, body)


def columns_grad_piece(count, left_flipped, right, store):
    def body(index):
        store(index, dot(left_flipped[...], right[:, columns_of(index)]).astype(BF16))

    loop(count, body)


def slope_piece(dy_low, w_down_rows, slope, d_up, b_up_grad):
    def body(index):
        columns = columns_of(index)
        found = (dot_nt(dy_low[...], w_down_rows(index)) * slope[:, columns].astype(F32)).astype(BF16)
        d_up[:, columns] = found
        b_up_grad[:, columns] = jnp.sum(found.astype(F32), 0, keepdims=True)

    loop(8, body)


def d_mixed_piece(dy_low, w_out_rows, d_mixed):
    def body(index):
        d_mixed[:, columns_of(index)] = dot_nt(dy_low[...], w_out_rows(index)).astype(BF16)

    loop(2, body)


def attention_back_piece(turned, probs, d_mixed, tables, d_joined, b_qkv_grad, start=0, stop=8):
    if start == 0:
        b_qkv_grad[...] = jnp.zeros_like(b_qkv_grad)

    def body(index):
        index = index + start
        sequence, pair = index // 4, index % 4
        rows, columns = columns_of(sequence, COUNT), columns_of(pair, LANE)
        q2, k2, v2 = (turned[rows, columns_of(pair + third * 4, LANE)] for third in range(3))
        dm2 = d_mixed[rows, columns]
        found = []
        for half in range(2):
            prob = probs[index * 2 + half]
            full = prob.astype(F32)
            d_probs = dot_nt(only_head(dm2, half), v2)
            d_scores = (
                full * (d_probs - jnp.sum(d_probs * full, -1, keepdims=True))
            ).astype(BF16)
            found.append((dot(d_scores, k2), dot_tn(d_scores, q2), dot_tn(prob, dm2)))
        for third in range(3):
            part = jnp.where(first_head(), found[0][third], found[1][third])
            if third == 0:
                part = part * HEAD_DIM**-0.5
            if third < 2:
                part = turn(part, tables, -1.0)
            part = part.astype(BF16)
            there = columns_of(pair + third * 4, LANE)
            d_joined[rows, there] = part
            b_qkv_grad[:, there] += jnp.sum(part.astype(F32), 0, keepdims=True)

    loop(stop - start, body)


def d_hidden_piece(d_joined, w_qkv_rows, d_up, w_up_rows, d_hidden):
    def body(index):
        d_hidden[:, columns_of(index)] = dot_nt(d_joined[...], w_qkv_rows(index)) + dot_nt(
            d_up[...], w_up_rows(index)
        )

    loop(4, body)


def norm_back_piece(x_ref, gain, dy, d_hidden, received, target, gain_grad, shift_grad):
    gain_grad[...] = jnp.zeros_like(gain_grad)
    shift_grad[...] = jnp.zeros_like(shift_grad)

    def body(index):
        rows = columns_of(index, 64)
        normed, inv_std = centre(x_ref[rows, :].astype(F32))
        total = d_hidden[rows, :] + received[rows, :]
        gain_grad[...] += jnp.sum(total * normed, 0, keepdims=True)
        shift_grad[...] += jnp.sum(total, 0, keepdims=True)
        scaled = total * gain[...]
        target[rows, :] = dy[rows, :].astype(F32) + inv_std * (
            scaled
            - jnp.mean(scaled, -1, keepdims=True)
            - normed * jnp.mean(scaled * normed, -1, keepdims=True)
        )

    loop(COUNT // 64, body)


class Pair:
    def __init__(self, send, recv):
        xl, xh, z, y, c = place()
        self.device = at(xl, xh, z, y, 1 - c)
        self.send, self.recv = send, recv

    def push(self, source, target, slot):
        pltpu.make_async_remote_copy(
            source,
            target,
            self.send.at[slot],
            self.recv.at[slot],
            device_id=self.device,
            device_id_type=MESH,
        ).start()

    def wait(self, source, target, slot):
        pltpu.make_async_copy(source, source, self.send.at[slot]).wait()
        pltpu.make_async_copy(target, target, self.recv.at[slot]).wait()


class Moves:
    def __init__(self, done):
        self.done = done
        self.count = 0
        self.open = []

    def start(self, source, target):
        copy = pltpu.make_async_copy(source, target, self.done.at[self.count])
        self.count += 1
        copy.start()
        self.open.append(copy)
        return copy

    def finish(self, copy):
        copy.wait()
        self.open = [other for other in self.open if other is not copy]


KEPT = (
    ("flipped", (D, BOTH), BF16),
    ("turned", (BOTH, 1536), BF16),
    ("probs", (16, COUNT, COUNT), BF16),
    ("mixed", (BOTH, 512), BF16),
    ("active", (BOTH, 2048), BF16),
    ("slope", (BOTH, 2048), BF16),
    ("gain", (1, D), F32),
)
WEIGHTS = GATHERED[1:]


def weight_shape(spec):
    name, by_columns, rows, columns, swapped, width = spec
    return (2 if by_columns else 1, 4, 4, rows, columns)


def all_rows(weight, columns):
    found = weight[:, :, :, :, columns]
    return found.reshape(-1, found.shape[-1])


def forward_kernel(tokens, b_qkv, b_up, ln_gain, ln_bias, out_bias, tables, qkv, up, out, down, *rest):
    rest = list(rest)

    def take(count):
        found = rest[:count]
        del rest[:count]
        return found

    (result, x_kept) = take(2)
    gathered = [take(4) for layer_at in range(LAYERS)]
    kept_out = [dict(zip((k[0] for k in KEPT), take(len(KEPT)))) for layer_at in range(LAYERS)]
    kept = [dict(zip((k[0] for k in KEPT), take(len(KEPT)))) for layer_at in range(LAYERS)]
    weights = [take(4) for layer_at in range(LAYERS)]
    vectors = [dict(zip(("b_qkv", "b_up", "shift", "out_bias"), take(4))) for layer_at in range(LAYERS)]
    owned, every, rows, x0, x1, last = take(6)
    hidden = take(2)
    partial, = take(1)
    received = take(2)
    send, recv, pair_send, pair_recv, moved = take(5)

    owned[...] = jnp.zeros_like(owned)
    for layer_at in range(LAYERS):
        for row, vector in enumerate((b_qkv, b_up, ln_gain, ln_bias, out_bias)):
            owned[5 * layer_at + row : 5 * layer_at + row + 1, : vector.shape[1]] = vector[
                layer_at : layer_at + 1, :
            ].astype(F32)
    xl, xh, z, y, c = place()
    meet(neighbours())
    pair = Pair(pair_send, pair_recv)
    moves = Moves(moved)

    streams = []
    for core in range(2):
        found = [
            Stream(0, GATHERED[0], owned_pieces("small", owned, 0), every, send, recv, xl, xh, z, y, core)
        ]
        for layer_at in range(LAYERS):
            for spec, source, target in zip(WEIGHTS, (qkv, up, out, down), gathered[layer_at]):
                found.append(
                    Stream(
                        len(found), spec, owned_pieces(spec[0], source, layer_at), target,
                        send, recv, xl, xh, z, y, core,
                    )
                )
        streams.append(found)
    count = len(streams[0])

    def tick(time):
        for core in range(2):

            @pl.when(c == core)
            def _():
                for stage in range(7):
                    if 0 <= time - stage < count:
                        getattr(streams[core][time - stage], f"stage{stage}")()

    loads = {}

    def load(layer_at, which):
        loads[layer_at, which] = moves.start(gathered[layer_at][which], weights[layer_at][which])

    def loaded(layer_at, which):
        moves.finish(loads[layer_at, which])

    def keep(layer_at, name):
        moves.start(kept[layer_at][name], kept_out[layer_at][name])

    own, other = pl.ds(0, COUNT), pl.ds(COUNT, COUNT)
    inputs = (x0, x1)

    def vectors_step():
        rows[...] = every[...].reshape(rows.shape)
        for core in range(2):

            @pl.when(c == core)
            def _():
                for layer_at in range(LAYERS):
                    for kind in KINDS:
                        target = kept[layer_at]["gain"] if kind == "gain" else vectors[layer_at][kind]
                        unpack_vector(rows, layer_at, kind, core, target)

        for layer_at in range(LAYERS):
            keep(layer_at, "gain")

    def norm_step(layer_at):
        norm_piece(inputs[layer_at], kept[layer_at]["gain"], vectors[layer_at]["shift"], hidden[layer_at])
        pair.push(hidden[layer_at].at[own], hidden[layer_at].at[other], 2 * layer_at)

    def joined_step(layer_at):
        pair.wait(hidden[layer_at].at[own], hidden[layer_at].at[other], 2 * layer_at)
        loaded(layer_at, 0)
        for third in range(3):
            joined_piece(
                third,
                hidden[layer_at],
                lambda n: all_rows(weights[layer_at][0], n),
                vectors[layer_at]["b_qkv"],
                tables,
                kept[layer_at]["turned"],
            )
        keep(layer_at, "turned")
        flip_piece(hidden[layer_at], kept[layer_at]["flipped"])
        keep(layer_at, "flipped")

    def attention_step(layer_at, start, stop):
        attention_piece(
            kept[layer_at]["turned"], kept[layer_at]["probs"], kept[layer_at]["mixed"], start, stop
        )
        if stop == 8:
            keep(layer_at, "probs")
            keep(layer_at, "mixed")

    def up_step(layer_at):
        loaded(layer_at, 1)
        up_piece(
            hidden[layer_at],
            lambda n: all_rows(weights[layer_at][1], n),
            vectors[layer_at]["b_up"],
            kept[layer_at]["active"],
            kept[layer_at]["slope"],
        )
        keep(layer_at, "active")
        keep(layer_at, "slope")

    def down_step(layer_at):
        loaded(layer_at, 2)
        loaded(layer_at, 3)
        if layer_at:
            pltpu.make_async_copy(partial.at[other], partial.at[other], pair_send.at[1]).wait()
        down_piece(
            kept[layer_at]["active"],
            lambda n: all_rows(weights[layer_at][3], n),
            kept[layer_at]["mixed"],
            lambda n: all_rows(weights[layer_at][2], n),
            partial,
        )
        pair.push(partial.at[other], received[layer_at], 2 * layer_at + 1)

    def residual_step(layer_at):
        target = received[layer_at]
        pltpu.make_async_copy(target, target, pair_recv.at[2 * layer_at + 1]).wait()
        residual_piece(
            inputs[layer_at],
            partial,
            target,
            vectors[layer_at]["out_bias"],
            x1 if layer_at == 0 else last,
        )
        if layer_at == 0:
            moves.start(x1, x_kept)
        else:
            pltpu.make_async_copy(partial.at[other], partial.at[other], pair_send.at[3]).wait()
            moves.start(last, result)

    x0[...] = tokens[...].astype(F32)
    for time in range(7):
        tick(time)
    vectors_step()
    norm_step(0)
    tick(7)
    load(0, 0)
    tick(8)
    load(0, 1)
    joined_step(0)
    tick(9)
    load(0, 2)
    attention_step(0, 0, 8)
    tick(10)
    load(0, 3)
    up_step(0)
    tick(11)
    load(1, 0)
    down_step(0)
    tick(12)
    load(1, 1)
    residual_step(0)
    norm_step(1)
    joined_step(1)
    tick(13)
    load(1, 2)
    attention_step(1, 0, 8)
    tick(14)
    load(1, 3)
    up_step(1)
    down_step(1)
    for core in range(2):

        @pl.when(c == core)
        def _():
            for stream in streams[core]:
                stream.finish()

    residual_step(1)
    for copy in list(moves.open):
        copy.wait()


def forward_call(tokens, b_qkv, b_up, ln_gain, ln_bias, out_bias, tables, qkv, up, out, down):
    vmem, hbm = pl.BlockSpec(memory_space=pltpu.VMEM), pl.BlockSpec(memory_space=pltpu.HBM)
    shape = jax.ShapeDtypeStruct
    outs = [shape((COUNT, D), BF16), shape((COUNT, D), F32)]
    scratch = []
    for layer_at in range(LAYERS):
        outs += [shape(weight_shape(spec), BF16) for spec in WEIGHTS]
    for layer_at in range(LAYERS):
        outs += [shape(dims, kind) for name, dims, kind in KEPT]
        scratch += [pltpu.VMEM(dims, kind) for name, dims, kind in KEPT]
    for layer_at in range(LAYERS):
        scratch += [pltpu.VMEM(weight_shape(spec), BF16) for spec in WEIGHTS]
    for layer_at in range(LAYERS):
        scratch += [pltpu.VMEM((1, n), F32) for n in (1536, 2048, D, D)]
    scratch += [
        pltpu.VMEM((OWNED_ROWS, LANE), F32),
        pltpu.VMEM((2, 4, 4, 2 * OWNED_ROWS, LANE), F32),
        pltpu.VMEM((64 * OWNED_ROWS, LANE), F32),
        pltpu.VMEM((COUNT, D), F32),
        pltpu.VMEM((COUNT, D), F32),
        pltpu.VMEM((COUNT, D), BF16),
        pltpu.VMEM((BOTH, D), BF16),
        pltpu.VMEM((BOTH, D), BF16),
        pltpu.VMEM((BOTH, D), F32),
        pltpu.VMEM((COUNT, D), F32),
        pltpu.VMEM((COUNT, D), F32),
        pltpu.SemaphoreType.DMA((1 + 4 * LAYERS, SLOTS)),
        pltpu.SemaphoreType.DMA((1 + 4 * LAYERS, SLOTS)),
        pltpu.SemaphoreType.DMA((4,)),
        pltpu.SemaphoreType.DMA((4,)),
        pltpu.SemaphoreType.DMA((40,)),
    ]
    return pl.pallas_call(
        forward_kernel,
        out_shape=outs,
        in_specs=[vmem] * 7 + [hbm] * 4,
        out_specs=[hbm] * len(outs),
        scratch_shapes=scratch,
        name="forward",
        compiler_params=pltpu.CompilerParams(
            collective_id=0, has_side_effects=True, vmem_limit_bytes=60 * 2**20
        ),
    )(tokens, b_qkv, b_up, ln_gain, ln_bias, out_bias, tables, qkv, up, out, down)


SUMMED = (
    ("qkv", True, 32, 1536, 3, 9),
    ("up", True, 32, 2048, 4, 12),
    ("out", False, 32, 1024, 2, 6),
    ("down", False, 128, 1024, 2, 6),
    ("small", True, 32, 128, 0, 1),
)
SUM_SLOTS = 18
BUFFERS = 9


def total_shape(spec):
    name, by_columns, rows, columns, swapped, width = spec
    return (2 if by_columns else 1, 4, 4, rows, columns)


def landing_shapes(spec):
    name, by_columns, rows, columns, swapped, width = spec
    banks = 2 if by_columns else 1
    kind = F32 if name == "small" else BF16
    wide = width * LANE
    return [
        pltpu.VMEM((banks, 4, 4, rows, swapped * LANE) if swapped else (8, LANE), kind),
        pltpu.VMEM((2, banks, 4, rows // 2, wide), kind),
        pltpu.VMEM((2, banks, 4, rows, wide), kind),
        pltpu.VMEM((banks, 4, rows, wide), kind),
        pltpu.VMEM((2, banks, rows // 2, wide), kind),
        pltpu.VMEM((2, banks, rows, wide), kind),
        pltpu.VMEM((3, rows, wide), kind),
        pltpu.VMEM((rows, columns), F32),
        pltpu.VMEM((2, 16, LANE), F32),
    ]


def add_into(target, first, *others):
    if len(others) == 1:
        target[...] = first[...] + others[0][...]
    else:
        found = first[...].astype(F32)
        for other in others:
            found = found + other[...].astype(F32)
        target[...] = found.astype(target.dtype)


class Sum:
    def __init__(self, number, which, before, total, landing, output, send, recv, free, where, core):
        spec = SUMMED[which]
        self.name, self.by_columns, self.rows, self.columns, self.swapped, self.width = spec
        self.number, self.which = number, which
        self.before = before
        self.after = not before and self.name != "small"
        self.total, self.output = total, output
        (
            self.swap,
            self.far_line,
            self.near_line,
            self.line,
            self.far_block,
            self.near_block,
            self.last,
            self.ready,
            self.tail,
        ) = landing
        self.send, self.recv, self.free = send, recv, free
        self.xl, self.xh, self.z, self.y = where
        self.core = core
        self.banks = 2 if self.by_columns else 1
        self.half = self.rows // 2
        s, w = self.swapped, self.width
        xl, xh, z, y = where
        self.wide = pl.ds(pl.multiple_of(xl * (s * LANE), LANE), w * LANE)
        self.mine = pl.ds(pl.multiple_of(xl * (w * LANE), LANE), max(s, 1) * LANE)
        self.theirs = pl.ds(pl.multiple_of((1 - xl) * (w * LANE), LANE), max(s, 1) * LANE)
        self.beside = at(1 - xl, xh, z, y, core)
        self.across = at(1 - xl, 1 - xh, z, y, core)
        self.beyond = at(xl, 1 - xh, z, y, core)
        self.sibling = at(xl, xh, z, y, 1 - core)
        self.partner = self.beside if core == 0 else self.across
        self.first, self.second = (y, z) if core == 0 else (z, y)
        self.sent = []

    def neighbour(self, ring, step):
        z, y = self.z, self.y
        if (ring == 0) == (self.core == 0):
            y = around(y, step)
        else:
            z = around(z, step)
        return at(self.xl, self.xh, z, y, self.core)

    def total_line(self, second, rows, columns):
        if self.core == 0:
            return self.total.at[:, second, :, rows, columns]
        return self.total.at[:, :, second, rows, columns]

    def push(self, source, target, slot, device, keep=True):
        if self.before and slot < 12:
            pl.semaphore_wait(self.free.at[self.which, slot], 1)
        pltpu.make_async_remote_copy(
            source(),
            target,
            self.send.at[self.number, slot],
            self.recv.at[self.number, slot],
            device_id=device,
            device_id_type=MESH,
        ).start()
        if keep:
            self.sent.append((source, slot))

    def release(self, slot, device):
        if self.after:
            pl.semaphore_signal(
                self.free.at[self.which, slot], inc=1, device_id=device, device_id_type=MESH
            )

    def arrived(self, region, slot):
        pltpu.make_async_copy(region, region, self.recv.at[self.number, slot]).wait()

    def settle(self):
        for source, slot in self.sent:
            pltpu.make_async_copy(source(), source(), self.send.at[self.number, slot]).wait()
        self.sent = []

    def part(self, core_of):
        return pl.ds(core_of * self.half, self.half)

    def stage1(self):
        if self.swapped:
            self.push(
                lambda: self.total.at[:, :, :, :, self.theirs], self.swap, 0, self.partner
            )

    def stage2(self):
        if self.swapped:
            self.arrived(self.swap, 0)

            def add(step):
                bank, z, y = step // 16, (step // 4) % 4, step % 4
                region = self.total.at[bank, z, y, :, self.mine]
                add_into(region, region, self.swap.at[bank, z, y])

            loop(self.banks * 16, add)
            self.release(0, self.partner)
        for half in range(2):
            self.push(
                lambda half=half: self.total_line(
                    around(self.second, 2), self.part(half), self.wide
                ),
                self.far_line.at[half],
                1 + half,
                self.neighbour(1, 1 - 2 * half),
            )

    def stage3(self):
        for half in range(2):
            self.arrived(self.far_line.at[half], 1 + half)
            toward = 1 - 2 * half
            rows = self.part(half)

            def add(step):
                bank, place_at = step // 4, step % 4
                region = self.total_line(around(self.second, toward), rows, self.wide).at[
                    bank, place_at
                ]
                add_into(region, region, self.far_line.at[half, bank, place_at])

            loop(self.banks * 4, add)
            self.release(1 + half, self.neighbour(1, -toward))
            self.push(
                lambda toward=toward: self.total_line(
                    around(self.second, toward), slice(None), self.wide
                ),
                self.near_line.at[half],
                3 + half,
                self.neighbour(1, toward),
            )

    def stage4(self):
        for half in range(2):
            self.arrived(self.near_line.at[half], 3 + half)

        def add(step):
            bank, place_at = step // 4, step % 4
            add_into(
                self.line.at[bank, place_at],
                self.total_line(self.second, slice(None), self.wide).at[bank, place_at],
                self.near_line.at[0, bank, place_at],
                self.near_line.at[1, bank, place_at],
            )

        loop(self.banks * 4, add)
        for half in range(2):
            self.release(3 + half, self.neighbour(1, 2 * half - 1))
        self.settle()
        for half in range(2):
            self.push(
                lambda half=half: self.line.at[:, around(self.first, 2), self.part(half), :],
                self.far_block.at[half],
                5 + half,
                self.neighbour(0, 1 - 2 * half),
            )

    def stage5(self):
        for half in range(2):
            self.arrived(self.far_block.at[half], 5 + half)
            toward = 1 - 2 * half
            for bank in range(self.banks):
                region = self.line.at[bank, around(self.first, toward), self.part(half), :]
                add_into(region, region, self.far_block.at[half, bank])
            self.release(5 + half, self.neighbour(0, -toward))
            self.push(
                lambda toward=toward: self.line.at[:, around(self.first, toward)],
                self.near_block.at[half],
                7 + half,
                self.neighbour(0, toward),
            )

    def own(self, bank):
        return self.line.at[bank, self.first]

    def stage6(self):
        for half in range(2):
            self.arrived(self.near_block.at[half], 7 + half)
        for bank in range(self.banks):
            add_into(
                self.own(bank),
                self.own(bank),
                self.near_block.at[0, bank],
                self.near_block.at[1, bank],
            )
        for half in range(2):
            self.release(7 + half, self.neighbour(0, 2 * half - 1))
        if self.by_columns:
            self.push(lambda: self.own(self.xh), self.last.at[0], 9, self.beside)
            self.push(lambda: self.own(1 - self.xh), self.last.at[1], 10, self.across)
            self.push(lambda: self.own(1 - self.xh), self.last.at[2], 11, self.beyond)
        else:

            @pl.when(self.xh == self.core)
            def _():
                self.push(lambda: self.own(0), self.last.at[0], 9, self.beside, False)

            @pl.when(self.xh != self.core)
            def _():
                self.push(lambda: self.own(0), self.last.at[1], 10, self.across, False)
                self.push(lambda: self.own(0), self.last.at[2], 11, self.beyond, False)

    def add_last(self):
        for slot in range(3):
            self.arrived(self.last.at[slot], 9 + slot)
        s, w = self.swapped, self.width
        c = w - s
        own = self.own(self.xh if self.by_columns else 0)
        self.ready[:, self.wide] = own[...].astype(F32) + self.last[2].astype(F32)
        if s:
            there = pl.ds(pl.multiple_of((1 - self.xl) * (c * LANE), LANE), s * LANE)
            self.ready[:, self.theirs] = self.last[0, :, there].astype(F32) + self.last[
                1, :, there
            ].astype(F32)
        if c:
            middle = pl.ds(s * LANE, c * LANE)
            there = pl.ds(pl.multiple_of(self.xl * (s * LANE), LANE), c * LANE)
            self.ready[:, middle] = (
                self.ready[:, middle]
                + self.last[0, :, there].astype(F32)
                + self.last[1, :, there].astype(F32)
            )
        for slot, device in ((9, self.beside), (10, self.across), (11, self.beyond)):
            self.release(slot, device)

    def pieces(self, core_of):
        rows = self.part(core_of)
        if self.name == "qkv":
            return [
                (
                    self.ready.at[rows, pl.ds(third * 512, 512)],
                    self.output.at[:, pl.ds(third * 1024 + self.core * 512, 512)],
                )
                for third in range(3)
            ]
        if self.name == "up":
            return [(self.ready.at[rows, :], self.output.at[:, pl.ds(self.core * 2048, 2048)])]
        return [(self.ready.at[rows, :], self.output)]

    def deliver(self):
        for index, (source, target) in enumerate(self.pieces(self.core)):
            pltpu.make_async_copy(source, target, self.recv.at[self.number, 15 + index]).start()
        for index, (source, target) in enumerate(self.pieces(1 - self.core)):
            self.push(lambda: source, target, 12 + index, self.sibling, False)

    def delivered(self):
        for index, (source, target) in enumerate(self.pieces(self.core)):
            pltpu.make_async_copy(source, target, self.recv.at[self.number, 15 + index]).wait()
        for index, (source, target) in enumerate(self.pieces(1 - self.core)):
            pltpu.make_async_copy(source, source, self.send.at[self.number, 12 + index]).wait()

    def stage7(self):
        if self.name == "small":
            self.add_last()
            self.push(
                lambda: self.ready.at[self.part(1 - self.core), :], self.tail.at[0], 12, self.sibling
            )
        elif self.by_columns:
            self.add_last()
            self.deliver()
        else:

            @pl.when(self.xh == self.core)
            def _():
                self.add_last()
                self.deliver()

    def stage8(self):
        core = self.core
        if self.name == "small":
            self.arrived(self.tail.at[0], 12)
            self.tail[1] = self.ready[self.part(core), :] + self.tail[0]
        elif self.by_columns:
            self.delivered()
            for index, (source, target) in enumerate(self.pieces(1 - core)):
                self.arrived(source, 12 + index)
        else:

            @pl.when(self.xh == core)
            def _():
                self.delivered()

            @pl.when(self.xh != core)
            def _():
                self.arrived(self.output, 12)

        self.settle()
        if not self.by_columns:

            @pl.when(self.xh == core)
            def _():
                own = self.own(0)
                pltpu.make_async_copy(own, own, self.send.at[self.number, 9]).wait()

            @pl.when(self.xh != core)
            def _():
                own = self.own(0)
                pltpu.make_async_copy(own, own, self.send.at[self.number, 10]).wait()
                pltpu.make_async_copy(own, own, self.send.at[self.number, 11]).wait()


QKV, UP, OUT, DOWN, SMALL = range(5)

SCHEDULE = """
start1 low1 gdown1 D1 slope1 gup1 U1 dmixed1 gout1 O1 attentionA1 D1 attentionB1 D1 dhidden1 U1 gqkv1 Q1 D1
late1 norm1 free1 start0 U1 O1 low0 D1 gdown0 D1 D0 U1 O1 slope0 Q1 gup0 U0 D1 O1 U1 dmixed0 gout0 O0
Q1 U1 O1 D1 attentionA0 Q1 D0 U1 O1 attentionB0 U1 O1 Q1 D0 U0 gqkv0 Q0 Q1 O1 O0 dhidden0 Q1 D0 U0
norm0 pack1 pack0 S0
""".split()


def whole_schedule():
    steps = list(SCHEDULE)
    stages = {}
    for step in steps:
        if step[0].isupper():
            stages[step] = stages.get(step, 0) + 1
    while any(stage < 8 for stage in stages.values()):
        for step in sorted(stages, key=lambda step: -stages[step]):
            if stages[step] < 8:
                stages[step] += 1
                steps.append(step)
    return steps


def row_tile(weight, index):
    banks, unused, same, rows, columns = weight.shape
    if rows == 128:
        found = weight[0, index // 2, pl.ds((index % 2) * 2, 2)]
    elif banks == 2:
        found = weight[index // 2, pl.ds((index % 2) * 2, 2)]
    else:
        found = weight[0, pl.ds(index * 2, 2)]
    return found.reshape(TILE, columns)


def store_row_tile(total):
    def store(index, found):
        banks, unused, same, rows, columns = total.shape
        if rows == 128:
            total[0, index // 2, pl.ds((index % 2) * 2, 2)] = found.reshape(2, 128, columns)
        else:
            total[0, pl.ds(index * 2, 2)] = found.reshape(2, 4, 32, columns)

    return store


def store_column_tile(total):
    def store(index, found):
        total[:, :, :, :, columns_of(index)] = found.reshape(2, 4, 4, 32, TILE)

    return store


def backward_kernel(schedule, tokens, x_kept, out_grad, tables, *rest):
    rest = list(rest)

    def take(count):
        found = rest[:count]
        del rest[:count]
        return found

    kept_in = [dict(zip((k[0] for k in KEPT), take(len(KEPT)))) for layer_at in range(LAYERS)]
    weights_in = [take(4) for layer_at in range(LAYERS)]
    in_grad, *large_out = take(5)
    small_out = take(5)
    kept = dict(zip((k[0] for k in KEPT), take(len(KEPT))))
    weights = take(4)
    gains = [kept["gain"], *take(1)]
    x_late, dy = take(2)
    dy_low = take(2)
    d_mixed, d_hidden = take(2)
    received = take(2)
    grads = [dict(zip(KINDS, take(5))) for layer_at in range(LAYERS)]
    small_rows, = take(1)
    totals = take(5)
    landing = [take(BUFFERS) for spec in SUMMED]
    send, recv, free, pair_send, pair_recv, moved = take(6)

    xl, xh, z, y, c = place()
    meet(neighbours())
    pair = Pair(pair_send, pair_recv)
    moves = Moves(moved)
    own, other = pl.ds(0, COUNT), pl.ds(COUNT, COUNT)

    sums = {}
    for core in range(2):
        number = 0
        for layer_at in (1, 0):
            for which in (QKV, UP, OUT, DOWN):
                sums[core, layer_at, which] = Sum(
                    number, which, layer_at == 0, totals[which], landing[which],
                    large_out[which].at[layer_at], send, recv, free, (xl, xh, z, y), core,
                )
                number += 1
        sums[core, 0, SMALL] = Sum(
            number, SMALL, False, totals[SMALL], landing[SMALL], None, send, recv, free,
            (xl, xh, z, y), core,
        )
    stage_of = {}

    def advance(layer_at, which):
        stage = stage_of[layer_at, which] = stage_of.get((layer_at, which), 0) + 1
        for core in range(2):

            @pl.when(c == core)
            def _():
                getattr(sums[core, layer_at, which], f"stage{stage}")()

    loads = {}

    def load(layer_at, name):
        if name in ("qkv", "up", "out", "down"):
            which = ("qkv", "up", "out", "down").index(name)
            loads[layer_at, name] = moves.start(weights_in[layer_at][which], weights[which])
        else:
            target = gains[layer_at] if name == "gain" else kept[name]
            loads[layer_at, name] = moves.start(kept_in[layer_at][name], target)

    def need(layer_at, *names):
        for name in names:
            if (layer_at, name) in loads:
                moves.finish(loads.pop((layer_at, name)))

    def used(layer_at, *names):
        if layer_at:
            for name in names:
                load(layer_at - 1, name)

    def start(layer_at):
        start_piece(dy, dy_low[layer_at], grads[layer_at]["out_bias"])
        pair.push(dy_low[layer_at].at[own], dy_low[layer_at].at[other], 2 * layer_at)

    def low_arrived(layer_at):
        pair.wait(dy_low[layer_at].at[own], dy_low[layer_at].at[other], 2 * layer_at)

    def gdown(layer_at):
        need(layer_at, "active")
        rows_grad_piece(8, kept["active"], dy_low[layer_at], store_row_tile(totals[DOWN]))
        used(layer_at, "active")

    def slope(layer_at):
        need(layer_at, "down", "slope")
        slope_piece(
            dy_low[layer_at], lambda n: row_tile(weights[DOWN], n), kept["slope"], kept["slope"],
            grads[layer_at]["b_up"],
        )
        used(layer_at, "down")

    def gup(layer_at):
        need(layer_at, "flipped")
        columns_grad_piece(8, kept["flipped"], kept["slope"], store_column_tile(totals[UP]))

    def dmixed(layer_at):
        need(layer_at, "out")
        d_mixed_piece(dy_low[layer_at], lambda n: row_tile(weights[OUT], n), d_mixed)
        used(layer_at, "out")

    def gout(layer_at):
        need(layer_at, "mixed")
        rows_grad_piece(2, kept["mixed"], dy_low[layer_at], store_row_tile(totals[OUT]))
        used(layer_at, "mixed")

    def attention(layer_at, first, stop):
        need(layer_at, "turned", "probs")
        attention_back_piece(
            kept["turned"], kept["probs"], d_mixed, tables, kept["turned"], grads[layer_at]["b_qkv"], first, stop
        )
        if stop == 8:
            used(layer_at, "probs")

    def dhidden(layer_at):
        need(layer_at, "qkv", "up")
        if layer_at == 0:
            pltpu.make_async_copy(
                d_hidden.at[other], d_hidden.at[other], pair_send.at[3]
            ).wait()
        d_hidden_piece(
            kept["turned"], lambda n: row_tile(weights[QKV], n), kept["slope"],
            lambda n: row_tile(weights[UP], n), d_hidden,
        )
        pair.push(d_hidden.at[other], received[layer_at], 2 * layer_at + 1)
        used(layer_at, "qkv", "up")

    def gqkv(layer_at):
        columns_grad_piece(6, kept["flipped"], kept["turned"], store_column_tile(totals[QKV]))

    def norm(layer_at):
        need(layer_at, "gain")
        target = received[layer_at]
        pltpu.make_async_copy(target, target, pair_recv.at[2 * layer_at + 1]).wait()
        norm_back_piece(
            x_late if layer_at else tokens, gains[layer_at], dy, d_hidden, target, dy,
            grads[layer_at]["gain"], grads[layer_at]["shift"],
        )
        if layer_at == 0:
            moves.start(dy, in_grad)

    def pack(layer_at):
        for core in range(2):

            @pl.when(c == core)
            def _():
                for kind in KINDS:
                    pack_vector(small_rows, layer_at, kind, core, grads[layer_at][kind])

        if layer_at == 0:
            totals[SMALL][...] = small_rows[...].reshape(totals[SMALL].shape)

    for name in ("active", "down", "slope", "flipped", "out", "mixed", "turned", "probs", "qkv", "up", "gain"):
        load(1, name)
    load(0, "gain")
    late = moves.start(x_kept, x_late)
    small_rows[...] = jnp.zeros_like(small_rows)
    dy[...] = out_grad[...].astype(F32)
    steps = {
        "start": start, "low": low_arrived, "gdown": gdown, "slope": slope, "gup": gup,
        "dmixed": dmixed, "gout": gout, "dhidden": dhidden, "gqkv": gqkv, "norm": norm, "pack": pack,
        "attention": lambda layer_at: attention(layer_at, 0, 8),
        "attentionA": lambda layer_at: attention(layer_at, 0, 4),
        "attentionB": lambda layer_at: attention(layer_at, 4, 8),
    }
    streams = {"Q": QKV, "U": UP, "O": OUT, "D": DOWN, "S": SMALL}
    for step in schedule:
        name, layer_at = step[:-1], int(step[-1])
        if name == "free":
            used(layer_at, "slope", "flipped", "turned")
        elif name == "late":
            moves.finish(late)
        elif name in streams:
            advance(layer_at, streams[name])
        else:
            steps[name](layer_at)
    pltpu.make_async_copy(d_hidden.at[other], d_hidden.at[other], pair_send.at[1]).wait()
    tail = landing[SMALL][8]
    for layer_at in range(LAYERS):
        for (kind, (row, size, factor, shift)), target in zip(KINDS.items(), small_out):
            at_row = 5 * layer_at + row
            target[layer_at : layer_at + 1, :] = tail[1, at_row : at_row + 1, :size]
    for copy in list(moves.open):
        copy.wait()


def backward_call(tokens, x_kept, out_grad, tables, kept, weights):
    vmem, hbm = pl.BlockSpec(memory_space=pltpu.VMEM), pl.BlockSpec(memory_space=pltpu.HBM)
    shape = jax.ShapeDtypeStruct
    flat = []
    for layer_at in range(LAYERS):
        flat += list(kept[layer_at])
    for layer_at in range(LAYERS):
        flat += list(weights[layer_at])
    scratch = [pltpu.VMEM(dims, kind) for name, dims, kind in KEPT]
    scratch += [pltpu.VMEM(weight_shape(spec), BF16) for spec in WEIGHTS]
    scratch += [
        pltpu.VMEM((1, D), F32),
        pltpu.VMEM((COUNT, D), F32),
        pltpu.VMEM((COUNT, D), F32),
        pltpu.VMEM((BOTH, D), BF16),
        pltpu.VMEM((BOTH, D), BF16),
        pltpu.VMEM((BOTH, 512), BF16),
        pltpu.VMEM((BOTH, D), F32),
        pltpu.VMEM((COUNT, D), F32),
        pltpu.VMEM((COUNT, D), F32),
    ]
    scratch += [pltpu.VMEM((1, n), F32) for n in (1536, 2048, D, D, D) * LAYERS]
    scratch += [pltpu.VMEM((64 * OWNED_ROWS, LANE), F32)]
    for spec in SUMMED:
        scratch.append(pltpu.VMEM(total_shape(spec), F32 if spec[0] == "small" else BF16))
    for spec in SUMMED:
        scratch += landing_shapes(spec)
    scratch += [
        pltpu.SemaphoreType.DMA((1 + 4 * LAYERS, SUM_SLOTS)),
        pltpu.SemaphoreType.DMA((1 + 4 * LAYERS, SUM_SLOTS)),
        pltpu.SemaphoreType.REGULAR((4, 12)),
        pltpu.SemaphoreType.DMA((4,)),
        pltpu.SemaphoreType.DMA((4,)),
        pltpu.SemaphoreType.DMA((40,)),
    ]
    return pl.pallas_call(
        functools.partial(backward_kernel, whole_schedule()),
        out_shape=[
            shape((COUNT, D), F32),
            shape((LAYERS, 16, 3072), F32),
            shape((LAYERS, 16, 4096), F32),
            shape((LAYERS, 16, 1024), F32),
            shape((LAYERS, 64, 1024), F32),
        ]
        + [shape((LAYERS, size), F32) for row, size, factor, shift in KINDS.values()],
        in_specs=[vmem, hbm, vmem, vmem] + [hbm] * len(flat),
        out_specs=[hbm] * 5 + [vmem] * 5,
        scratch_shapes=scratch,
        name="backward",
        compiler_params=pltpu.CompilerParams(
            collective_id=1, has_side_effects=True, vmem_limit_bytes=63 * 2**20
        ),
    )(tokens, x_kept, out_grad, tables, *flat)


def on_device(
    tokens, w_qkv, b_qkv, w_out, w_up, b_up, w_down, ln_gain, ln_bias, out_bias, out_grad
):
    tables = jnp.asarray(turn_tables())
    found = forward_call(
        tokens, b_qkv, b_up, ln_gain, ln_bias, out_bias, tables, w_qkv, w_up, w_out, w_down
    )
    current, x_kept = found[:2]
    weights = [found[2 + 4 * layer_at : 6 + 4 * layer_at] for layer_at in range(LAYERS)]
    first = 2 + 4 * LAYERS
    kept = [
        found[first + len(KEPT) * layer_at : first + len(KEPT) * (layer_at + 1)]
        for layer_at in range(LAYERS)
    ]
    upstream, g_qkv, g_up, g_out, g_down, *small = backward_call(
        tokens, x_kept, out_grad, tables, kept, weights
    )
    g_b_qkv, g_b_up, g_gain, g_shift, g_out_bias = small
    return (
        current,
        upstream,
        g_qkv,
        g_b_qkv,
        g_out,
        g_up,
        g_b_up,
        g_down,
        g_gain,
        g_shift,
        g_out_bias,
    )


def solution(mesh):
    placed = (
        P(("rep", "shard"), None),
        P(None, "shard", None),
        P(None, "shard"),
        P(None, "shard", None),
        P(None, "shard", None),
        P(None, "shard"),
        P(None, "shard", None),
        P(None, "shard"),
        P(None, "shard"),
        P(None, "shard"),
        P(("rep", "shard"), None),
    )
    return jax.shard_map(
        on_device,
        mesh=mesh,
        in_specs=placed,
        out_specs=(
            P(("rep", "shard"), None),
            P(("rep", "shard"), None),
            P(None, "shard", None),
            P(None, "shard"),
            P(None, "shard", None),
            P(None, "shard", None),
            P(None, "shard"),
            P(None, "shard", None),
            P(None, "shard"),
            P(None, "shard"),
            P(None, "shard"),
        ),
        check_vma=False,
    )
```

time: 3210 us -> 321 us (0.10)
  waiting for transfers between devices: 2240 us -> 0 us
  blocking collectives: 647 us -> 0 us
  Pallas kernels: 0 us -> 311 us
  matrix products: 183 us -> 0 us
  other arithmetic: 54.8 us -> 0 us
  local copies, waits for them, and re-layouts: 49.6 us -> 9 us
    reduce_scatter x8 -> x0, waiting for transfers between devices: 2000 us -> none  [the longest x2 711 us: reduce_layer(): lax.psum_scatter(full[5], 'shard', scatter_dimension=0, tiled=True)]
    unnamed x2 -> x0, blocking collectives: 647 us -> none
    pallas_call x0 -> x2, Pallas kernels: none -> 311 us  [the longest x1 168 us: backward_call(): pl.pallas_call(functools.partial(backward_kernel, whole_schedule()), out_...]
    dot_general x36 -> x0, matrix products: 183 us -> none  [the longest x8 57.4 us: contract_rows(): lax.dot_general(left, right, (((0,), (0,)), ((), ())), preferred_element_...]
    all_gather x8 -> x0, waiting for transfers between devices: 170 us -> none  [the longest x2 67.8 us: fetch_forward(): lax.all_gather(stacks[5][layer_at], 'shard', axis=0, tiled=True)]
    psum x2 -> x0, waiting for transfers between devices: 68.2 us -> none  [the longest x1 37.7 us: reduce_layer(): lax.psum(pieces[0].astype(jnp.bfloat16), 'rep').astype(jnp.float32)]
  transfers between devices with their start and end apart: 18 -> 0, of which waited for: 12 -> 0; matrix products, arithmetic and copies ran while one was open for 9% -> 0% of each run, Pallas kernels for 0% -> 0%
where the time goes in v3:
time: 321 us
  Pallas kernels  311 us (97%)
  local copies, waits for them, and re-layouts  9 us (3%)
    pallas_call x1, Pallas kernels, backward_call(): pl.pallas_call(functools.partial(backward_kernel, whole_schedule()), out_...  168 us
    pallas_call x1, Pallas kernels, forward_call(): pl.pallas_call(forward_kernel, out_shape=outs, in_specs=[vmem] * 7 + [hbm...  144 us
    unnamed x31, local copies, waits for them, and re-layouts  9 us

profile of v3, /device:TPU:1, one launch (start us, length us, event | category | flops | bytes accessed | tf_op | source)
XLA Modules:
  0.0 321.0 jit_solution(11216424639874021705)
XLA Ops:
  0.6 143.7 %forward.1 = (bf16[256,1024]{1,0:T(8,128)(2,1)}, f32[256,1024]{1,0:T(8,128)}, bf16[2,4,4,32,1536]{4,3,2,1,0:T(8,128)(2,1)}, bf16[2,4,4,32,2048]{4,3,2,1,0:T(8,12...) custom-call(bf16[256,1024]{1,0:T(8,128)(2,1)} %tokens.3, ...), custom_call_target="tpu_custom_call" | custom-call | tf_op jit(solution)/shard_map/forward/pallas_call | solution.py:883
  144.4 0.0 copy-start.2
  144.4 167.6 %backward.1 = (f32[256,1024]{1,0:T(8,128)}, f32[2,16,3072]{2,1,0:T(8,128)}, f32[2,16,4096]{2,1,0:T(8,128)}, f32[2,16,1024]{2,1,0:T(8,128)}, f32[2,64,1024]{2,1,0...) custom-call(bf16[256,1024]{1,0:T(8,128)(2,1)} %tokens.3, ...), custom_call_target="tpu_custom_call" | custom-call | tf_op jit(solution)/shard_map/backward/pallas_call | solution.py:1518
  312.0 0.0 copy-start.3
  312.0 0.0 copy-start.9
  312.0 0.0 copy-start.4
  312.0 0.0 copy-done.2
  312.0 0.0 copy-start.1
  312.0 0.8 copy.34
  312.8 0.0 copy-start.8
  312.8 0.0 copy-start
  312.8 2.4 copy.35
  315.2 0.0 copy-done.3
  315.2 0.0 copy-start.7
  315.2 0.0 copy-start.6
  315.2 0.0 copy-start.5
  315.2 0.7 copy.36
  315.9 0.0 copy-done.9
  315.9 0.6 copy.37
  316.5 0.0 copy-done.4
  316.5 0.7 copy.38
  317.2 0.0 copy-done.1
  317.2 0.8 copy.39
  318.0 0.0 copy-done.8
  318.0 0.6 copy.40
  318.5 0.0 copy-done
  318.5 0.8 copy.41
  319.3 0.0 copy-done.7
  319.3 0.6 copy.42
  319.9 0.0 copy-done.6
  319.9 0.6 copy.43
  320.5 0.0 copy-done.5
  320.5 0.6 copy.44
Async XLA Ops:
  144.4 167.6 %copy-start.2 = (bf16[256,1024]{1,0:T(8,128)(2,1)S(1)}, bf16[256,1024]{1,0:T(8,128)(2,1)}, u32[]{:S(2)}) copy-start(bf16[256,1024]{1,0:T(8,128)(2,1)} %get-tuple-element.90) | copy-start | bytes 1572868
  312.0 3.2 %copy-start.3 = (f32[2,16,3072]{2,1,0:T(8,128)S(1)}, f32[2,16,3072]{2,1,0:T(8,128)}, u32[]{:S(2)}) copy-start(f32[2,16,3072]{2,1,0:T(8,128)} %get-tuple-element.92) | copy-start | bytes 1179652
  312.0 4.0 %copy-start.9 = (f32[2,48]{1,0:T(2,128)S(1)}, f32[2,48]{1,0:T(2,128)}, u32[]{:S(2)}) copy-start(f32[2,48]{1,0:T(2,128)} %get-tuple-element.93) | copy-start | bytes 1156
  312.0 4.5 %copy-start.4 = (f32[2,16,1024]{2,1,0:T(8,128)S(1)}, f32[2,16,1024]{2,1,0:T(8,128)}, u32[]{:S(2)}) copy-start(f32[2,16,1024]{2,1,0:T(8,128)} %get-tuple-element.94) | copy-start | bytes 393220
  312.0 5.2 %copy-start.1 = (f32[2,16,4096]{2,1,0:T(8,128)S(1)}, f32[2,16,4096]{2,1,0:T(8,128)}, u32[]{:S(2)}) copy-start(f32[2,16,4096]{2,1,0:T(8,128)} %get-tuple-element.95) | copy-start | bytes 1572868
  312.8 5.2 %copy-start.8 = (f32[2,64]{1,0:T(2,128)S(1)}, f32[2,64]{1,0:T(2,128)}, u32[]{:S(2)}) copy-start(f32[2,64]{1,0:T(2,128)} %get-tuple-element.96) | copy-start | bytes 1540
  312.8 5.7 %copy-start = (f32[2,64,1024]{2,1,0:T(8,128)S(1)}, f32[2,64,1024]{2,1,0:T(8,128)}, u32[]{:S(2)}) copy-start(f32[2,64,1024]{2,1,0:T(8,128)} %get-tuple-element.97) | copy-start | bytes 1572868
  315.2 4.1 %copy-start.7 = (f32[2,16]{1,0:T(2,128)S(1)}, f32[2,16]{1,0:T(2,128)}, u32[]{:S(2)}) copy-start(f32[2,16]{1,0:T(2,128)} %get-tuple-element.98) | copy-start | bytes 388
  315.2 4.7 %copy-start.6 = (f32[2,16]{1,0:T(2,128)S(1)}, f32[2,16]{1,0:T(2,128)}, u32[]{:S(2)}) copy-start(f32[2,16]{1,0:T(2,128)} %get-tuple-element.99) | copy-start | bytes 388
  315.2 5.3 %copy-start.5 = (f32[2,16]{1,0:T(2,128)S(1)}, f32[2,16]{1,0:T(2,128)}, u32[]{:S(2)}) copy-start(f32[2,16]{1,0:T(2,128)} %get-tuple-element.100) | copy-start | bytes 388

commit v4 on v3

--- a/solution.py
+++ b/solution.py
@@ -8,6 +8,32 @@
 from jax.experimental import pallas as pl
 from jax.experimental.pallas import tpu as pltpu
 from jax.sharding import PartitionSpec as P
+
+
+STEP_NAMES = (
+    "s", "q", "u", "o", "d", "Q", "U", "O", "D", "S", "vec", "fnorm", "joined", "fattnA",
+    "fattnB", "up", "down", "res", "start", "low", "gdown", "slope", "gup", "dmixed", "gout",
+    "battnA", "battnB", "dhidden", "gqkv", "norm", "pack",
+)
+(
+    s0, s1, q0, q1, u0, u1, o0, o1, d0, d1, Q0, Q1, U0, U1, O0, O1, D0, D1, S0, S1, vec0, vec1,
+    fnorm0, fnorm1, joined0, joined1, fattnA0, fattnA1, fattnB0, fattnB1, up0, up1, down0, down1,
+    res0, res1, start0, start1, low0, low1, gdown0, gdown1, slope0, slope1, gup0, gup1, dmixed0,
+    dmixed1, gout0, gout1, battnA0, battnA1, battnB0, battnB1, dhidden0, dhidden1, gqkv0, gqkv1,
+    norm0, norm1, pack0, pack1,
+) = range(2 * len(STEP_NAMES))
+SCHEDULE = (
+    s0, o0, q0, o1, s0, o0, u0, s0, q0, o1, o0, d0, s0, u1, q1, q0, u0, s0, o1, q0, d1, d0, d0,
+    u0, q1, q0, d0, s0, s0, vec0, q1, fnorm0, q0, o0, u0, d0, o0, q0, joined0, u0, fattnA0, o0,
+    q1, d1, u1, o1, u0, d0, fattnB0, u1, o0, u0, q1, u1, d0, up0, q1, down0, d1, o1, u1, q1, res0,
+    fnorm1, o1, d1, joined1, start1, u1, fattnA1, o1, d1, fattnB1, u1, low1, dmixed1, battnA1, d1,
+    gout1, up1, O1, gdown1, D1, d1, battnB1, slope1, O1, gup1, U1, O1, D1, down1, gqkv1, D1, Q1,
+    res1, dhidden1, U1, O1, norm1, start0, low0, O1, Q1, gout0, D1, dmixed0, O0, U1, gdown0, D0,
+    D1, Q1, battnA0, O0, slope0, D1, U1, gup0, U0, D0, U1, O0, battnB0, Q1, D0, gqkv0, Q0, U0, D1,
+    dhidden0, Q1, D1, D0, Q0, U1, pack1, O1, U0, norm0, pack0, U1, U1, S0, Q1, Q0, D0, O1, U0, O1,
+    Q1, S0, U0, D0, O0, Q1, Q0, S0, U0, O0, Q0, S0, O0, S0, Q0, D0, O0, U0, S0, Q0, D0, S0, Q0,
+    O0, U0, S0,
+)
 
 
 MESH = pl.DeviceIdType.MESH
@@ -231,6 +257,7 @@
     def finish(self):
         for region, slot in self.sent:
             pltpu.make_async_copy(region(), region(), self.send.at[self.number, slot]).wait()
+        self.sent = []
         if not self.by_columns:
 
             @pl.when(self.xh != self.core)
@@ -390,7 +417,7 @@
 def norm_piece(x_ref, gain, shift, hidden):
     def body(index):
         rows = columns_of(index, 64)
-        normed, unused = centre(x_ref[rows, :])
+        normed, unused = centre(x_ref[rows, :].astype(F32))
         hidden[rows, :] = (normed * gain[...] + shift[...]).astype(BF16)
 
     loop(COUNT // 64, body)
@@ -468,7 +495,9 @@
     def body(index):
         rows = columns_of(index, 64)
         target[rows, :] = (
-            x_ref[rows, :] + (partial[rows, :] + received[rows, :]) + out_bias[...]
+            x_ref[rows, :].astype(F32)
+            + (partial[rows, :] + received[rows, :])
+            + out_bias[...]
         ).astype(target.dtype)
 
     loop(COUNT // 64, body)
@@ -590,309 +619,6 @@
     loop(COUNT // 64, body)
 
 
-class Pair:
-    def __init__(self, send, recv):
-        xl, xh, z, y, c = place()
-        self.device = at(xl, xh, z, y, 1 - c)
-        self.send, self.recv = send, recv
-
-    def push(self, source, target, slot):
-        pltpu.make_async_remote_copy(
-            source,
-            target,
-            self.send.at[slot],
-            self.recv.at[slot],
-            device_id=self.device,
-            device_id_type=MESH,
-        ).start()
-
-    def wait(self, source, target, slot):
-        pltpu.make_async_copy(source, source, self.send.at[slot]).wait()
-        pltpu.make_async_copy(target, target, self.recv.at[slot]).wait()
-
-
-class Moves:
-    def __init__(self, done):
-        self.done = done
-        self.count = 0
-        self.open = []
-
-    def start(self, source, target):
-        copy = pltpu.make_async_copy(source, target, self.done.at[self.count])
-        self.count += 1
-        copy.start()
-        self.open.append(copy)
-        return copy
-
-    def finish(self, copy):
-        copy.wait()
-        self.open = [other for other in self.open if other is not copy]
-
-
-KEPT = (
-    ("flipped", (D, BOTH), BF16),
-    ("turned", (BOTH, 1536), BF16),
-    ("probs", (16, COUNT, COUNT), BF16),
-    ("mixed", (BOTH, 512), BF16),
-    ("active", (BOTH, 2048), BF16),
-    ("slope", (BOTH, 2048), BF16),
-    ("gain", (1, D), F32),
-)
-WEIGHTS = GATHERED[1:]
-
-
-def weight_shape(spec):
-    name, by_columns, rows, columns, swapped, width = spec
-    return (2 if by_columns else 1, 4, 4, rows, columns)
-
-
-def all_rows(weight, columns):
-    found = weight[:, :, :, :, columns]
-    return found.reshape(-1, found.shape[-1])
-
-
-def forward_kernel(tokens, b_qkv, b_up, ln_gain, ln_bias, out_bias, tables, qkv, up, out, down, *rest):
-    rest = list(rest)
-
-    def take(count):
-        found = rest[:count]
-        del rest[:count]
-        return found
-
-    (result, x_kept) = take(2)
-    gathered = [take(4) for layer_at in range(LAYERS)]
-    kept_out = [dict(zip((k[0] for k in KEPT), take(len(KEPT)))) for layer_at in range(LAYERS)]
-    kept = [dict(zip((k[0] for k in KEPT), take(len(KEPT)))) for layer_at in range(LAYERS)]
-    weights = [take(4) for layer_at in range(LAYERS)]
-    vectors = [dict(zip(("b_qkv", "b_up", "shift", "out_bias"), take(4))) for layer_at in range(LAYERS)]
-    owned, every, rows, x0, x1, last = take(6)
-    hidden = take(2)
-    partial, = take(1)
-    received = take(2)
-    send, recv, pair_send, pair_recv, moved = take(5)
-
-    owned[...] = jnp.zeros_like(owned)
-    for layer_at in range(LAYERS):
-        for row, vector in enumerate((b_qkv, b_up, ln_gain, ln_bias, out_bias)):
-            owned[5 * layer_at + row : 5 * layer_at + row + 1, : vector.shape[1]] = vector[
-                layer_at : layer_at + 1, :
-            ].astype(F32)
-    xl, xh, z, y, c = place()
-    meet(neighbours())
-    pair = Pair(pair_send, pair_recv)
-    moves = Moves(moved)
-
-    streams = []
-    for core in range(2):
-        found = [
-            Stream(0, GATHERED[0], owned_pieces("small", owned, 0), every, send, recv, xl, xh, z, y, core)
-        ]
-        for layer_at in range(LAYERS):
-            for spec, source, target in zip(WEIGHTS, (qkv, up, out, down), gathered[layer_at]):
-                found.append(
-                    Stream(
-                        len(found), spec, owned_pieces(spec[0], source, layer_at), target,
-                        send, recv, xl, xh, z, y, core,
-                    )
-                )
-        streams.append(found)
-    count = len(streams[0])
-
-    def tick(time):
-        for core in range(2):
-
-            @pl.when(c == core)
-            def _():
-                for stage in range(7):
-                    if 0 <= time - stage < count:
-                        getattr(streams[core][time - stage], f"stage{stage}")()
-
-    loads = {}
-
-    def load(layer_at, which):
-        loads[layer_at, which] = moves.start(gathered[layer_at][which], weights[layer_at][which])
-
-    def loaded(layer_at, which):
-        moves.finish(loads[layer_at, which])
-
-    def keep(layer_at, name):
-        moves.start(kept[layer_at][name], kept_out[layer_at][name])
-
-    own, other = pl.ds(0, COUNT), pl.ds(COUNT, COUNT)
-    inputs = (x0, x1)
-
-    def vectors_step():
-        rows[...] = every[...].reshape(rows.shape)
-        for core in range(2):
-
-            @pl.when(c == core)
-            def _():
-                for layer_at in range(LAYERS):
-                    for kind in KINDS:
-                        target = kept[layer_at]["gain"] if kind == "gain" else vectors[layer_at][kind]
-                        unpack_vector(rows, layer_at, kind, core, target)
-
-        for layer_at in range(LAYERS):
-            keep(layer_at, "gain")
-
-    def norm_step(layer_at):
-        norm_piece(inputs[layer_at], kept[layer_at]["gain"], vectors[layer_at]["shift"], hidden[layer_at])
-        pair.push(hidden[layer_at].at[own], hidden[layer_at].at[other], 2 * layer_at)
-
-    def joined_step(layer_at):
-        pair.wait(hidden[layer_at].at[own], hidden[layer_at].at[other], 2 * layer_at)
-        loaded(layer_at, 0)
-        for third in range(3):
-            joined_piece(
-                third,
-                hidden[layer_at],
-                lambda n: all_rows(weights[layer_at][0], n),
-                vectors[layer_at]["b_qkv"],
-                tables,
-                kept[layer_at]["turned"],
-            )
-        keep(layer_at, "turned")
-        flip_piece(hidden[layer_at], kept[layer_at]["flipped"])
-        keep(layer_at, "flipped")
-
-    def attention_step(layer_at, start, stop):
-        attention_piece(
-            kept[layer_at]["turned"], kept[layer_at]["probs"], kept[layer_at]["mixed"], start, stop
-        )
-        if stop == 8:
-            keep(layer_at, "probs")
-            keep(layer_at, "mixed")
-
-    def up_step(layer_at):
-        loaded(layer_at, 1)
-        up_piece(
-            hidden[layer_at],
-            lambda n: all_rows(weights[layer_at][1], n),
-            vectors[layer_at]["b_up"],
-            kept[layer_at]["active"],
-            kept[layer_at]["slope"],
-        )
-        keep(layer_at, "active")
-        keep(layer_at, "slope")
-
-    def down_step(layer_at):
-        loaded(layer_at, 2)
-        loaded(layer_at, 3)
-        if layer_at:
-            pltpu.make_async_copy(partial.at[other], partial.at[other], pair_send.at[1]).wait()
-        down_piece(
-            kept[layer_at]["active"],
-            lambda n: all_rows(weights[layer_at][3], n),
-            kept[layer_at]["mixed"],
-            lambda n: all_rows(weights[layer_at][2], n),
-            partial,
-        )
-        pair.push(partial.at[other], received[layer_at], 2 * layer_at + 1)
-
-    def residual_step(layer_at):
-        target = received[layer_at]
-        pltpu.make_async_copy(target, target, pair_recv.at[2 * layer_at + 1]).wait()
-        residual_piece(
-            inputs[layer_at],
-            partial,
-            target,
-            vectors[layer_at]["out_bias"],
-            x1 if layer_at == 0 else last,
-        )
-        if layer_at == 0:
-            moves.start(x1, x_kept)
-        else:
-            pltpu.make_async_copy(partial.at[other], partial.at[other], pair_send.at[3]).wait()
-            moves.start(last, result)
-
-    x0[...] = tokens[...].astype(F32)
-    for time in range(7):
-        tick(time)
-    vectors_step()
-    norm_step(0)
-    tick(7)
-    load(0, 0)
-    tick(8)
-    load(0, 1)
-    joined_step(0)
-    tick(9)
-    load(0, 2)
-    attention_step(0, 0, 8)
-    tick(10)
-    load(0, 3)
-    up_step(0)
-    tick(11)
-    load(1, 0)
-    down_step(0)
-    tick(12)
-    load(1, 1)
-    residual_step(0)
-    norm_step(1)
-    joined_step(1)
-    tick(13)
-    load(1, 2)
-    attention_step(1, 0, 8)
-    tick(14)
-    load(1, 3)
-    up_step(1)
-    down_step(1)
-    for core in range(2):
-
-        @pl.when(c == core)
-        def _():
-            for stream in streams[core]:
-                stream.finish()
-
-    residual_step(1)
-    for copy in list(moves.open):
-        copy.wait()
-
-
-def forward_call(tokens, b_qkv, b_up, ln_gain, ln_bias, out_bias, tables, qkv, up, out, down):
-    vmem, hbm = pl.BlockSpec(memory_space=pltpu.VMEM), pl.BlockSpec(memory_space=pltpu.HBM)
-    shape = jax.ShapeDtypeStruct
-    outs = [shape((COUNT, D), BF16), shape((COUNT, D), F32)]
-    scratch = []
-    for layer_at in range(LAYERS):
-        outs += [shape(weight_shape(spec), BF16) for spec in WEIGHTS]
-    for layer_at in range(LAYERS):
-        outs += [shape(dims, kind) for name, dims, kind in KEPT]
-        scratch += [pltpu.VMEM(dims, kind) for name, dims, kind in KEPT]
-    for layer_at in range(LAYERS):
-        scratch += [pltpu.VMEM(weight_shape(spec), BF16) for spec in WEIGHTS]
-    for layer_at in range(LAYERS):
-        scratch += [pltpu.VMEM((1, n), F32) for n in (1536, 2048, D, D)]
-    scratch += [
-        pltpu.VMEM((OWNED_ROWS, LANE), F32),
-        pltpu.VMEM((2, 4, 4, 2 * OWNED_ROWS, LANE), F32),
-        pltpu.VMEM((64 * OWNED_ROWS, LANE), F32),
-        pltpu.VMEM((COUNT, D), F32),
-        pltpu.VMEM((COUNT, D), F32),
-        pltpu.VMEM((COUNT, D), BF16),
-        pltpu.VMEM((BOTH, D), BF16),
-        pltpu.VMEM((BOTH, D), BF16),
-        pltpu.VMEM((BOTH, D), F32),
-        pltpu.VMEM((COUNT, D), F32),
-        pltpu.VMEM((COUNT, D), F32),
-        pltpu.SemaphoreType.DMA((1 + 4 * LAYERS, SLOTS)),
-        pltpu.SemaphoreType.DMA((1 + 4 * LAYERS, SLOTS)),
-        pltpu.SemaphoreType.DMA((4,)),
-        pltpu.SemaphoreType.DMA((4,)),
-        pltpu.SemaphoreType.DMA((40,)),
-    ]
-    return pl.pallas_call(
-        forward_kernel,
-        out_shape=outs,
-        in_specs=[vmem] * 7 + [hbm] * 4,
-        out_specs=[hbm] * len(outs),
-        scratch_shapes=scratch,
-        name="forward",
-        compiler_params=pltpu.CompilerParams(
-            collective_id=0, has_side_effects=True, vmem_limit_bytes=60 * 2**20
-        ),
-    )(tokens, b_qkv, b_up, ln_gain, ln_bias, out_bias, tables, qkv, up, out, down)
-
-
 SUMMED = (
     ("qkv", True, 32, 1536, 3, 9),
     ("up", True, 32, 2048, 4, 12),
@@ -935,6 +661,9 @@
         for other in others:
             found = found + other[...].astype(F32)
         target[...] = found.astype(target.dtype)
+
+
+sum_loop = loop
 
 
 class Sum:
@@ -1033,7 +762,7 @@
                 region = self.total.at[bank, z, y, :, self.mine]
                 add_into(region, region, self.swap.at[bank, z, y])
 
-            loop(self.banks * 16, add)
+            sum_loop(self.banks * 16, add)
             self.release(0, self.partner)
         for half in range(2):
             self.push(
@@ -1058,7 +787,7 @@
                 ]
                 add_into(region, region, self.far_line.at[half, bank, place_at])
 
-            loop(self.banks * 4, add)
+            sum_loop(self.banks * 4, add)
             self.release(1 + half, self.neighbour(1, -toward))
             self.push(
                 lambda toward=toward: self.total_line(
@@ -1082,7 +811,7 @@
                 self.near_line.at[1, bank, place_at],
             )
 
-        loop(self.banks * 4, add)
+        sum_loop(self.banks * 4, add)
         for half in range(2):
             self.release(3 + half, self.neighbour(1, 2 * half - 1))
         self.settle()
@@ -1239,27 +968,107 @@
 
 
 QKV, UP, OUT, DOWN, SMALL = range(5)
-
-SCHEDULE = """
-start1 low1 gdown1 D1 slope1 gup1 U1 dmixed1 gout1 O1 attentionA1 D1 attentionB1 D1 dhidden1 U1 gqkv1 Q1 D1
-late1 norm1 free1 start0 U1 O1 low0 D1 gdown0 D1 D0 U1 O1 slope0 Q1 gup0 U0 D1 O1 U1 dmixed0 gout0 O0
-Q1 U1 O1 D1 attentionA0 Q1 D0 U1 O1 attentionB0 U1 O1 Q1 D0 U0 gqkv0 Q0 Q1 O1 O0 dhidden0 Q1 D0 U0
-norm0 pack1 pack0 S0
-""".split()
-
-
-def whole_schedule():
-    steps = list(SCHEDULE)
-    stages = {}
-    for step in steps:
-        if step[0].isupper():
-            stages[step] = stages.get(step, 0) + 1
-    while any(stage < 8 for stage in stages.values()):
-        for step in sorted(stages, key=lambda step: -stages[step]):
-            if stages[step] < 8:
-                stages[step] += 1
-                steps.append(step)
-    return steps
+WEIGHTS = GATHERED[1:]
+WEIGHT_NAMES = tuple(spec[0] for spec in WEIGHTS)
+
+FLIPPED, TURNED, PROBS, MIXED, ACTIVE = range(5)
+
+KEPT = (
+    (FLIPPED, (D, BOTH), BF16),
+    (TURNED, (BOTH, 1536), BF16),
+    (PROBS, (16, COUNT, COUNT), BF16),
+    (MIXED, (BOTH, 512), BF16),
+    (ACTIVE, (BOTH, 2048), BF16),
+    ("slope", (BOTH, 2048), BF16),
+)
+KEPT_NAMES = tuple(name for name, dims, kind in KEPT)
+
+TOUCHED = {
+    "joined": ("qkv", TURNED, FLIPPED),
+    "fattnA": (TURNED, PROBS, MIXED),
+    "fattnB": (TURNED, PROBS, MIXED),
+    "up": ("up", ACTIVE, "slope"),
+    "down": ("down", "out", ACTIVE, MIXED),
+    "gdown": (ACTIVE,),
+    "slope": ("down", "slope"),
+    "gup": (FLIPPED, "slope"),
+    "dmixed": ("out",),
+    "gout": (MIXED,),
+    "battnA": (TURNED, PROBS),
+    "battnB": (TURNED, PROBS),
+    "dhidden": ("qkv", "up", TURNED, "slope"),
+    "gqkv": (FLIPPED, TURNED),
+}
+FORWARD = ("joined", "fattnA", "fattnB", "up", "down")
+WHOLE_AFTER = {
+    TURNED: "joined",
+    FLIPPED: "joined",
+    PROBS: "fattnB",
+    MIXED: "fattnB",
+    ACTIVE: "up",
+    "slope": "up",
+}
+GATHERS = {"s": 0, "q": 1, "u": 2, "o": 3, "d": 4}
+SUMS = {"Q": QKV, "U": UP, "O": OUT, "D": DOWN, "S": SMALL}
+
+
+class Pair:
+    def __init__(self, send, recv):
+        xl, xh, z, y, c = place()
+        self.device = at(xl, xh, z, y, 1 - c)
+        self.send, self.recv = send, recv
+
+    def push(self, source, target, slot):
+        pltpu.make_async_remote_copy(
+            source,
+            target,
+            self.send.at[slot],
+            self.recv.at[slot],
+            device_id=self.device,
+            device_id_type=MESH,
+        ).start()
+
+    def sent(self, source, slot):
+        pltpu.make_async_copy(source, source, self.send.at[slot]).wait()
+
+    def arrived(self, target, slot):
+        pltpu.make_async_copy(target, target, self.recv.at[slot]).wait()
+
+
+class Moves:
+    def __init__(self, done):
+        self.done = done
+        self.count = 0
+        self.open = []
+
+    def start(self, source, target):
+        copy = pltpu.make_async_copy(source, target, self.done.at[self.count])
+        self.count += 1
+        copy.start()
+        self.open.append(copy)
+        return copy
+
+    def finish(self, copy):
+        if any(other is copy for other in self.open):
+            copy.wait()
+            self.open = [other for other in self.open if other is not copy]
+
+
+EARLY, LATE, LAST, GATHER = range(4)
+
+
+def phase_of(step, layer_at):
+    return LATE if layer_at else (EARLY if step in FORWARD else LAST)
+
+
+def weight_shape(spec):
+    name, by_columns, rows, columns, swapped, width = spec
+    return (2 if by_columns else 1, 4, 4, rows, columns)
+
+
+def all_rows(weight, columns):
+    found = weight[:, :, :, :, columns]
+    return found.reshape(-1, found.shape[-1])
 
 
 def row_tile(weight, index):
@@ -1291,7 +1100,7 @@
     return store
 
 
-def backward_kernel(schedule, tokens, x_kept, out_grad, tables, *rest):
+def blocks_kernel(schedule, tokens, out_grad, b_qkv, b_up, ln_gain, ln_bias, out_bias, tables, *rest):
     rest = list(rest)
 
     def take(count):
@@ -1299,137 +1108,220 @@
         del rest[:count]
         return found
 
-    kept_in = [dict(zip((k[0] for k in KEPT), take(len(KEPT)))) for layer_at in range(LAYERS)]
-    weights_in = [take(4) for layer_at in range(LAYERS)]
-    in_grad, *large_out = take(5)
-    small_out = take(5)
-    kept = dict(zip((k[0] for k in KEPT), take(len(KEPT))))
-    weights = take(4)
-    gains = [kept["gain"], *take(1)]
-    x_late, dy = take(2)
-    dy_low = take(2)
-    d_mixed, d_hidden = take(2)
-    received = take(2)
+    owned_weights = take(4)
+    result, in_grad = take(2)
+    large_out = take(4)
+    gathered = [take(4) for layer_at in range(LAYERS)]
+    spilled = dict(zip(KEPT_NAMES, take(len(KEPT))))
+    (small_out,) = take(1)
+    held = dict(zip(KEPT_NAMES + WEIGHT_NAMES, take(len(KEPT) + 4)))
+    vectors = [dict(zip(KINDS, take(5))) for layer_at in range(LAYERS)]
     grads = [dict(zip(KINDS, take(5))) for layer_at in range(LAYERS)]
-    small_rows, = take(1)
+    owned, rows, x_late, dy = take(4)
+    early, late = take(2)
+    d_mixed, partial = take(2)
+    received_one, received_two = take(2)
     totals = take(5)
     landing = [take(BUFFERS) for spec in SUMMED]
-    send, recv, free, pair_send, pair_recv, moved = take(6)
-
+    send, recv, sum_send, sum_recv, free, pair_send, pair_recv, moved = take(8)
+    every = totals[SMALL]
+    hidden, dy_low = (early, late), (late, early)
+    received = (received_one, received_two)
+    received_grad = (received_one, received_one)
+    inputs = (tokens, x_late)
+
+    owned[...] = jnp.zeros_like(owned)
+    for layer_at in range(LAYERS):
+        for row, vector in enumerate((b_qkv, b_up, ln_gain, ln_bias, out_bias)):
+            owned[5 * layer_at + row : 5 * layer_at + row + 1, : vector.shape[1]] = vector[
+                layer_at : layer_at + 1, :
+            ].astype(F32)
     xl, xh, z, y, c = place()
+    where = (xl, xh, z, y)
     meet(neighbours())
     pair = Pair(pair_send, pair_recv)
     moves = Moves(moved)
     own, other = pl.ds(0, COUNT), pl.ds(COUNT, COUNT)
 
-    sums = {}
+    streams, sums = {}, {}
     for core in range(2):
+        streams[core, 0, 0] = Stream(
+            0, GATHERED[0], owned_pieces("small", owned, 0), every, send, recv, *where, core
+        )
         number = 0
-        for layer_at in (1, 0):
-            for which in (QKV, UP, OUT, DOWN):
+        for layer_at in range(LAYERS):
+            for which in range(4):
+                number += 1
+                streams[core, layer_at, which + 1] = Stream(
+                    number, WEIGHTS[which],
+                    owned_pieces(WEIGHT_NAMES[which], owned_weights[which], layer_at),
+                    gathered[layer_at][which], send, recv, *where, core,
+                )
                 sums[core, layer_at, which] = Sum(
                     number, which, layer_at == 0, totals[which], landing[which],
-                    large_out[which].at[layer_at], send, recv, free, (xl, xh, z, y), core,
+                    large_out[which].at[layer_at], sum_send, sum_recv, free, where, core,
                 )
-                number += 1
         sums[core, 0, SMALL] = Sum(
-            number, SMALL, False, totals[SMALL], landing[SMALL], None, send, recv, free,
-            (xl, xh, z, y), core,
+            0, SMALL, False, totals[SMALL], landing[SMALL], None, sum_send, sum_recv, free, where, core
         )
     stage_of = {}
 
-    def advance(layer_at, which):
-        stage = stage_of[layer_at, which] = stage_of.get((layer_at, which), 0) + 1
+    def advance(table, layer_at, which, first):
+        key = (id(table), layer_at, which)
+        stage = stage_of[key] = stage_of.get(key, first - 1) + 1
         for core in range(2):
 
             @pl.when(c == core)
             def _():
-                getattr(sums[core, layer_at, which], f"stage{stage}")()
-
-    loads = {}
-
-    def load(layer_at, name):
-        if name in ("qkv", "up", "out", "down"):
-            which = ("qkv", "up", "out", "down").index(name)
-            loads[layer_at, name] = moves.start(weights_in[layer_at][which], weights[which])
+                getattr(table[core, layer_at, which], f"stage{stage}")()
+
+        return stage
+
+    pending = {}
+    for step, layer_at in schedule:
+        for name in TOUCHED.get(step, ()):
+            turn_of = phase_of(step, layer_at)
+            pending[name, turn_of] = pending.get((name, turn_of), 0) + 1
+    for name in WEIGHT_NAMES:
+        for layer_at in range(LAYERS):
+            pending[name, GATHER + layer_at] = 1
+    loads, keeps = {}, {}
+
+    def settle_load(name):
+        if name in WEIGHT_NAMES:
+            which = WEIGHT_NAMES.index(name)
+            if not pending[name, GATHER] and (name, 0) not in loads:
+                loads[name, 0] = moves.start(gathered[0][which], held[name])
+            if not pending[name, GATHER + 1] and not pending[name, EARLY] and (name, 1) not in loads:
+                loads[name, 1] = moves.start(gathered[1][which], held[name])
+            source = gathered[0][which]
         else:
-            target = gains[layer_at] if name == "gain" else kept[name]
-            loads[layer_at, name] = moves.start(kept_in[layer_at][name], target)
-
-    def need(layer_at, *names):
-        for name in names:
-            if (layer_at, name) in loads:
-                moves.finish(loads.pop((layer_at, name)))
-
-    def used(layer_at, *names):
+            source = spilled[name]
+        if not pending[name, EARLY] and not pending[name, LATE] and (name, 2) not in loads:
+            loads[name, 2] = moves.start(source, held[name])
+
+    def before(step, layer_at):
+        for name in TOUCHED.get(step, ()):
+            if name in WEIGHT_NAMES:
+                moves.finish(loads[name, phase_of(step, layer_at)])
+            elif layer_at == 0 and step not in FORWARD:
+                moves.finish(loads[name, 2])
+            elif layer_at == 1 and step in FORWARD:
+                moves.finish(keeps[name])
+
+    def after(step, layer_at):
+        for name in TOUCHED.get(step, ()):
+            if layer_at == 0 and WHOLE_AFTER.get(name) == step:
+                keeps[name] = moves.start(held[name], spilled[name])
+            pending[name, phase_of(step, layer_at)] -= 1
+            settle_load(name)
+
+    def vec(layer_at):
+        rows[...] = every[...].reshape(rows.shape)
+        for core in range(2):
+
+            @pl.when(c == core)
+            def _():
+                for layer in range(LAYERS):
+                    for kind in KINDS:
+                        unpack_vector(rows, layer, kind, core, vectors[layer][kind])
+
+        rows[...] = jnp.zeros_like(rows)
+
+    def fnorm(layer_at):
+        norm_piece(inputs[layer_at], vectors[layer_at]["gain"], vectors[layer_at]["shift"], hidden[layer_at])
+        pair.push(hidden[layer_at].at[own], hidden[layer_at].at[other], layer_at)
+
+    def joined(layer_at):
+        pair.sent(hidden[layer_at].at[own], layer_at)
+        pair.arrived(hidden[layer_at].at[other], layer_at)
+        for third in range(3):
+            joined_piece(
+                third, hidden[layer_at], lambda n: all_rows(held["qkv"], n),
+                vectors[layer_at]["b_qkv"], tables, held[TURNED],
+            )
+        flip_piece(hidden[layer_at], held[FLIPPED])
+
+    def fattn(start, stop):
+        return lambda layer_at: attention_piece(held[TURNED], held[PROBS], held[MIXED], start, stop)
+
+    def up(layer_at):
+        up_piece(
+            hidden[layer_at], lambda n: all_rows(held["up"], n), vectors[layer_at]["b_up"],
+            held[ACTIVE], held["slope"],
+        )
+
+    def down(layer_at):
         if layer_at:
-            for name in names:
-                load(layer_at - 1, name)
+            pair.sent(partial.at[other], 2)
+        down_piece(
+            held[ACTIVE], lambda n: all_rows(held["down"], n), held[MIXED],
+            lambda n: all_rows(held["out"], n), partial,
+        )
+        pair.push(partial.at[other], received[layer_at], 2 + layer_at)
+
+    def res(layer_at):
+        pair.arrived(received[layer_at], 2 + layer_at)
+        target = late.at[own] if layer_at else x_late
+        residual_piece(
+            inputs[layer_at], partial, received[layer_at], vectors[layer_at]["out_bias"], target
+        )
+        if layer_at:
+            loads["result"] = moves.start(target, result)
 
     def start(layer_at):
+        if layer_at:
+            for half in range(2):
+                moves.finish(loads["out_grad", half])
+                dy[:, pl.ds(half * 512, 512)] = d_mixed[pl.ds(half * COUNT, COUNT), :].astype(F32)
+        else:
+            moves.finish(loads["result"])
         start_piece(dy, dy_low[layer_at], grads[layer_at]["out_bias"])
-        pair.push(dy_low[layer_at].at[own], dy_low[layer_at].at[other], 2 * layer_at)
-
-    def low_arrived(layer_at):
-        pair.wait(dy_low[layer_at].at[own], dy_low[layer_at].at[other], 2 * layer_at)
+        pair.push(dy_low[layer_at].at[own], dy_low[layer_at].at[other], 4 + layer_at)
+
+    def low(layer_at):
+        pair.sent(dy_low[layer_at].at[own], 4 + layer_at)
+        pair.arrived(dy_low[layer_at].at[other], 4 + layer_at)
 
     def gdown(layer_at):
-        need(layer_at, "active")
-        rows_grad_piece(8, kept["active"], dy_low[layer_at], store_row_tile(totals[DOWN]))
-        used(layer_at, "active")
+        rows_grad_piece(8, held[ACTIVE], dy_low[layer_at], store_row_tile(totals[DOWN]))
 
     def slope(layer_at):
-        need(layer_at, "down", "slope")
         slope_piece(
-            dy_low[layer_at], lambda n: row_tile(weights[DOWN], n), kept["slope"], kept["slope"],
+            dy_low[layer_at], lambda n: row_tile(held["down"], n), held["slope"], held["slope"],
             grads[layer_at]["b_up"],
         )
-        used(layer_at, "down")
 
     def gup(layer_at):
-        need(layer_at, "flipped")
-        columns_grad_piece(8, kept["flipped"], kept["slope"], store_column_tile(totals[UP]))
+        columns_grad_piece(8, held[FLIPPED], held["slope"], store_column_tile(totals[UP]))
 
     def dmixed(layer_at):
-        need(layer_at, "out")
-        d_mixed_piece(dy_low[layer_at], lambda n: row_tile(weights[OUT], n), d_mixed)
-        used(layer_at, "out")
+        d_mixed_piece(dy_low[layer_at], lambda n: row_tile(held["out"], n), d_mixed)
 
     def gout(layer_at):
-        need(layer_at, "mixed")
-        rows_grad_piece(2, kept["mixed"], dy_low[layer_at], store_row_tile(totals[OUT]))
-        used(layer_at, "mixed")
-
-    def attention(layer_at, first, stop):
-        need(layer_at, "turned", "probs")
-        attention_back_piece(
-            kept["turned"], kept["probs"], d_mixed, tables, kept["turned"], grads[layer_at]["b_qkv"], first, stop
-        )
-        if stop == 8:
-            used(layer_at, "probs")
+        rows_grad_piece(2, held[MIXED], dy_low[layer_at], store_row_tile(totals[OUT]))
+
+    def battn(first, stop):
+        return lambda layer_at: attention_back_piece(
+            held[TURNED], held[PROBS], d_mixed, tables, held[TURNED], grads[layer_at]["b_qkv"],
+            first, stop,
+        )
 
     def dhidden(layer_at):
-        need(layer_at, "qkv", "up")
-        if layer_at == 0:
-            pltpu.make_async_copy(
-                d_hidden.at[other], d_hidden.at[other], pair_send.at[3]
-            ).wait()
+        pair.sent(partial.at[other], 3 if layer_at else 7)
         d_hidden_piece(
-            kept["turned"], lambda n: row_tile(weights[QKV], n), kept["slope"],
-            lambda n: row_tile(weights[UP], n), d_hidden,
-        )
-        pair.push(d_hidden.at[other], received[layer_at], 2 * layer_at + 1)
-        used(layer_at, "qkv", "up")
+            held[TURNED], lambda n: row_tile(held["qkv"], n), held["slope"],
+            lambda n: row_tile(held["up"], n), partial,
+        )
+        pair.push(partial.at[other], received_grad[layer_at], 6 + layer_at)
 
     def gqkv(layer_at):
-        columns_grad_piece(6, kept["flipped"], kept["turned"], store_column_tile(totals[QKV]))
+        columns_grad_piece(6, held[FLIPPED], held[TURNED], store_column_tile(totals[QKV]))
 
     def norm(layer_at):
-        need(layer_at, "gain")
-        target = received[layer_at]
-        pltpu.make_async_copy(target, target, pair_recv.at[2 * layer_at + 1]).wait()
+        pair.arrived(received_grad[layer_at], 6 + layer_at)
         norm_back_piece(
-            x_late if layer_at else tokens, gains[layer_at], dy, d_hidden, target, dy,
+            inputs[layer_at], vectors[layer_at]["gain"], dy, partial, received_grad[layer_at], dy,
             grads[layer_at]["gain"], grads[layer_at]["shift"],
         )
         if layer_at == 0:
@@ -1441,57 +1333,73 @@
             @pl.when(c == core)
             def _():
                 for kind in KINDS:
-                    pack_vector(small_rows, layer_at, kind, core, grads[layer_at][kind])
+                    pack_vector(rows, layer_at, kind, core, grads[layer_at][kind])
+                if layer_at == 0:
+                    streams[core, 0, 0].finish()
 
         if layer_at == 0:
-            totals[SMALL][...] = small_rows[...].reshape(totals[SMALL].shape)
-
-    for name in ("active", "down", "slope", "flipped", "out", "mixed", "turned", "probs", "qkv", "up", "gain"):
-        load(1, name)
-    load(0, "gain")
-    late = moves.start(x_kept, x_late)
-    small_rows[...] = jnp.zeros_like(small_rows)
-    dy[...] = out_grad[...].astype(F32)
+            totals[SMALL][...] = rows[...].reshape(totals[SMALL].shape)
+
+    for half in range(2):
+        loads["out_grad", half] = moves.start(
+            out_grad.at[:, pl.ds(half * 512, 512)], d_mixed.at[pl.ds(half * COUNT, COUNT), :]
+        )
     steps = {
-        "start": start, "low": low_arrived, "gdown": gdown, "slope": slope, "gup": gup,
-        "dmixed": dmixed, "gout": gout, "dhidden": dhidden, "gqkv": gqkv, "norm": norm, "pack": pack,
-        "attention": lambda layer_at: attention(layer_at, 0, 8),
-        "attentionA": lambda layer_at: attention(layer_at, 0, 4),
-        "attentionB": lambda layer_at: attention(layer_at, 4, 8),
+        "vec": vec, "fnorm": fnorm, "joined": joined, "fattnA": fattn(0, 4), "fattnB": fattn(4, 8),
+        "up": up, "down": down, "res": res, "start": start, "low": low, "gdown": gdown, "slope": slope,
+        "gup": gup, "dmixed": dmixed, "gout": gout, "battnA": battn(0, 4), "battnB": battn(4, 8),
+        "dhidden": dhidden, "gqkv": gqkv, "norm": norm, "pack": pack,
     }
-    streams = {"Q": QKV, "U": UP, "O": OUT, "D": DOWN, "S": SMALL}
-    for step in schedule:
-        name, layer_at = step[:-1], int(step[-1])
-        if name == "free":
-            used(layer_at, "slope", "flipped", "turned")
-        elif name == "late":
-            moves.finish(late)
-        elif name in streams:
-            advance(layer_at, streams[name])
-        else:
-            steps[name](layer_at)
-    pltpu.make_async_copy(d_hidden.at[other], d_hidden.at[other], pair_send.at[1]).wait()
-    tail = landing[SMALL][8]
-    for layer_at in range(LAYERS):
-        for (kind, (row, size, factor, shift)), target in zip(KINDS.items(), small_out):
-            at_row = 5 * layer_at + row
-            target[layer_at : layer_at + 1, :] = tail[1, at_row : at_row + 1, :size]
+    for name, layer_at in schedule:
+        with jax.named_scope(name):
+            if name in GATHERS:
+                stage = advance(streams, layer_at, GATHERS[name], 0)
+                if stage == 6 and GATHERS[name]:
+                    weight = WEIGHT_NAMES[GATHERS[name] - 1]
+                    pending[weight, GATHER + layer_at] = 0
+                    settle_load(weight)
+            elif name in SUMS:
+                advance(sums, layer_at, SUMS[name], 1)
+            else:
+                before(name, layer_at)
+                steps[name](layer_at)
+                after(name, layer_at)
+    pair.sent(partial.at[other], 6)
+    for core in range(2):
+
+        @pl.when(c == core)
+        def _():
+            for (core_of, layer_at, which), stream in streams.items():
+                if core_of == core:
+                    stream.finish()
+
+    small_out[...] = landing[SMALL][8][1]
     for copy in list(moves.open):
         copy.wait()
 
 
-def backward_call(tokens, x_kept, out_grad, tables, kept, weights):
+def blocks_call(tokens, out_grad, b_qkv, b_up, ln_gain, ln_bias, out_bias, tables, *owned_weights):
     vmem, hbm = pl.BlockSpec(memory_space=pltpu.VMEM), pl.BlockSpec(memory_space=pltpu.HBM)
     shape = jax.ShapeDtypeStruct
-    flat = []
+    outs = [
+        shape((COUNT, D), BF16),
+        shape((COUNT, D), F32),
+        shape((LAYERS, 16, 3072), F32),
+        shape((LAYERS, 16, 4096), F32),
+        shape((LAYERS, 16, 1024), F32),
+        shape((LAYERS, 64, 1024), F32),
+    ]
     for layer_at in range(LAYERS):
-        flat += list(kept[layer_at])
-    for layer_at in range(LAYERS):
-        flat += list(weights[layer_at])
+        outs += [shape(weight_shape(spec), BF16) for spec in WEIGHTS]
+    outs += [shape(dims, kind) for name, dims, kind in KEPT]
+    in_hbm = len(outs)
+    outs += [shape((OWNED_ROWS, LANE), F32)]
     scratch = [pltpu.VMEM(dims, kind) for name, dims, kind in KEPT]
     scratch += [pltpu.VMEM(weight_shape(spec), BF16) for spec in WEIGHTS]
+    scratch += [pltpu.VMEM((1, n), F32) for n in (1536, 2048, D, D, D) * (2 * LAYERS)]
     scratch += [
-        pltpu.VMEM((1, D), F32),
+        pltpu.VMEM((OWNED_ROWS, LANE), F32),
+        pltpu.VMEM((64 * OWNED_ROWS, LANE), F32),
         pltpu.VMEM((COUNT, D), F32),
         pltpu.VMEM((COUNT, D), F32),
         pltpu.VMEM((BOTH, D), BF16),
@@ -1501,61 +1409,85 @@
         pltpu.VMEM((COUNT, D), F32),
         pltpu.VMEM((COUNT, D), F32),
     ]
-    scratch += [pltpu.VMEM((1, n), F32) for n in (1536, 2048, D, D, D) * LAYERS]
-    scratch += [pltpu.VMEM((64 * OWNED_ROWS, LANE), F32)]
     for spec in SUMMED:
         scratch.append(pltpu.VMEM(total_shape(spec), F32 if spec[0] == "small" else BF16))
     for spec in SUMMED:
         scratch += landing_shapes(spec)
+    count = 1 + 4 * LAYERS
     scratch += [
-        pltpu.SemaphoreType.DMA((1 + 4 * LAYERS, SUM_SLOTS)),
-        pltpu.SemaphoreType.DMA((1 + 4 * LAYERS, SUM_SLOTS)),
+        pltpu.SemaphoreType.DMA((count, SLOTS)),
+        pltpu.SemaphoreType.DMA((count, SLOTS)),
+        pltpu.SemaphoreType.DMA((count, SUM_SLOTS)),
+        pltpu.SemaphoreType.DMA((count, SUM_SLOTS)),
         pltpu.SemaphoreType.REGULAR((4, 12)),
-        pltpu.SemaphoreType.DMA((4,)),
-        pltpu.SemaphoreType.DMA((4,)),
+        pltpu.SemaphoreType.DMA((8,)),
+        pltpu.SemaphoreType.DMA((8,)),
         pltpu.SemaphoreType.DMA((40,)),
     ]
+    found = pl.pallas_call(
+        functools.partial(blocks_kernel, [(STEP_NAMES[step // 2], step % 2) for step in SCHEDULE]),
+        out_shape=outs,
+        in_specs=[vmem, hbm] + [vmem] * 6 + [hbm] * 4,
+        out_specs=[hbm] * in_hbm + [vmem],
+        scratch_shapes=scratch,
+        name="blocks",
+        compiler_params=pltpu.CompilerParams(
+            collective_id=0, has_side_effects=True, vmem_limit_bytes=63 * 2**20
+        ),
+    )(tokens, out_grad, b_qkv, b_up, ln_gain, ln_bias, out_bias, tables, *owned_weights)
+    return found[:6] + found[in_hbm:]
+
+
+def hand_over_kernel(*refs):
+    sources, small, targets, parts = refs[:6], refs[6], refs[7:13], refs[13:18]
+    held, (read, written) = refs[18:24], refs[24:]
+    copies_in, copies_out = [
+        [
+            pltpu.make_async_copy(source, target, done.at[number])
+            for number, (source, target) in enumerate(zip(left, right))
+        ]
+        for left, right, done in ((sources, held, read), (held, targets, written))
+    ]
+    for copy in copies_in:
+        copy.start()
+    for layer_at in range(LAYERS):
+        for (row, size, factor, shift), target in zip(KINDS.values(), parts):
+            at_row = 5 * layer_at + row
+            target[layer_at : layer_at + 1, :] = small[at_row : at_row + 1, :size]
+    for copy, onward in zip(copies_in, copies_out):
+        copy.wait()
+        onward.start()
+    for copy in copies_out:
+        copy.wait()
+
+
+def hand_over(found):
+    vmem, hbm = pl.BlockSpec(memory_space=pltpu.VMEM), pl.BlockSpec(memory_space=pltpu.HBM)
+    shape = jax.ShapeDtypeStruct
     return pl.pallas_call(
-        functools.partial(backward_kernel, whole_schedule()),
-        out_shape=[
-            shape((COUNT, D), F32),
-            shape((LAYERS, 16, 3072), F32),
-            shape((LAYERS, 16, 4096), F32),
-            shape((LAYERS, 16, 1024), F32),
-            shape((LAYERS, 64, 1024), F32),
-        ]
+        hand_over_kernel,
+        out_shape=[shape(item.shape, item.dtype) for item in found[:6]]
         + [shape((LAYERS, size), F32) for row, size, factor, shift in KINDS.values()],
-        in_specs=[vmem, hbm, vmem, vmem] + [hbm] * len(flat),
-        out_specs=[hbm] * 5 + [vmem] * 5,
-        scratch_shapes=scratch,
-        name="backward",
-        compiler_params=pltpu.CompilerParams(
-            collective_id=1, has_side_effects=True, vmem_limit_bytes=63 * 2**20
-        ),
-    )(tokens, x_kept, out_grad, tables, *flat)
+        in_specs=[hbm] * 6 + [vmem],
+        out_specs=[hbm] * 6 + [vmem] * 5,
+        scratch_shapes=[pltpu.VMEM(item.shape, item.dtype) for item in found[:6]]
+        + [pltpu.SemaphoreType.DMA((6,))] * 2,
+        name="hand_over",
+    )(*found)
 
 
 def on_device(
     tokens, w_qkv, b_qkv, w_out, w_up, b_up, w_down, ln_gain, ln_bias, out_bias, out_grad
 ):
     tables = jnp.asarray(turn_tables())
-    found = forward_call(
-        tokens, b_qkv, b_up, ln_gain, ln_bias, out_bias, tables, w_qkv, w_up, w_out, w_down
+    found = blocks_call(
+        tokens, out_grad, b_qkv, b_up, ln_gain, ln_bias, out_bias, tables, w_qkv, w_up, w_out, w_down
     )
-    current, x_kept = found[:2]
-    weights = [found[2 + 4 * layer_at : 6 + 4 * layer_at] for layer_at in range(LAYERS)]
-    first = 2 + 4 * LAYERS
-    kept = [
-        found[first + len(KEPT) * layer_at : first + len(KEPT) * (layer_at + 1)]
-        for layer_at in range(LAYERS)
-    ]
-    upstream, g_qkv, g_up, g_out, g_down, *small = backward_call(
-        tokens, x_kept, out_grad, tables, kept, weights
-    )
+    result, in_grad, g_qkv, g_up, g_out, g_down, *small = hand_over(found)
     g_b_qkv, g_b_up, g_gain, g_shift, g_out_bias = small
     return (
-        current,
-        upstream,
+        result,
+        in_grad,
         g_qkv,
         g_b_qkv,
         g_out,

time: 321 us -> 271 us (0.84)
  Pallas kernels: 311 us -> 270 us
  local copies, waits for them, and re-layouts: 9 us -> 0 us
    pallas_call x2, Pallas kernels: 311 us -> 270 us  [the longest x1 266 us: blocks_call(): pl.pallas_call(functools.partial(blocks_kernel, [(STEP_NAMES[step // 2],...]
    unnamed x31 -> x0, local copies, waits for them, and re-layouts: 9 us -> none
where the time goes in v4:
time: 271 us
  Pallas kernels  270 us (100%)
    pallas_call x1, Pallas kernels, blocks_call(): pl.pallas_call(functools.partial(blocks_kernel, [(STEP_NAMES[step // 2],...  266 us

profile of v4, /device:TPU:1, one launch (start us, length us, event | category | flops | bytes accessed | tf_op | source)
XLA Modules:
  0.0 270.7 jit_solution(6161660443772842828)
XLA Ops:
  0.6 265.6 %blocks.1 = (bf16[256,1024]{1,0:T(8,128)(2,1)}, f32[256,1024]{1,0:T(8,128)}, f32[2,16,3072]{2,1,0:T(8,128)}, f32[2,16,4096]{2,1,0:T(8,128)}, f32[2,16,1024]{2,1,...) custom-call(bf16[256,1024]{1,0:T(8,128)(2,1)} %tokens.1, ...), custom_call_target="tpu_custom_call" | custom-call | tf_op jit(solution)/shard_map/blocks/pallas_call | solution.py:1427
  266.3 4.3 %hand_over.1 = (bf16[256,1024]{1,0:T(8,128)(2,1)}, f32[256,1024]{1,0:T(8,128)}, f32[2,16,3072]{2,1,0:T(8,128)}, f32[2,16,4096]{2,1,0:T(8,128)}, f32[2,16,1024]{2...) custom-call(bf16[256,1024]{1,0:T(8,128)(2,1)} %get-tuple-element.29., ...), custom_call_target="tpu_custom_call" | custom-call | tf_op jit(solution)/shard_map/hand_over/pallas_call | solution.py:1467

commit v5 on v4

--- a/solution.py
+++ b/solution.py
@@ -11,28 +11,30 @@
 
 
 STEP_NAMES = (
-    "s", "q", "u", "o", "d", "Q", "U", "O", "D", "S", "vec", "fnorm", "joined", "fattnA",
-    "fattnB", "up", "down", "res", "start", "low", "gdown", "slope", "gup", "dmixed", "gout",
+    "s", "q", "u", "o", "d", "Q", "R", "U", "V", "O", "D", "E", "S", "vec", "fnorm", "joined",
+    "fattn", "up", "down", "res", "start", "low", "gdown", "slope", "gup", "dmixed", "gout",
     "battnA", "battnB", "dhidden", "gqkv", "norm", "pack",
 )
 (
-    s0, s1, q0, q1, u0, u1, o0, o1, d0, d1, Q0, Q1, U0, U1, O0, O1, D0, D1, S0, S1, vec0, vec1,
-    fnorm0, fnorm1, joined0, joined1, fattnA0, fattnA1, fattnB0, fattnB1, up0, up1, down0, down1,
-    res0, res1, start0, start1, low0, low1, gdown0, gdown1, slope0, slope1, gup0, gup1, dmixed0,
-    dmixed1, gout0, gout1, battnA0, battnA1, battnB0, battnB1, dhidden0, dhidden1, gqkv0, gqkv1,
-    norm0, norm1, pack0, pack1,
+    s0, s1, q0, q1, u0, u1, o0, o1, d0, d1, Q0, Q1, R0, R1, U0, U1, V0, V1, O0, O1, D0, D1, E0,
+    E1, S0, S1, vec0, vec1, fnorm0, fnorm1, joined0, joined1, fattn0, fattn1, up0, up1, down0,
+    down1, res0, res1, start0, start1, low0, low1, gdown0, gdown1, slope0, slope1, gup0, gup1,
+    dmixed0, dmixed1, gout0, gout1, battnA0, battnA1, battnB0, battnB1, dhidden0, dhidden1, gqkv0,
+    gqkv1, norm0, norm1, pack0, pack1,
 ) = range(2 * len(STEP_NAMES))
 SCHEDULE = (
-    s0, o0, q0, o1, s0, o0, u0, s0, q0, o1, o0, d0, s0, u1, q1, q0, u0, s0, o1, q0, d1, d0, d0,
-    u0, q1, q0, d0, s0, s0, vec0, q1, fnorm0, q0, o0, u0, d0, o0, q0, joined0, u0, fattnA0, o0,
-    q1, d1, u1, o1, u0, d0, fattnB0, u1, o0, u0, q1, u1, d0, up0, q1, down0, d1, o1, u1, q1, res0,
-    fnorm1, o1, d1, joined1, start1, u1, fattnA1, o1, d1, fattnB1, u1, low1, dmixed1, battnA1, d1,
-    gout1, up1, O1, gdown1, D1, d1, battnB1, slope1, O1, gup1, U1, O1, D1, down1, gqkv1, D1, Q1,
-    res1, dhidden1, U1, O1, norm1, start0, low0, O1, Q1, gout0, D1, dmixed0, O0, U1, gdown0, D0,
-    D1, Q1, battnA0, O0, slope0, D1, U1, gup0, U0, D0, U1, O0, battnB0, Q1, D0, gqkv0, Q0, U0, D1,
-    dhidden0, Q1, D1, D0, Q0, U1, pack1, O1, U0, norm0, pack0, U1, U1, S0, Q1, Q0, D0, O1, U0, O1,
-    Q1, S0, U0, D0, O0, Q1, Q0, S0, U0, O0, Q0, S0, O0, S0, Q0, D0, O0, U0, S0, Q0, D0, S0, Q0,
-    O0, U0, S0,
+    o1, s0, q0, q1, o1, o0, u0, s0, q0, s0, d0, q1, o0, q0, s0, d1, u0, o0, q0, u1, o1, u0, o0,
+    u0, d0, q0, q1, o0, s0, d0, d0, u0, s0, s0, vec0, q0, d0, q1, fnorm0, u0, o1, u1, q0, o0,
+    joined0, d0, u1, d1, q1, fattn0, u1, u0, o0, d0, up0, q1, down0, d1, o1, u1, res0, q1, fnorm1,
+    d1, o1, joined1, u1, start1, fattn1, low1, gout1, o1, O1, u1, O1, dmixed1, d1, up1, gdown1,
+    d1, D1, D1, E1, O1, battnA1, battnB1, d1, D1, gqkv1, Q1, Q1, O1, slope1, gup1, V1, O1, D1, E1,
+    Q1, down1, U1, U1, E1, D1, R1, res1, dhidden1, V1, U1, norm1, start0, E1, V1, Q1, O1, low0,
+    gdown0, E0, D0, R1, gout0, D0, slope0, E1, U1, R1, V1, O0, O0, gup0, U0, U0, D1, U1, D0,
+    dmixed0, R1, V0, E0, battnA0, O0, D1, Q1, battnB0, U0, U1, gqkv0, E1, Q1, D1, D0, R0,
+    dhidden0, V0, E1, V1, E0, Q0, D0, pack1, E1, U1, Q1, U1, U0, Q0, O1, V1, norm0, R1, O1, V0,
+    O0, U0, D0, E0, R1, V1, O0, Q1, V1, R0, Q0, pack0, O0, S0, D0, S0, U0, R0, R1, V0, Q0, S0, O0,
+    U0, R1, V0, E0, R0, D0, Q0, S0, V0, E0, R0, Q0, O0, S0, R0, V0, S0, Q0, E0, R0, V0, Q0, S0,
+    S0, R0, E0, U0,
 )
 
 
@@ -55,19 +57,31 @@
     return lax.rem(value + (step + 4), 4)
 
 
-def meet(others):
+def greet(others):
     barrier = pltpu.get_barrier_semaphore()
     for other in others:
         pl.semaphore_signal(barrier, inc=1, device_id=other, device_id_type=MESH)
-    pl.semaphore_wait(barrier, len(others))
-
-
+    return len(others)
+
+
+def await_greetings(count):
+    pl.semaphore_wait(pltpu.get_barrier_semaphore(), count)
+
+
+SMALL_GATHERED = ("small", True, 32, 128, 0, 1)
 GATHERED = (
-    ("small", True, 32, 128, 0, 1),
-    ("qkv", True, 32, 1536, 4, 8),
-    ("up", True, 32, 2048, 5, 11),
-    ("out", False, 32, 1024, 3, 5),
-    ("down", False, 128, 1024, 3, 5),
+    (
+        ("qkv", True, 32, 1536, 4, 8),
+        ("up", True, 32, 2048, 6, 10),
+        ("out", False, 32, 1024, 3, 5),
+        ("down", False, 128, 1024, 3, 5),
+    ),
+    (
+        ("qkv", True, 32, 1536, 4, 8),
+        ("up", True, 32, 2048, 4, 12),
+        ("out", False, 32, 1024, 2, 6),
+        ("down", False, 128, 1024, 2, 6),
+    ),
 )
 SLOTS = 18
 
@@ -307,6 +321,7 @@
 F32 = jnp.float32
 BF16 = jnp.bfloat16
 TILE = 256
+WIDE = 512
 
 
 def turn_tables():
@@ -424,21 +439,18 @@
 
 
 def joined_piece(third, hidden, w_qkv, b_qkv, tables, target):
-    def body(index):
-        columns = columns_of(index + third * 2)
-        found = dot(hidden[...], w_qkv(columns)) + b_qkv[:, columns]
-        for sequence in range(2):
-            for pair in range(2):
-                part = found[sequence * COUNT : (sequence + 1) * COUNT, pair * LANE : (pair + 1) * LANE]
-                if third < 2:
-                    part = turn(part, tables, 1.0)
-                if third == 0:
-                    part = part * HEAD_DIM**-0.5
-                target[
-                    pl.ds(sequence * COUNT, COUNT), columns_of(index * 2 + pair + third * 4, LANE)
-                ] = part.astype(BF16)
-
-    loop(2, body)
+    columns = pl.ds(third * 512, 512)
+    found = dot(hidden[...], w_qkv(columns)) + b_qkv[:, columns]
+    for sequence in range(2):
+        for pair in range(4):
+            part = found[sequence * COUNT : (sequence + 1) * COUNT, pair * LANE : (pair + 1) * LANE]
+            if third < 2:
+                part = turn(part, tables, 1.0)
+            if third == 0:
+                part = part * HEAD_DIM**-0.5
+            target[
+                pl.ds(sequence * COUNT, COUNT), pl.ds(pair * LANE + third * 512, LANE)
+            ] = part.astype(BF16)
 
 
 def first_head():
@@ -450,45 +462,52 @@
     return jnp.where(keep, values, jnp.zeros_like(values))
 
 
-def attention_piece(turned, probs, mixed, start=0, stop=8):
-    def body(index):
-        index = index + start
-        sequence, pair = index // 4, index % 4
-        rows, columns = columns_of(sequence, COUNT), columns_of(pair, LANE)
-        q2, k2, v2 = (turned[rows, columns_of(pair + third * 4, LANE)] for third in range(3))
-        causal = lax.broadcasted_iota(jnp.int32, (COUNT, COUNT), 0) >= lax.broadcasted_iota(
+def pair_of_heads(turned, index):
+    sequence, pair = index // 4, index % 4
+    rows, columns = columns_of(sequence, COUNT), columns_of(pair, LANE)
+    return rows, columns, *(turned[rows, columns_of(pair + third * 4, LANE)] for third in range(3))
+
+
+def attention_piece(turned, probs, mixed):
+    def one(index):
+        rows, columns, q2, k2, v2 = pair_of_heads(turned, index)
+        causal = lax.broadcasted_iota(jnp.int32, (COUNT, COUNT), 0) <= lax.broadcasted_iota(
             jnp.int32, (COUNT, COUNT), 1
         )
         out = []
         for half in range(2):
-            scores = jnp.where(causal, dot_nt(only_head(q2, half), k2), FILL)
-            expo = jnp.exp(scores - jnp.max(scores, -1, keepdims=True))
-            prob = (expo * (1.0 / jnp.sum(expo, -1, keepdims=True))).astype(BF16)
+            scores = jnp.where(causal, dot_nt(k2, only_head(q2, half)), FILL)
+            expo = jnp.exp(scores - jnp.max(scores, 0, keepdims=True))
+            prob = (expo * (1.0 / jnp.sum(expo, 0, keepdims=True))).astype(BF16)
             probs[index * 2 + half] = prob
-            out.append(dot(prob, v2))
+            out.append(dot_tn(prob, v2))
         mixed[rows, columns] = jnp.where(first_head(), out[0], out[1]).astype(BF16)
 
-    loop(stop - start, body)
+    def body(index):
+        for pair in range(4):
+            one(index * 4 + pair)
+
+    loop(2, body)
 
 
 def up_piece(hidden, w_up, b_up, active, slope):
     def body(index):
-        columns = columns_of(index)
+        columns = columns_of(index, WIDE)
         upward = dot(hidden[...], w_up(columns)) + b_up[:, columns]
         spread = 0.5 + 0.5 * lax.erf(upward * (0.5**0.5))
         active[:, columns] = (upward * spread).astype(BF16)
         dense = jnp.exp(upward * upward * -0.5) * (1.0 / math.sqrt(2.0 * math.pi))
         slope[:, columns] = (spread + upward * dense).astype(BF16)
 
-    loop(8, body)
+    loop(2048 // WIDE, body)
 
 
 def down_piece(active, w_down, mixed, w_out, partial):
     def body(index):
-        columns = columns_of(index)
+        columns = columns_of(index, WIDE)
         partial[:, columns] = dot(mixed[...], w_out(columns)) + dot(active[...], w_down(columns))
 
-    loop(4, body)
+    loop(D // WIDE, body)
 
 
 def residual_piece(x_ref, partial, received, out_bias, target):
@@ -506,7 +525,7 @@
 def start_piece(dy, dy_low, out_bias_grad):
     def body(index):
         rows = columns_of(index, 64)
-        values = dy[rows, :]
+        values = dy[rows, :].astype(F32)
         dy_low[rows, :] = values.astype(BF16)
         out_bias_grad[...] += jnp.sum(values, 0, keepdims=True)
 
@@ -526,77 +545,65 @@
         loop(columns // TILE, body)
 
 
-def rows_grad_piece(count, left, right, store):
+def rows_grad_piece(size, left, right, store):
     def body(index):
-        store(index, dot_tn(left[:, columns_of(index)], right[...]).astype(BF16))
-
-    loop(count, body)
-
-
-def columns_grad_piece(count, left_flipped, right, store):
+        store(index, dot_tn(left[:, columns_of(index, size)], right[...]).astype(BF16))
+
+    loop(left.shape[1] // size, body)
+
+
+def columns_grad_piece(size, left_flipped, right, store):
     def body(index):
-        store(index, dot(left_flipped[...], right[:, columns_of(index)]).astype(BF16))
-
-    loop(count, body)
+        store(index, dot(left_flipped[...], right[:, columns_of(index, size)]).astype(BF16))
+
+    loop(right.shape[1] // size, body)
 
 
 def slope_piece(dy_low, w_down_rows, slope, d_up, b_up_grad):
     def body(index):
-        columns = columns_of(index)
+        columns = columns_of(index, D)
         found = (dot_nt(dy_low[...], w_down_rows(index)) * slope[:, columns].astype(F32)).astype(BF16)
         d_up[:, columns] = found
         b_up_grad[:, columns] = jnp.sum(found.astype(F32), 0, keepdims=True)
 
-    loop(8, body)
+    loop(2048 // D, body)
 
 
 def d_mixed_piece(dy_low, w_out_rows, d_mixed):
-    def body(index):
-        d_mixed[:, columns_of(index)] = dot_nt(dy_low[...], w_out_rows(index)).astype(BF16)
-
-    loop(2, body)
-
-
-def attention_back_piece(turned, probs, d_mixed, tables, d_joined, b_qkv_grad, start=0, stop=8):
-    if start == 0:
+    d_mixed[...] = dot_nt(dy_low[...], w_out_rows(0)).astype(BF16)
+
+
+def attention_back_piece(turned, probs, d_mixed, tables, d_joined, b_qkv_grad, sequence):
+    if sequence == 0:
         b_qkv_grad[...] = jnp.zeros_like(b_qkv_grad)
-
-    def body(index):
-        index = index + start
-        sequence, pair = index // 4, index % 4
-        rows, columns = columns_of(sequence, COUNT), columns_of(pair, LANE)
-        q2, k2, v2 = (turned[rows, columns_of(pair + third * 4, LANE)] for third in range(3))
+    for index in range(sequence * 4, sequence * 4 + 4):
+        rows, columns, q2, k2, v2 = pair_of_heads(turned, index)
         dm2 = d_mixed[rows, columns]
-        found = []
-        for half in range(2):
-            prob = probs[index * 2 + half]
+        both_probs = [probs[index * 2 + half] for half in range(2)]
+        d_scores = []
+        for half, prob in enumerate(both_probs):
             full = prob.astype(F32)
-            d_probs = dot_nt(only_head(dm2, half), v2)
-            d_scores = (
-                full * (d_probs - jnp.sum(d_probs * full, -1, keepdims=True))
-            ).astype(BF16)
-            found.append((dot(d_scores, k2), dot_tn(d_scores, q2), dot_tn(prob, dm2)))
-        for third in range(3):
-            part = jnp.where(first_head(), found[0][third], found[1][third])
-            if third == 0:
-                part = part * HEAD_DIM**-0.5
+            d_probs = dot_nt(v2, only_head(dm2, half))
+            d_scores.append(
+                (full * (d_probs - jnp.sum(d_probs * full, 0, keepdims=True))).astype(BF16)
+            )
+        apart = lambda values: jnp.concatenate([only_head(values, 0), only_head(values, 1)], 0)
+        parts = (
+            dot_tn(jnp.concatenate(d_scores, 0), apart(k2)) * HEAD_DIM**-0.5,
+            dot(jnp.concatenate(d_scores, 1), apart(q2)),
+            dot(jnp.concatenate(both_probs, 1), apart(dm2)),
+        )
+        for third, part in enumerate(parts):
             if third < 2:
                 part = turn(part, tables, -1.0)
             part = part.astype(BF16)
-            there = columns_of(pair + third * 4, LANE)
+            there = columns_of(index % 4 + third * 4, LANE)
             d_joined[rows, there] = part
             b_qkv_grad[:, there] += jnp.sum(part.astype(F32), 0, keepdims=True)
 
-    loop(stop - start, body)
-
 
 def d_hidden_piece(d_joined, w_qkv_rows, d_up, w_up_rows, d_hidden):
-    def body(index):
-        d_hidden[:, columns_of(index)] = dot_nt(d_joined[...], w_qkv_rows(index)) + dot_nt(
-            d_up[...], w_up_rows(index)
-        )
-
-    loop(4, body)
+    d_hidden[...] = dot_nt(d_joined[...], w_qkv_rows(0)) + dot_nt(d_up[...], w_up_rows(0))
 
 
 def norm_back_piece(x_ref, gain, dy, d_hidden, received, target, gain_grad, shift_grad):
@@ -620,25 +627,25 @@
 
 
 SUMMED = (
-    ("qkv", True, 32, 1536, 3, 9),
-    ("up", True, 32, 2048, 4, 12),
-    ("out", False, 32, 1024, 2, 6),
-    ("down", False, 128, 1024, 2, 6),
-    ("small", True, 32, 128, 0, 1),
+    (0, True, 32, 0, 768, 0, 6),
+    (0, True, 32, 768, 768, 3, 3),
+    (1, True, 32, 0, 1024, 0, 8),
+    (1, True, 32, 1024, 1024, 4, 4),
+    (2, False, 32, 0, 1024, 0, 8),
+    (3, False, 128, 0, 512, 0, 4),
+    (3, False, 128, 512, 512, 2, 2),
+    (4, True, 32, 0, 128, 0, 1),
 )
+SMALL_SUM = 7
+QKV, UP, OUT, DOWN, SMALL = range(5)
 SUM_SLOTS = 18
 BUFFERS = 9
 
 
-def total_shape(spec):
-    name, by_columns, rows, columns, swapped, width = spec
-    return (2 if by_columns else 1, 4, 4, rows, columns)
-
-
 def landing_shapes(spec):
-    name, by_columns, rows, columns, swapped, width = spec
+    gradient, by_columns, rows, base, columns, swapped, width = spec
     banks = 2 if by_columns else 1
-    kind = F32 if name == "small" else BF16
+    kind = F32 if gradient == SMALL else BF16
     wide = width * LANE
     return [
         pltpu.VMEM((banks, 4, 4, rows, swapped * LANE) if swapped else (8, LANE), kind),
@@ -649,7 +656,7 @@
         pltpu.VMEM((2, banks, rows, wide), kind),
         pltpu.VMEM((3, rows, wide), kind),
         pltpu.VMEM((rows, columns), F32),
-        pltpu.VMEM((2, 16, LANE), F32),
+        pltpu.VMEM((2, 16 if gradient == SMALL else 1, LANE), F32),
     ]
 
 
@@ -669,10 +676,11 @@
 class Sum:
     def __init__(self, number, which, before, total, landing, output, send, recv, free, where, core):
         spec = SUMMED[which]
-        self.name, self.by_columns, self.rows, self.columns, self.swapped, self.width = spec
+        self.gradient, self.by_columns, self.rows, base, self.columns, self.swapped, self.width = spec
+        self.base = base
         self.number, self.which = number, which
         self.before = before
-        self.after = not before and self.name != "small"
+        self.after = not before and self.gradient != SMALL
         self.total, self.output = total, output
         (
             self.swap,
@@ -692,9 +700,11 @@
         self.half = self.rows // 2
         s, w = self.swapped, self.width
         xl, xh, z, y = where
-        self.wide = pl.ds(pl.multiple_of(xl * (s * LANE), LANE), w * LANE)
-        self.mine = pl.ds(pl.multiple_of(xl * (w * LANE), LANE), max(s, 1) * LANE)
-        self.theirs = pl.ds(pl.multiple_of((1 - xl) * (w * LANE), LANE), max(s, 1) * LANE)
+        self.wide = pl.ds(pl.multiple_of(base + xl * (s * LANE), LANE), w * LANE)
+        self.mine = pl.ds(pl.multiple_of(base + xl * (w * LANE), LANE), max(s, 1) * LANE)
+        self.theirs = pl.ds(pl.multiple_of(base + (1 - xl) * (w * LANE), LANE), max(s, 1) * LANE)
+        self.wide_here = pl.ds(pl.multiple_of(xl * (s * LANE), LANE), w * LANE)
+        self.theirs_here = pl.ds(pl.multiple_of((1 - xl) * (w * LANE), LANE), max(s, 1) * LANE)
         self.beside = at(1 - xl, xh, z, y, core)
         self.across = at(1 - xl, 1 - xh, z, y, core)
         self.beyond = at(xl, 1 - xh, z, y, core)
@@ -758,11 +768,11 @@
             self.arrived(self.swap, 0)
 
             def add(step):
-                bank, z, y = step // 16, (step // 4) % 4, step % 4
-                region = self.total.at[bank, z, y, :, self.mine]
-                add_into(region, region, self.swap.at[bank, z, y])
-
-            sum_loop(self.banks * 16, add)
+                bank, z = step // 4, step % 4
+                region = self.total.at[bank, z, :, :, self.mine]
+                add_into(region, region, self.swap.at[bank, z])
+
+            sum_loop(self.banks * 4, add)
             self.release(0, self.partner)
         for half in range(2):
             self.push(
@@ -874,10 +884,10 @@
         s, w = self.swapped, self.width
         c = w - s
         own = self.own(self.xh if self.by_columns else 0)
-        self.ready[:, self.wide] = own[...].astype(F32) + self.last[2].astype(F32)
+        self.ready[:, self.wide_here] = own[...].astype(F32) + self.last[2].astype(F32)
         if s:
             there = pl.ds(pl.multiple_of((1 - self.xl) * (c * LANE), LANE), s * LANE)
-            self.ready[:, self.theirs] = self.last[0, :, there].astype(F32) + self.last[
+            self.ready[:, self.theirs_here] = self.last[0, :, there].astype(F32) + self.last[
                 1, :, there
             ].astype(F32)
         if c:
@@ -892,18 +902,23 @@
             self.release(slot, device)
 
     def pieces(self, core_of):
-        rows = self.part(core_of)
-        if self.name == "qkv":
-            return [
+        rows, base, columns = self.part(core_of), self.base, self.columns
+        if self.gradient != QKV:
+            first = base + (self.core * 2048 if self.gradient == UP else 0)
+            return [(self.ready.at[rows, :], self.output.at[:, pl.ds(first, columns)])]
+        found = []
+        start = base
+        while start < base + columns:
+            third, within = start // 512, start % 512
+            run = min(512 - within, base + columns - start)
+            found.append(
                 (
-                    self.ready.at[rows, pl.ds(third * 512, 512)],
-                    self.output.at[:, pl.ds(third * 1024 + self.core * 512, 512)],
+                    self.ready.at[rows, pl.ds(start - base, run)],
+                    self.output.at[:, pl.ds(third * 1024 + self.core * 512 + within, run)],
                 )
-                for third in range(3)
-            ]
-        if self.name == "up":
-            return [(self.ready.at[rows, :], self.output.at[:, pl.ds(self.core * 2048, 2048)])]
-        return [(self.ready.at[rows, :], self.output)]
+            )
+            start += run
+        return found
 
     def deliver(self):
         for index, (source, target) in enumerate(self.pieces(self.core)):
@@ -918,7 +933,7 @@
             pltpu.make_async_copy(source, source, self.send.at[self.number, 12 + index]).wait()
 
     def stage7(self):
-        if self.name == "small":
+        if self.gradient == SMALL:
             self.add_last()
             self.push(
                 lambda: self.ready.at[self.part(1 - self.core), :], self.tail.at[0], 12, self.sibling
@@ -935,7 +950,7 @@
 
     def stage8(self):
         core = self.core
-        if self.name == "small":
+        if self.gradient == SMALL:
             self.arrived(self.tail.at[0], 12)
             self.tail[1] = self.ready[self.part(core), :] + self.tail[0]
         elif self.by_columns:
@@ -950,7 +965,7 @@
 
             @pl.when(self.xh != core)
             def _():
-                self.arrived(self.output, 12)
+                self.arrived(self.output.at[:, pl.ds(self.base, self.columns)], 12)
 
         self.settle()
         if not self.by_columns:
@@ -967,8 +982,7 @@
                 pltpu.make_async_copy(own, own, self.send.at[self.number, 11]).wait()
 
 
-QKV, UP, OUT, DOWN, SMALL = range(5)
-WEIGHTS = GATHERED[1:]
+WEIGHTS = GATHERED[0]
 WEIGHT_NAMES = tuple(spec[0] for spec in WEIGHTS)
 
 FLIPPED, TURNED, PROBS, MIXED, ACTIVE = range(5)
@@ -985,8 +999,7 @@
 
 TOUCHED = {
     "joined": ("qkv", TURNED, FLIPPED),
-    "fattnA": (TURNED, PROBS, MIXED),
-    "fattnB": (TURNED, PROBS, MIXED),
+    "fattn": (TURNED, PROBS, MIXED),
     "up": ("up", ACTIVE, "slope"),
     "down": ("down", "out", ACTIVE, MIXED),
     "gdown": (ACTIVE,),
@@ -999,17 +1012,17 @@
     "dhidden": ("qkv", "up", TURNED, "slope"),
     "gqkv": (FLIPPED, TURNED),
 }
-FORWARD = ("joined", "fattnA", "fattnB", "up", "down")
+FORWARD = ("joined", "fattn", "up", "down")
 WHOLE_AFTER = {
     TURNED: "joined",
     FLIPPED: "joined",
-    PROBS: "fattnB",
-    MIXED: "fattnB",
+    PROBS: "fattn",
+    MIXED: "fattn",
     ACTIVE: "up",
     "slope": "up",
 }
 GATHERS = {"s": 0, "q": 1, "u": 2, "o": 3, "d": 4}
-SUMS = {"Q": QKV, "U": UP, "O": OUT, "D": DOWN, "S": SMALL}
+SUMS = {"Q": 0, "R": 1, "U": 2, "V": 3, "O": 4, "D": 5, "E": 6, "S": SMALL_SUM}
 
 
 class Pair:
@@ -1071,36 +1084,34 @@
     return found.reshape(-1, found.shape[-1])
 
 
-def row_tile(weight, index):
+def row_tile(weight, index, size):
     banks, unused, same, rows, columns = weight.shape
-    if rows == 128:
-        found = weight[0, index // 2, pl.ds((index % 2) * 2, 2)]
-    elif banks == 2:
-        found = weight[index // 2, pl.ds((index % 2) * 2, 2)]
-    else:
-        found = weight[0, pl.ds(index * 2, 2)]
-    return found.reshape(TILE, columns)
+    count = size // WIDE
+    found = weight[0, pl.ds(index * count, count)] if rows == 128 else weight[pl.ds(index * count, count)]
+    return found.reshape(size, columns)
 
 
 def store_row_tile(total):
     def store(index, found):
         banks, unused, same, rows, columns = total.shape
         if rows == 128:
-            total[0, index // 2, pl.ds((index % 2) * 2, 2)] = found.reshape(2, 128, columns)
+            count = found.shape[0] // WIDE
+            total[0, pl.ds(index * count, count)] = found.reshape(count, 4, 128, columns)
         else:
-            total[0, pl.ds(index * 2, 2)] = found.reshape(2, 4, 32, columns)
+            total[0] = found.reshape(4, 4, 32, columns)
 
     return store
 
 
 def store_column_tile(total):
     def store(index, found):
-        total[:, :, :, :, columns_of(index)] = found.reshape(2, 4, 4, 32, TILE)
+        width = found.shape[1]
+        total[:, :, :, :, columns_of(index, width)] = found.reshape(2, 4, 4, 32, width)
 
     return store
 
 
-def blocks_kernel(schedule, tokens, out_grad, b_qkv, b_up, ln_gain, ln_bias, out_bias, tables, *rest):
+def blocks_kernel(schedule, b_qkv, b_up, ln_gain, ln_bias, out_bias, *rest):
     rest = list(rest)
 
     def take(count):
@@ -1108,6 +1119,7 @@
         del rest[:count]
         return found
 
+    arguments = take(3)
     owned_weights = take(4)
     result, in_grad = take(2)
     large_out = take(4)
@@ -1117,19 +1129,25 @@
     held = dict(zip(KEPT_NAMES + WEIGHT_NAMES, take(len(KEPT) + 4)))
     vectors = [dict(zip(KINDS, take(5))) for layer_at in range(LAYERS)]
     grads = [dict(zip(KINDS, take(5))) for layer_at in range(LAYERS)]
-    owned, rows, x_late, dy = take(4)
+    owned, x_late, dy = take(3)
+    tokens, out_grad, tables = copies = take(3)
     early, late = take(2)
     d_mixed, partial = take(2)
-    received_one, received_two = take(2)
+    (received_one,) = take(1)
     totals = take(5)
     landing = [take(BUFFERS) for spec in SUMMED]
     send, recv, sum_send, sum_recv, free, pair_send, pair_recv, moved = take(8)
     every = totals[SMALL]
+    rows = every.reshape(64 * OWNED_ROWS, LANE)
     hidden, dy_low = (early, late), (late, early)
-    received = (received_one, received_two)
+    received = (received_one, dy)
     received_grad = (received_one, received_one)
     inputs = (tokens, x_late)
-
+    upstream = (dy, out_grad)
+
+    greeted = greet(neighbours())
+    moves = Moves(moved)
+    arriving = [moves.start(source, target) for source, target in zip(arguments, copies)]
     owned[...] = jnp.zeros_like(owned)
     for layer_at in range(LAYERS):
         for row, vector in enumerate((b_qkv, b_up, ln_gain, ln_bias, out_bias)):
@@ -1138,32 +1156,34 @@
             ].astype(F32)
     xl, xh, z, y, c = place()
     where = (xl, xh, z, y)
-    meet(neighbours())
+    await_greetings(greeted)
     pair = Pair(pair_send, pair_recv)
-    moves = Moves(moved)
     own, other = pl.ds(0, COUNT), pl.ds(COUNT, COUNT)
 
     streams, sums = {}, {}
     for core in range(2):
         streams[core, 0, 0] = Stream(
-            0, GATHERED[0], owned_pieces("small", owned, 0), every, send, recv, *where, core
+            0, SMALL_GATHERED, owned_pieces("small", owned, 0), every, send, recv, *where, core
         )
         number = 0
         for layer_at in range(LAYERS):
             for which in range(4):
                 number += 1
                 streams[core, layer_at, which + 1] = Stream(
-                    number, WEIGHTS[which],
+                    number, GATHERED[layer_at][which],
                     owned_pieces(WEIGHT_NAMES[which], owned_weights[which], layer_at),
                     gathered[layer_at][which], send, recv, *where, core,
                 )
+        number = 0
+        for which, spec in enumerate(SUMMED):
+            gradient = spec[0]
+            for layer_at in range(1 if gradient == SMALL else LAYERS):
                 sums[core, layer_at, which] = Sum(
-                    number, which, layer_at == 0, totals[which], landing[which],
-                    large_out[which].at[layer_at], sum_send, sum_recv, free, where, core,
+                    number, which, layer_at == 0 and gradient != SMALL, totals[gradient], landing[which],
+                    None if gradient == SMALL else large_out[gradient].at[layer_at],
+                    sum_send, sum_recv, free, where, core,
                 )
-        sums[core, 0, SMALL] = Sum(
-            0, SMALL, False, totals[SMALL], landing[SMALL], None, sum_send, sum_recv, free, where, core
-        )
+                number += 1
     stage_of = {}
 
     def advance(table, layer_at, which, first):
@@ -1217,7 +1237,6 @@
             settle_load(name)
 
     def vec(layer_at):
-        rows[...] = every[...].reshape(rows.shape)
         for core in range(2):
 
             @pl.when(c == core)
@@ -1226,9 +1245,10 @@
                     for kind in KINDS:
                         unpack_vector(rows, layer, kind, core, vectors[layer][kind])
 
-        rows[...] = jnp.zeros_like(rows)
-
     def fnorm(layer_at):
+        if layer_at == 0:
+            for copy in arriving:
+                moves.finish(copy)
         norm_piece(inputs[layer_at], vectors[layer_at]["gain"], vectors[layer_at]["shift"], hidden[layer_at])
         pair.push(hidden[layer_at].at[own], hidden[layer_at].at[other], layer_at)
 
@@ -1242,8 +1262,8 @@
             )
         flip_piece(hidden[layer_at], held[FLIPPED])
 
-    def fattn(start, stop):
-        return lambda layer_at: attention_piece(held[TURNED], held[PROBS], held[MIXED], start, stop)
+    def fattn(layer_at):
+        attention_piece(held[TURNED], held[PROBS], held[MIXED])
 
     def up(layer_at):
         up_piece(
@@ -1270,13 +1290,9 @@
             loads["result"] = moves.start(target, result)
 
     def start(layer_at):
-        if layer_at:
-            for half in range(2):
-                moves.finish(loads["out_grad", half])
-                dy[:, pl.ds(half * 512, 512)] = d_mixed[pl.ds(half * COUNT, COUNT), :].astype(F32)
-        else:
+        if not layer_at:
             moves.finish(loads["result"])
-        start_piece(dy, dy_low[layer_at], grads[layer_at]["out_bias"])
+        start_piece(upstream[layer_at], dy_low[layer_at], grads[layer_at]["out_bias"])
         pair.push(dy_low[layer_at].at[own], dy_low[layer_at].at[other], 4 + layer_at)
 
     def low(layer_at):
@@ -1284,44 +1300,44 @@
         pair.arrived(dy_low[layer_at].at[other], 4 + layer_at)
 
     def gdown(layer_at):
-        rows_grad_piece(8, held[ACTIVE], dy_low[layer_at], store_row_tile(totals[DOWN]))
+        rows_grad_piece(D, held[ACTIVE], dy_low[layer_at], store_row_tile(totals[DOWN]))
 
     def slope(layer_at):
         slope_piece(
-            dy_low[layer_at], lambda n: row_tile(held["down"], n), held["slope"], held["slope"],
+            dy_low[layer_at], lambda n: row_tile(held["down"], n, D), held["slope"], held["slope"],
             grads[layer_at]["b_up"],
         )
 
     def gup(layer_at):
-        columns_grad_piece(8, held[FLIPPED], held["slope"], store_column_tile(totals[UP]))
+        columns_grad_piece(D, held[FLIPPED], held["slope"], store_column_tile(totals[UP]))
 
     def dmixed(layer_at):
-        d_mixed_piece(dy_low[layer_at], lambda n: row_tile(held["out"], n), d_mixed)
+        d_mixed_piece(dy_low[layer_at], lambda n: row_tile(held["out"], n, WIDE), d_mixed)
 
     def gout(layer_at):
-        rows_grad_piece(2, held[MIXED], dy_low[layer_at], store_row_tile(totals[OUT]))
-
-    def battn(first, stop):
+        rows_grad_piece(WIDE, held[MIXED], dy_low[layer_at], store_row_tile(totals[OUT]))
+
+    def battn(sequence):
         return lambda layer_at: attention_back_piece(
             held[TURNED], held[PROBS], d_mixed, tables, held[TURNED], grads[layer_at]["b_qkv"],
-            first, stop,
+            sequence,
         )
 
     def dhidden(layer_at):
         pair.sent(partial.at[other], 3 if layer_at else 7)
         d_hidden_piece(
-            held[TURNED], lambda n: row_tile(held["qkv"], n), held["slope"],
-            lambda n: row_tile(held["up"], n), partial,
+            held[TURNED], lambda n: row_tile(held["qkv"], n, D), held["slope"],
+            lambda n: row_tile(held["up"], n, D), partial,
         )
         pair.push(partial.at[other], received_grad[layer_at], 6 + layer_at)
 
     def gqkv(layer_at):
-        columns_grad_piece(6, held[FLIPPED], held[TURNED], store_column_tile(totals[QKV]))
+        columns_grad_piece(1536, held[FLIPPED], held[TURNED], store_column_tile(totals[QKV]))
 
     def norm(layer_at):
         pair.arrived(received_grad[layer_at], 6 + layer_at)
         norm_back_piece(
-            inputs[layer_at], vectors[layer_at]["gain"], dy, partial, received_grad[layer_at], dy,
+            inputs[layer_at], vectors[layer_at]["gain"], upstream[layer_at], partial, received_grad[layer_at], dy,
             grads[layer_at]["gain"], grads[layer_at]["shift"],
         )
         if layer_at == 0:
@@ -1332,22 +1348,16 @@
 
             @pl.when(c == core)
             def _():
+                if layer_at:
+                    streams[core, 0, 0].finish()
+                    every[...] = jnp.zeros_like(every)
                 for kind in KINDS:
                     pack_vector(rows, layer_at, kind, core, grads[layer_at][kind])
-                if layer_at == 0:
-                    streams[core, 0, 0].finish()
-
-        if layer_at == 0:
-            totals[SMALL][...] = rows[...].reshape(totals[SMALL].shape)
-
-    for half in range(2):
-        loads["out_grad", half] = moves.start(
-            out_grad.at[:, pl.ds(half * 512, 512)], d_mixed.at[pl.ds(half * COUNT, COUNT), :]
-        )
+
     steps = {
-        "vec": vec, "fnorm": fnorm, "joined": joined, "fattnA": fattn(0, 4), "fattnB": fattn(4, 8),
+        "vec": vec, "fnorm": fnorm, "joined": joined, "fattn": fattn,
         "up": up, "down": down, "res": res, "start": start, "low": low, "gdown": gdown, "slope": slope,
-        "gup": gup, "dmixed": dmixed, "gout": gout, "battnA": battn(0, 4), "battnB": battn(4, 8),
+        "gup": gup, "dmixed": dmixed, "gout": gout, "battnA": battn(0), "battnB": battn(1),
         "dhidden": dhidden, "gqkv": gqkv, "norm": norm, "pack": pack,
     }
     for name, layer_at in schedule:
@@ -1373,12 +1383,12 @@
                 if core_of == core:
                     stream.finish()
 
-    small_out[...] = landing[SMALL][8][1]
+    small_out[...] = landing[SMALL_SUM][8][1]
     for copy in list(moves.open):
         copy.wait()
 
 
-def blocks_call(tokens, out_grad, b_qkv, b_up, ln_gain, ln_bias, out_bias, tables, *owned_weights):
+def blocks_call(tokens, out_grad, tables, vectors, owned_weights):
     vmem, hbm = pl.BlockSpec(memory_space=pltpu.VMEM), pl.BlockSpec(memory_space=pltpu.HBM)
     shape = jax.ShapeDtypeStruct
     outs = [
@@ -1399,27 +1409,28 @@
     scratch += [pltpu.VMEM((1, n), F32) for n in (1536, 2048, D, D, D) * (2 * LAYERS)]
     scratch += [
         pltpu.VMEM((OWNED_ROWS, LANE), F32),
-        pltpu.VMEM((64 * OWNED_ROWS, LANE), F32),
         pltpu.VMEM((COUNT, D), F32),
         pltpu.VMEM((COUNT, D), F32),
+        pltpu.VMEM((COUNT, D), BF16),
+        pltpu.VMEM((COUNT, D), BF16),
+        pltpu.VMEM((3, COUNT, LANE), F32),
         pltpu.VMEM((BOTH, D), BF16),
         pltpu.VMEM((BOTH, D), BF16),
         pltpu.VMEM((BOTH, 512), BF16),
         pltpu.VMEM((BOTH, D), F32),
         pltpu.VMEM((COUNT, D), F32),
-        pltpu.VMEM((COUNT, D), F32),
     ]
-    for spec in SUMMED:
-        scratch.append(pltpu.VMEM(total_shape(spec), F32 if spec[0] == "small" else BF16))
+    scratch += [pltpu.VMEM(weight_shape(spec), BF16) for spec in WEIGHTS]
+    scratch.append(pltpu.VMEM(weight_shape(SMALL_GATHERED), F32))
     for spec in SUMMED:
         scratch += landing_shapes(spec)
     count = 1 + 4 * LAYERS
     scratch += [
         pltpu.SemaphoreType.DMA((count, SLOTS)),
         pltpu.SemaphoreType.DMA((count, SLOTS)),
-        pltpu.SemaphoreType.DMA((count, SUM_SLOTS)),
-        pltpu.SemaphoreType.DMA((count, SUM_SLOTS)),
-        pltpu.SemaphoreType.REGULAR((4, 12)),
+        pltpu.SemaphoreType.DMA((2 * len(SUMMED), SUM_SLOTS)),
+        pltpu.SemaphoreType.DMA((2 * len(SUMMED), SUM_SLOTS)),
+        pltpu.SemaphoreType.REGULAR((len(SUMMED), 12)),
         pltpu.SemaphoreType.DMA((8,)),
         pltpu.SemaphoreType.DMA((8,)),
         pltpu.SemaphoreType.DMA((40,)),
@@ -1427,14 +1438,14 @@
     found = pl.pallas_call(
         functools.partial(blocks_kernel, [(STEP_NAMES[step // 2], step % 2) for step in SCHEDULE]),
         out_shape=outs,
-        in_specs=[vmem, hbm] + [vmem] * 6 + [hbm] * 4,
+        in_specs=[vmem] * 5 + [hbm] * 7,
         out_specs=[hbm] * in_hbm + [vmem],
         scratch_shapes=scratch,
         name="blocks",
         compiler_params=pltpu.CompilerParams(
-            collective_id=0, has_side_effects=True, vmem_limit_bytes=63 * 2**20
+            collective_id=0, has_side_effects=True, vmem_limit_bytes=639 * 2**20 // 10
         ),
-    )(tokens, out_grad, b_qkv, b_up, ln_gain, ln_bias, out_bias, tables, *owned_weights)
+    )(*vectors, tokens, out_grad, tables, *owned_weights)
     return found[:6] + found[in_hbm:]
 
 
@@ -1481,7 +1492,11 @@
 ):
     tables = jnp.asarray(turn_tables())
     found = blocks_call(
-        tokens, out_grad, b_qkv, b_up, ln_gain, ln_bias, out_bias, tables, w_qkv, w_up, w_out, w_down
+        tokens,
+        out_grad,
+        tables,
+        (b_qkv, b_up, ln_gain, ln_bias, out_bias),
+        (w_qkv, w_up, w_out, w_down),
     )
     result, in_grad, g_qkv, g_up, g_out, g_down, *small = hand_over(found)
     g_b_qkv, g_b_up, g_gain, g_shift, g_out_bias = small

time: 271 us -> 246 us (0.908); the launches traced: 271 us -> 242 us
  Pallas kernels: 270 us -> 241 us
    pallas_call x1, Pallas kernels: 266 us -> 237 us  [blocks_call(): pl.pallas_call(functools.partial(blocks_kernel, [(STEP_NAMES[step // 2],...]
where the time goes in v5:
time: 246 us; the launch traced here: 242 us
  Pallas kernels  241 us (98%)
    pallas_call x1, Pallas kernels, blocks_call(): pl.pallas_call(functools.partial(blocks_kernel, [(STEP_NAMES[step // 2],...  237 us

profile of v5, /device:TPU:1, one launch (start us, length us, event | category | flops | bytes accessed | tf_op | source)
XLA Modules:
  0.0 241.7 jit_solution(3915966259721448738)
XLA Ops:
  0.6 236.6 %blocks.1 = (bf16[256,1024]{1,0:T(8,128)(2,1)}, f32[256,1024]{1,0:T(8,128)}, f32[2,16,3072]{2,1,0:T(8,128)}, f32[2,16,4096]{2,1,0:T(8,128)}, f32[2,16,1024]{2,1,...) custom-call(bf16[2,48]{1,0:T(2,128)(2,1)} %b_qkv.1, ...), custom_call_target="tpu_custom_call" | custom-call | tf_op jit(solution)/shard_map/blocks/pallas_call | solution.py:1438
  237.2 4.3 %hand_over.1 = (bf16[256,1024]{1,0:T(8,128)(2,1)}, f32[256,1024]{1,0:T(8,128)}, f32[2,16,3072]{2,1,0:T(8,128)}, f32[2,16,4096]{2,1,0:T(8,128)}, f32[2,16,1024]{2...) custom-call(bf16[256,1024]{1,0:T(8,128)(2,1)} %get-tuple-element.29., ...), custom_call_target="tpu_custom_call" | custom-call | tf_op jit(solution)/shard_map/hand_over/pallas_call | solution.py:1478

commit v6 on v5

--- a/solution.py
+++ b/solution.py
@@ -23,18 +23,17 @@
     gqkv1, norm0, norm1, pack0, pack1,
 ) = range(2 * len(STEP_NAMES))
 SCHEDULE = (
-    o1, s0, q0, q1, o1, o0, u0, s0, q0, s0, d0, q1, o0, q0, s0, d1, u0, o0, q0, u1, o1, u0, o0,
-    u0, d0, q0, q1, o0, s0, d0, d0, u0, s0, s0, vec0, q0, d0, q1, fnorm0, u0, o1, u1, q0, o0,
-    joined0, d0, u1, d1, q1, fattn0, u1, u0, o0, d0, up0, q1, down0, d1, o1, u1, res0, q1, fnorm1,
-    d1, o1, joined1, u1, start1, fattn1, low1, gout1, o1, O1, u1, O1, dmixed1, d1, up1, gdown1,
-    d1, D1, D1, E1, O1, battnA1, battnB1, d1, D1, gqkv1, Q1, Q1, O1, slope1, gup1, V1, O1, D1, E1,
-    Q1, down1, U1, U1, E1, D1, R1, res1, dhidden1, V1, U1, norm1, start0, E1, V1, Q1, O1, low0,
-    gdown0, E0, D0, R1, gout0, D0, slope0, E1, U1, R1, V1, O0, O0, gup0, U0, U0, D1, U1, D0,
-    dmixed0, R1, V0, E0, battnA0, O0, D1, Q1, battnB0, U0, U1, gqkv0, E1, Q1, D1, D0, R0,
-    dhidden0, V0, E1, V1, E0, Q0, D0, pack1, E1, U1, Q1, U1, U0, Q0, O1, V1, norm0, R1, O1, V0,
-    O0, U0, D0, E0, R1, V1, O0, Q1, V1, R0, Q0, pack0, O0, S0, D0, S0, U0, R0, R1, V0, Q0, S0, O0,
-    U0, R1, V0, E0, R0, D0, Q0, S0, V0, E0, R0, Q0, O0, S0, R0, V0, S0, Q0, E0, R0, V0, Q0, S0,
-    S0, R0, E0, U0,
+    o0, s0, q0, o1, q1, d0, d1, o0, u0, s0, q0, o0, o1, s0, q1, q0, o0, u1, d0, q0, o0, q1, s0,
+    d0, u0, o1, q0, d0, o0, u0, q0, s0, u0, d0, u0, q1, s0, s0, u1, vec0, q0, o1, fnorm0, u0, d0,
+    u1, d1, joined0, q1, u1, u0, o0, fattn0, d0, up0, q1, down0, o1, d1, u1, res0, q1, fnorm1, o1,
+    d1, joined1, u1, start1, o1, fattn1, low1, gout1, O1, O1, u1, dmixed1, d1, up1, gdown1, d1,
+    D1, D1, E1, O1, battnA1, battnB1, d1, D1, gqkv1, O1, Q1, Q1, slope1, gup1, V1, O1, D1, U1, E1,
+    Q1, down1, D1, U1, R1, E1, res1, dhidden1, V1, Q1, U1, D1, norm1, start0, E1, V1, low0,
+    gdown0, R1, gout0, E0, D0, D0, O0, U1, slope0, O0, O1, U1, R1, dmixed0, V1, Q1, gup0, V0, E1,
+    U0, O0, U0, V1, D0, U1, battnA0, battnB0, E0, dhidden0, U0, D1, R1, Q1, V1, E1, O1, D1, gqkv0,
+    U1, E0, O1, R0, U1, Q1, D0, norm0, V0, Q0, U0, Q0, E1, pack1, D0, O0, E1, U0, Q1, V1, R1, V0,
+    R0, Q0, R1, U0, pack0, S0, S0, R0, R1, E0, V1, R1, V0, Q0, O0, S0, U0, D0, V0, E0, R0, Q0, O0,
+    S0, V0, E0, R0, Q0, S0, D0, V0, R0, S0, O0, Q0, E0, U0, R0, O0, D0, V0, Q0, S0, S0, R0, E0,
 )
 
 

time: 246 us -> 245 us (level)
  no operation moved by 1% of the time
where the time goes in v6:
time: 245 us; the launch traced here: 241 us
  Pallas kernels  240 us (98%)
    pallas_call x1, Pallas kernels, blocks_call(): pl.pallas_call(functools.partial(blocks_kernel, [(STEP_NAMES[step // 2],...  236 us

profile of v6, /device:TPU:1, one launch (start us, length us, event | category | flops | bytes accessed | tf_op | source)
XLA Modules:
  0.0 241.1 jit_solution(4671125857771958780)
XLA Ops:
  0.6 236.0 %blocks.1 = (bf16[256,1024]{1,0:T(8,128)(2,1)}, f32[256,1024]{1,0:T(8,128)}, f32[2,16,3072]{2,1,0:T(8,128)}, f32[2,16,4096]{2,1,0:T(8,128)}, f32[2,16,1024]{2,1,...) custom-call(bf16[2,48]{1,0:T(2,128)(2,1)} %b_qkv.1, ...), custom_call_target="tpu_custom_call" | custom-call | tf_op jit(solution)/shard_map/blocks/pallas_call | solution.py:1437
  236.7 4.3 %hand_over.1 = (bf16[256,1024]{1,0:T(8,128)(2,1)}, f32[256,1024]{1,0:T(8,128)}, f32[2,16,3072]{2,1,0:T(8,128)}, f32[2,16,4096]{2,1,0:T(8,128)}, f32[2,16,1024]{2...) custom-call(bf16[256,1024]{1,0:T(8,128)(2,1)} %get-tuple-element.29., ...), custom_call_target="tpu_custom_call" | custom-call | tf_op jit(solution)/shard_map/hand_over/pallas_call | solution.py:1477
